TPU v7x, 32 devices: a whole 2x2x4 slice. The times are simulated.
32 devices in a mesh: section: 2 (over y), blk: 4 (over z), fsdp: 4 (over x, core).
Axes of the slice: x: 2, y: 2, z: 4, core: 2. Of those that a mesh axis runs over, the one named last changes fastest.
Arguments:
- tokens_in: bfloat16 [8, 1024, 896], P('fsdp', 'blk'), may hold values from -6 to 6
- positions: int32 [8, 1024], P('fsdp', 'blk'), may hold values from 0 to 511, as said below
- doc_ids: int32 [8, 1024], P('fsdp'), may hold values from 0 to 3, as said below
- out_grad: bfloat16 [8, 1024, 896], P('fsdp', 'blk'), may hold values from -6 to 6
- norm1_gain: float32 [2, 896], P('section'), may hold values from 0.25 to 1.75
- w_qkv: bfloat16 [2, 896, 1152], P('section', ('blk', 'fsdp')), may hold values from -0.1875 to 0.1875
- b_qkv: float32 [2, 1152], P('section'), may hold values from -1.25 to 1.25
- w_out: bfloat16 [2, 896, 896], P('section', ('blk', 'fsdp')), may hold values from -0.75 to 0.75
- norm2_gain: float32 [2, 896], P('section'), may hold values from 0.25 to 1.75
- w_gate_up: bfloat16 [2, 896, 9728], P('section', ('blk', 'fsdp')), may hold values from -0.1875 to 0.1875
- w_down: bfloat16 [2, 4864, 896], P('section', ('blk', 'fsdp')), may hold values from -0.078125 to 0.078125
Outputs:
- block_out: float32 [2, 8, 1024, 896], P('section', 'fsdp', 'blk')
- input_grad: float32 [2, 8, 1024, 896], P('section', 'fsdp', 'blk')
- grad_norm1_gain: float32 [2, 896], P('section')
- grad_w_qkv: float32 [2, 896, 1152], P('section', ('blk', 'fsdp'))
- grad_b_qkv: float32 [2, 1152], P('section')
- grad_w_out: float32 [2, 896, 896], P('section', ('blk', 'fsdp'))
- grad_norm2_gain: float32 [2, 896], P('section')
- grad_w_gate_up: float32 [2, 896, 9728], P('section', ('blk', 'fsdp'))
- grad_w_down: float32 [2, 4864, 896], P('section', ('blk', 'fsdp'))
Inputs may be any that keep to these rules, and one draw needn't show every extreme that they name: `doc_ids`: each token's document number within its sequence: never falling, four documents in every sequence, exactly one of them of 512 tokens. `positions`: each token's place within its document, 0 at the document's first token.
All inputs are finite; a program needn't handle non-finite values.
Results may differ from a plain program's by a relative error of at most 0.017.
Values may be sent and summed in bfloat16 or wider, within the bound.
A program may use at most 320 MiB of HBM per device.

v0:
```python
import math

import jax
import jax.numpy as jnp
from jax import lax
from jax.sharding import PartitionSpec as P

H = 14
KVH = 2
HD = 64
FF = 4864


def passed_along(value, axis, steps):
    count = lax.axis_size(axis)
    leading, last = (max(0, -steps), min(count, count - steps))
    return lax.ppermute(value, axis, [(source, source + steps) for source in range(leading, last)])


def rms_scale(values):
    return lax.rsqrt(jnp.mean(values * values, axis=-1, keepdims=True) + 1e-06)


def angles(positions):
    half_size = HD // 2
    freq = jnp.exp(jnp.arange(half_size, dtype=jnp.float32) * (-2.0 / HD) * math.log(1000000.0))
    phase = positions.astype(jnp.float32)[:, None] * freq[None, :]
    return (jnp.cos(phase)[:, None, :], jnp.sin(phase)[:, None, :])


def rotate(values, cos_part, sin_part):
    half_size = values.shape[-1] // 2
    part_one = values[..., :half_size]
    part_two = values[..., half_size:]
    return jnp.concatenate(
        [part_one * cos_part - part_two * sin_part, part_two * cos_part + part_one * sin_part],
        axis=-1,
    )


def unrotate(grads, cos_part, sin_part):
    half_size = grads.shape[-1] // 2
    part_one = grads[..., :half_size]
    part_two = grads[..., half_size:]
    return jnp.concatenate(
        [part_one * cos_part + part_two * sin_part, part_two * cos_part - part_one * sin_part],
        axis=-1,
    )


def allowed_keys(docs, row_start, row_count):
    query_rows = row_start + jnp.arange(row_count, dtype=jnp.int32)
    query_docs = lax.dynamic_slice_in_dim(docs, row_start, row_count)
    key_rows = jnp.arange(docs.shape[0], dtype=jnp.int32)
    return (key_rows[None, :] <= query_rows[:, None]) & (docs[None, :] == query_docs[:, None])


def head_slices(queries, pairs_all, kv_head):
    group_size = H // KVH
    query_group = queries[:, kv_head * group_size : (kv_head + 1) * group_size, :]
    key_part = pairs_all[:, kv_head * HD : (kv_head + 1) * HD]
    value_part = pairs_all[:, (KVH + kv_head) * HD : (KVH + kv_head + 1) * HD]
    return (query_group, key_part, value_part)


def attend_forward(queries, pairs_all, allowed):
    head_scale = HD ** (-0.5)
    head_outputs = []
    log_totals = []
    for kv_head in range(KVH):
        query_group, key_part, value_part = head_slices(queries, pairs_all, kv_head)
        scores = (
            jnp.einsum("tjd,kd->jtk", query_group, key_part, preferred_element_type=jnp.float32)
            * head_scale
        )
        scores = jnp.where(allowed[None], scores, -1e30)
        top_score = jnp.max(scores, axis=-1, keepdims=True)
        log_total = top_score + jnp.log(
            jnp.sum(jnp.exp(scores - top_score), axis=-1, keepdims=True)
        )
        weights_low = jnp.exp(scores - log_total).astype(jnp.bfloat16)
        head_outputs.append(
            jnp.einsum("jtk,kd->tjd", weights_low, value_part, preferred_element_type=jnp.float32)
        )
        log_totals.append(log_total)
    return (jnp.concatenate(head_outputs, axis=1), jnp.stack(log_totals))


def attend_backward(grad_mixed, queries, pairs_all, log_totals, allowed):
    group_size = H // KVH
    head_scale = HD ** (-0.5)
    query_grads = []
    key_grads = []
    value_grads = []
    for kv_head in range(KVH):
        query_group, key_part, value_part = head_slices(queries, pairs_all, kv_head)
        grad_group = grad_mixed[:, kv_head * group_size : (kv_head + 1) * group_size, :]
        scores = (
            jnp.einsum("tjd,kd->jtk", query_group, key_part, preferred_element_type=jnp.float32)
            * head_scale
        )
        scores = jnp.where(allowed[None], scores, -1e30)
        probabilities = jnp.exp(scores - log_totals[kv_head])
        grad_probabilities = jnp.einsum(
            "tjd,kd->jtk", grad_group, value_part, preferred_element_type=jnp.float32
        )
        row_inner = jnp.sum(probabilities * grad_probabilities, axis=-1, keepdims=True)
        grad_scores = (probabilities * (grad_probabilities - row_inner)).astype(jnp.bfloat16)
        query_grads.append(
            jnp.einsum("jtk,kd->tjd", grad_scores, key_part, preferred_element_type=jnp.float32)
            * head_scale
        )
        key_grads.append(
            jnp.einsum("jtk,tjd->kd", grad_scores, query_group, preferred_element_type=jnp.float32)
            * head_scale
        )
        value_grads.append(
            jnp.einsum(
                "jtk,tjd->kd",
                probabilities.astype(jnp.bfloat16),
                grad_group,
                preferred_element_type=jnp.float32,
            )
        )
    return (jnp.concatenate(query_grads, axis=1), jnp.concatenate(key_grads + value_grads, axis=1))


def layer_forward(hidden, positions, docs, row_start, weights, small_params):
    weight_qkv, weight_out, weight_gate_up, weight_down = weights
    gain_one, bias_qkv, gain_two = small_params
    row_count = hidden.shape[0]
    attn_width = H * HD
    scale_one = rms_scale(hidden)
    normed = (hidden * scale_one * gain_one).astype(jnp.bfloat16)
    joined = jnp.dot(normed, weight_qkv, preferred_element_type=jnp.float32) + bias_qkv
    cos_part, sin_part = angles(positions)
    queries = rotate(joined[:, :attn_width].reshape(row_count, H, HD), cos_part, sin_part).astype(
        jnp.bfloat16
    )
    key_heads = rotate(
        joined[:, attn_width : attn_width + KVH * HD].reshape(row_count, KVH, HD),
        cos_part,
        sin_part,
    ).astype(jnp.bfloat16)
    value_heads = joined[:, attn_width + KVH * HD :].astype(jnp.bfloat16)
    pairs = jnp.concatenate([key_heads.reshape(row_count, KVH * HD), value_heads], axis=1)
    pairs_all = lax.all_gather(pairs, "blk", axis=0, tiled=True)
    allowed = allowed_keys(docs, row_start, row_count)
    attended, log_totals = attend_forward(queries, pairs_all, allowed)
    mixed_low = attended.reshape(row_count, attn_width).astype(jnp.bfloat16)
    residual = hidden + jnp.dot(mixed_low, weight_out, preferred_element_type=jnp.float32)
    scale_two = rms_scale(residual)
    normed_two = (residual * scale_two * gain_two).astype(jnp.bfloat16)
    gate_up = jnp.dot(normed_two, weight_gate_up, preferred_element_type=jnp.float32)
    gate_part = gate_up[:, :FF]
    up_part = gate_up[:, FF:]
    inner_low = (gate_part * jax.nn.sigmoid(gate_part) * up_part).astype(jnp.bfloat16)
    output = residual + jnp.dot(inner_low, weight_down, preferred_element_type=jnp.float32)
    saved_acts = (
        hidden,
        scale_one,
        normed,
        queries,
        pairs_all,
        log_totals,
        allowed,
        cos_part,
        sin_part,
        mixed_low,
        residual,
        scale_two,
        normed_two,
        gate_up,
        inner_low,
    )
    return (output, saved_acts)


def layer_backward(grad_out, saved_acts, weights, small_params):
    weight_qkv, weight_out, weight_gate_up, weight_down = weights
    gain_one, bias_qkv, gain_two = small_params
    (
        hidden,
        scale_one,
        normed,
        queries,
        pairs_all,
        log_totals,
        allowed,
        cos_part,
        sin_part,
        mixed_low,
        residual,
        scale_two,
        normed_two,
        gate_up,
        inner_low,
    ) = saved_acts
    row_count = hidden.shape[0]
    over_rows = (((0,), (0,)), ((), ()))
    over_cols = (((1,), (1,)), ((), ()))
    grad_branch = grad_out.astype(jnp.bfloat16)
    term_down = lax.dot_general(
        inner_low, grad_branch, over_rows, preferred_element_type=jnp.float32
    )
    grad_inner = lax.dot_general(
        grad_branch, weight_down, over_cols, preferred_element_type=jnp.float32
    )
    gate_part = gate_up[:, :FF]
    up_part = gate_up[:, FF:]
    sigmoid_gate = jax.nn.sigmoid(gate_part)
    grad_gate = grad_inner * up_part * sigmoid_gate * (1.0 + gate_part * (1.0 - sigmoid_gate))
    grad_up = grad_inner * gate_part * sigmoid_gate
    grad_gate_up = jnp.concatenate([grad_gate, grad_up], axis=1).astype(jnp.bfloat16)
    term_gate_up = lax.dot_general(
        normed_two, grad_gate_up, over_rows, preferred_element_type=jnp.float32
    )
    grad_normed_two = lax.dot_general(
        grad_gate_up, weight_gate_up, over_cols, preferred_element_type=jnp.float32
    )
    unit_two = residual * scale_two
    term_gain_two = jnp.sum(grad_normed_two * unit_two, axis=0)
    grad_unit_two = grad_normed_two * gain_two
    grad_residual = grad_out + scale_two * (
        grad_unit_two - unit_two * jnp.mean(grad_unit_two * unit_two, axis=-1, keepdims=True)
    )
    grad_residual_low = grad_residual.astype(jnp.bfloat16)
    term_out = lax.dot_general(
        mixed_low, grad_residual_low, over_rows, preferred_element_type=jnp.float32
    )
    grad_mixed = lax.dot_general(
        grad_residual_low, weight_out, over_cols, preferred_element_type=jnp.float32
    )
    grad_mixed = grad_mixed.astype(jnp.bfloat16).reshape(row_count, H, HD)
    grad_queries, grad_pairs = attend_backward(grad_mixed, queries, pairs_all, log_totals, allowed)
    grad_pairs_local = lax.psum_scatter(
        grad_pairs.astype(jnp.bfloat16), "blk", scatter_dimension=0, tiled=True
    ).astype(jnp.float32)
    grad_query_cols = unrotate(grad_queries, cos_part, sin_part).reshape(row_count, H * HD)
    grad_key_cols = unrotate(
        grad_pairs_local[:, : KVH * HD].reshape(row_count, KVH, HD), cos_part, sin_part
    ).reshape(row_count, KVH * HD)
    grad_joined = jnp.concatenate(
        [grad_query_cols, grad_key_cols, grad_pairs_local[:, KVH * HD :]], axis=1
    ).astype(jnp.bfloat16)
    term_bias = jnp.sum(grad_joined, axis=0, dtype=jnp.float32)
    term_qkv = lax.dot_general(normed, grad_joined, over_rows, preferred_element_type=jnp.float32)
    grad_normed = lax.dot_general(
        grad_joined, weight_qkv, over_cols, preferred_element_type=jnp.float32
    )
    unit_one = hidden * scale_one
    term_gain_one = jnp.sum(grad_normed * unit_one, axis=0)
    grad_unit_one = grad_normed * gain_one
    grad_hidden = grad_residual + scale_one * (
        grad_unit_one - unit_one * jnp.mean(grad_unit_one * unit_one, axis=-1, keepdims=True)
    )
    return (
        grad_hidden,
        (term_qkv, term_out, term_gate_up, term_down),
        (term_gain_one, term_bias, term_gain_two),
    )


def reduce_weights(weight_terms):
    return (
        lax.psum_scatter(weight_terms[0], ("blk", "fsdp"), scatter_dimension=0, tiled=True),
        lax.psum_scatter(weight_terms[1], ("blk", "fsdp"), scatter_dimension=0, tiled=True),
        lax.psum_scatter(weight_terms[2], ("blk", "fsdp"), scatter_dimension=0, tiled=True),
        lax.psum_scatter(weight_terms[3], ("blk", "fsdp"), scatter_dimension=0, tiled=True),
    )


def add_trees(left_tree, right_tree):
    return tuple((left_part + right_part for left_part, right_part in zip(left_tree, right_tree)))


def shards(
    tokens_in,
    positions,
    doc_ids,
    out_grad,
    norm1_gain,
    w_qkv,
    b_qkv,
    w_out,
    norm2_gain,
    w_gate_up,
    w_down,
):
    section_index = lax.axis_index("section")
    is_first = section_index == 0
    is_last = jnp.logical_not(is_first)
    micro_count = tokens_in.shape[0]
    row_count = tokens_in.shape[1]
    row_start = lax.axis_index("blk") * row_count
    weights = (
        lax.all_gather(w_qkv[0], ("blk", "fsdp"), axis=0, tiled=True),
        lax.all_gather(w_out[0], ("blk", "fsdp"), axis=0, tiled=True),
        lax.all_gather(w_gate_up[0], ("blk", "fsdp"), axis=0, tiled=True),
        lax.all_gather(w_down[0], ("blk", "fsdp"), axis=0, tiled=True),
    )
    small_params = (norm1_gain[0], b_qkv[0], norm2_gain[0])
    received = jnp.zeros((row_count, tokens_in.shape[2]), jnp.bfloat16)
    step_outputs = []
    step_saved = []
    for step_index in range(micro_count + 1):
        lower_seq = min(step_index, micro_count - 1)
        upper_seq = max(step_index - 1, 0)
        hidden = jnp.where(
            is_first, tokens_in[lower_seq].astype(jnp.float32), received.astype(jnp.float32)
        )
        step_positions = jnp.where(is_first, positions[lower_seq], positions[upper_seq])
        step_docs = jnp.where(is_first, doc_ids[lower_seq], doc_ids[upper_seq])
        output, saved_acts = layer_forward(
            hidden, step_positions, step_docs, row_start, weights, small_params
        )
        if step_index < micro_count:
            received = passed_along(output.astype(jnp.bfloat16), "section", 1)
        step_outputs.append(output)
        step_saved.append(saved_acts)
    back_received = jnp.zeros((row_count, tokens_in.shape[2]), jnp.bfloat16)
    step_grads = []
    weight_shares = None
    weight_totals = None
    small_totals = None
    for step_index in range(micro_count + 1):
        upper_seq = min(step_index, micro_count - 1)
        saved_acts = jax.tree.map(
            lambda upper_part, lower_part: jnp.where(is_last, upper_part, lower_part),
            step_saved[min(step_index + 1, micro_count)],
            step_saved[max(step_index - 1, 0)],
        )
        live_factor = 1.0 if step_index < micro_count else 0.0
        cotangent = out_grad[upper_seq].astype(jnp.float32) * live_factor
        grad_out = jnp.where(is_last, cotangent, back_received.astype(jnp.float32))
        grad_hidden, weight_terms, small_terms = layer_backward(
            grad_out, saved_acts, weights, small_params
        )
        if step_index < micro_count:
            back_received = passed_along(grad_hidden.astype(jnp.bfloat16), "section", -1)
        step_grads.append(grad_hidden)
        small_totals = small_terms if small_totals is None else add_trees(small_totals, small_terms)
        weight_totals = (
            weight_terms if weight_totals is None else add_trees(weight_totals, weight_terms)
        )
        if step_index >= 1:
            shares = reduce_weights(weight_totals)
            weight_shares = shares if weight_shares is None else add_trees(weight_shares, shares)
            weight_totals = None
    small_sums = lax.psum((small_totals[0], small_totals[1], small_totals[2]), ("blk", "fsdp"))
    block_rows = [
        jnp.where(is_first, step_outputs[seq_number], step_outputs[seq_number + 1])
        for seq_number in range(micro_count)
    ]
    grad_rows = [
        jnp.where(is_last, step_grads[seq_number], step_grads[seq_number + 1])
        for seq_number in range(micro_count)
    ]
    block_out = jnp.stack(block_rows)[None]
    input_grad = jnp.stack(grad_rows)[None]
    return (
        block_out,
        input_grad,
        small_sums[0][None],
        weight_shares[0][None],
        small_sums[1][None],
        weight_shares[1][None],
        small_sums[2][None],
        weight_shares[2][None],
        weight_shares[3][None],
    )


def solution(mesh):
    return jax.shard_map(
        shards,
        mesh=mesh,
        in_specs=(
            P("fsdp", "blk", None),
            P("fsdp", "blk"),
            P("fsdp", None),
            P("fsdp", "blk", None),
            P("section", None),
            P("section", ("blk", "fsdp"), None),
            P("section", None),
            P("section", ("blk", "fsdp"), None),
            P("section", None),
            P("section", ("blk", "fsdp"), None),
            P("section", ("blk", "fsdp"), None),
        ),
        out_specs=(
            P("section", "fsdp", "blk", None),
            P("section", "fsdp", "blk", None),
            P("section", None),
            P("section", ("blk", "fsdp"), None),
            P("section", None),
            P("section", ("blk", "fsdp"), None),
            P("section", None),
            P("section", ("blk", "fsdp"), None),
            P("section", ("blk", "fsdp"), None),
        ),
        check_vma=False,
    )
```

profile of v0, /device:TPU:0, one launch (start us, length us, event | category | flops | bytes accessed | tf_op | source)
XLA Modules:
  0.0 1409.0 jit_solution(15739748016441984658)
XLA Ops:
  18.5 35.7 %all-gather.9.cloned.1.call-done = bf16[1,896,1152]{2,1,0:T(8,128)(2,1)} async-done(((bf16[1,56,1152]{2,1,0:T(8,128)(2,1)}), bf16[1,896,1152]{2,1,0:T(8,128)(2,1)}) %all-gather.9.cloned.1.call-update) | async-done | bytes 2064400 | tf_op jit(solution)/shard_map/all_gather | solution.py:297
  57.5 16.9 %all_gather.22 = bf16[1024,256]{1,0:T(8,128)(2,1)S(1)} all-gather(bf16[256,256]{1,0:T(8,128)(2,1)S(1)} %pad_maximum_fusion.27), channel_id=1, replica_groups=mesh['section'=2,'blk'=4,'fsdp'=4] {'blk'}, dimensions={0}, use_global_device_ids=true | all-gather | bytes 655360 | tf_op jit(solution)/shard_map/all_gather | solution.py:147
  85.0 11.3 all-gather.11.cloned.1.call-done
  99.6 89.4 %all-gather.13.cloned.1.call-done = bf16[1,896,9728]{2,1,0:T(8,128)(2,1)} async-done(((bf16[1,56,9728]{2,1,0:T(8,128)(2,1)}), bf16[1,896,9728]{2,1,0:T(8,128)(2,1)}) %all-gather.13.cloned.1.call-update) | async-done | bytes 17432592 | tf_op jit(solution)/shard_map/all_gather | solution.py:299
  189.0 9.0 fusion.10
  203.2 64.8 %all-gather.15.cloned.1.call-done = bf16[1,4864,896]{2,1,0:T(8,128)(2,1)} async-done(((bf16[1,304,896]{2,1,0:T(8,128)(2,1)}), bf16[1,4864,896]{2,1,0:T(8,128)(2,1)}) %all-gather.15.cloned.1.call-update) | async-done | bytes 8716304 | tf_op jit(solution)/shard_map/all_gather | solution.py:300
  268.0 7.5 fusion.396
  281.4 8.1 collective-permute-done
  294.4 15.6 %all_gather.26 = bf16[1024,256]{1,0:T(8,128)(2,1)S(1)} all-gather(bf16[256,256]{1,0:T(8,128)(2,1)S(1)} %pad_maximum_fusion.28), channel_id=1, replica_groups=mesh['section'=2,'blk'=4,'fsdp'=4] {'blk'}, dimensions={0}, use_global_device_ids=true | all-gather | bytes 655360 | tf_op jit(solution)/shard_map/all_gather | solution.py:147
  333.8 17.2 %broadcast_select_fusion.2 = (f32[256,9728]{1,0:T(8,128)}, f32[256,9728]{1,0:T(8,128)}) fusion(f32[256,9728]{1,0:T(8,128)} %copy-done, pred[]{:T(512)S(6)} %not.3, bf16[256,896]{1,0:T(8,128)(2,1)S(1)} %multiply_convert_fusion.5, bf16[1,896,9728]{2,1,0:T(8,128)(2,1)} %all-gather.13.cloned.1.call-done), kind=kOutput, calls=%fused_computation.127 | convolution fusion | flops 4465229824 | bytes 47775744 | tf_op jit(solution)/shard_map/dot_general | solution.py:154
  358.9 10.3 fusion.68
  369.2 12.9 multiply_reduce_fusion.2
  405.7 11.4 fusion.51
  456.5 16.8 %all_gather.27 = bf16[1024,256]{1,0:T(8,128)(2,1)} all-gather(bf16[256,256]{1,0:T(8,128)(2,1)S(1)} %pad_maximum_fusion.29), channel_id=1, replica_groups=mesh['section'=2,'blk'=4,'fsdp'=4] {'blk'}, dimensions={0}, use_global_device_ids=true | all-gather | bytes 655360 | tf_op jit(solution)/shard_map/all_gather | solution.py:147
  498.5 25.2 %broadcast_select_fusion = (f32[256,9728]{1,0:T(8,128)}, f32[256,9728]{1,0:T(8,128)}, f32[256,9728]{1,0:T(8,128)}) fusion(f32[256,9728]{1,0:T(8,128)} %get-tuple-element.156, pred[]{:T(512)S(6)} %not.3, f32[256,9728]{1,0:T(8,128)} %copy-done, bf16[256,896]{1,0:T(8,128)(2,1)S(1)} %multiply_convert_fusion.3, ...), kind=kOutput, calls=%fused_computation.125 | convolution fusion | flops 4467720192 | bytes 67698688 | tf_op jit(solution)/shard_map/dot_general | solution.py:154
  528.4 11.7 fusion.65
  540.1 12.9 multiply_reduce_fusion.1
  576.1 11.0 fusion.41
  600.6 12.5 reduce-scatter.14.cloned.1.call-done
  632.5 10.5 fusion.62
  643.1 12.6 multiply_reduce_fusion
  679.1 11.0 fusion.31
  724.9 10.3 fusion.113
  741.7 7.8 fusion.111
  749.5 21.3 %add_add_fusion.1 = f32[4864,896]{1,0:T(8,128)} fusion(f32[4864,896]{1,0:T(8,128)} %fusion.113, f32[4864,896]{1,0:T(8,128)} %fusion.111, bf16[256,4864]{1,0:T(8,128)(2,1)} %copy-done.20, bf16[256,4864]{1,0:T(8,128)(2,1)} %fusion.70, pred[]{:T(512)S(6)} %not.3, bf16[256,896]{1,0:T(8,128)(2,1)} %copy-done.118, bf16[2,256,896]{2,1,0:T(8,128)(2,1)} %param.14), kind=kOutput, calls=%fused_computation.13 | convolution fusion | flops 2242478080 | bytes 58196992 | tf_op jit(solution)/shard_map/dot_general | solution.py:203
  772.0 19.1 %fusion.109 = f32[896,9728]{1,0:T(8,128)} fusion(bf16[256,4864]{1,0:T(8,128)(2,1)} %get-tuple-element.55, bf16[256,4864]{1,0:T(8,128)(2,1)} %get-tuple-element.54, bf16[256,896]{1,0:T(8,128)(2,1)S(1)} %copy-done.37, bf16[256,896]{1,0:T(8,128)(2,1)S(1)} %copy-done.59, pred[]{:T(512)S(6)} %not.3), kind=kOutput, calls=%fused_computation.161 | convolution fusion | flops 4472930304 | bytes 40763392 | tf_op jit(solution)/shard_map/dot_general | solution.py:215
  791.1 19.9 %fusion.108 = f32[896,9728]{1,0:T(8,128)} fusion(bf16[256,4864]{1,0:T(8,128)(2,1)} %get-tuple-element.53, bf16[256,4864]{1,0:T(8,128)(2,1)S(1)} %copy-done.107, bf16[256,896]{1,0:T(8,128)(2,1)S(1)} %copy-done.64, bf16[256,896]{1,0:T(8,128)(2,1)S(1)} %copy-done.59, pred[]{:T(512)S(6)} %not.3), kind=kOutput, calls=%fused_computation.160 | convolution fusion | flops 4472930304 | bytes 40763392 | tf_op jit(solution)/shard_map/dot_general | solution.py:215
  811.0 37.5 %add_add_fusion = f32[896,9728]{1,0:T(8,128)} fusion(f32[896,9728]{1,0:T(8,128)} %fusion.109, f32[896,9728]{1,0:T(8,128)} %fusion.108, bf16[256,4864]{1,0:T(8,128)(2,1)} %get-tuple-element.51, bf16[256,4864]{1,0:T(8,128)(2,1)} %get-tuple-element.50, bf16[256,896]{1,0:T(8,128)(2,1)S(1)} %copy-done.64, bf16[256,896]{1,0:T(8,128)(2,1)S(1)} %copy-done.37, pred[]{:T(512)S(6)} %not.3), kind=kOutput, calls=%fused_computation | convolution fusion | flops 4490362880 | bytes 110493696 | tf_op jit(solution)/shard_map/dot_general | solution.py:215
  850.7 6.8 fusion.160
  861.4 58.7 %all-reduce.2 = (f32[1,896]{1,0:T(1,128)}, f32[1,1152]{1,0:T(1,128)}, f32[1,896]{1,0:T(1,128)}) all-reduce(f32[1,896]{1,0:T(1,128)S(1)} %broadcast_in_dim.168, f32[1,1152]{1,0:T(1,128)S(1)} %broadcast_in_dim.170, f32[1,896]{1,0:T(1,128)S(1)} %broadcast_in_dim.172), channel_id=1, replica_groups=mesh['section'=2,'blk'=4,'fsdp'=4] {'blk','fsdp'}, use_global_device_ids=true, to_apply=%region_36.37 | all-reduce | flops 2944 | bytes 23552 | tf_op jit(solution)/shard_map/psum | solution.py:350
  924.4 127.7 %reduce-scatter.20.cloned.1.call-done = f32[304,896]{1,0:T(8,128)} async-done(((f32[4864,896]{1,0:T(8,128)}), f32[304,896]{1,0:T(8,128)}) %reduce-scatter.20.cloned.1.call-update) | async-done | bytes 1089552 | tf_op jit(solution)/shard_map/reduce_scatter | solution.py:269
  1052.1 350.1 %reduce-scatter.18.cloned.1.call-done = f32[56,9728]{1,0:T(8,128)} async-done(((f32[896,9728]{1,0:T(8,128)}), f32[56,9728]{1,0:T(8,128)}) %reduce-scatter.18.cloned.1.call-update) | async-done | bytes 2179088 | tf_op jit(solution)/shard_map/reduce_scatter | solution.py:268
  (611 shorter events, 298.5 us)
Async XLA Ops:
  7.2 47.0 %all-gather.9.cloned.1.call-start = ((), (), s32[]{:S(2)}) async-start(), calls=%async_computation.10 | async-start | bytes 2193408 | tf_op jit(solution)/shard_map/all_gather | solution.py:297
  7.9 88.4 %all-gather.11.cloned.1.call-start = ((), (), s32[]{:S(2)}) async-start(), calls=%async_computation.11 | async-start | bytes 1705984 | tf_op jit(solution)/shard_map/all_gather | solution.py:298
  8.7 180.3 %all-gather.13.cloned.1.call-start = ((), (), s32[]{:S(2)}) async-start(), calls=%async_computation.12 | async-start | bytes 18522112 | tf_op jit(solution)/shard_map/all_gather | solution.py:299
  9.4 258.6 %all-gather.15.cloned.1.call-start = ((), (), s32[]{:S(2)}) async-start(), calls=%async_computation.13 | async-start | bytes 9261056 | tf_op jit(solution)/shard_map/all_gather | solution.py:300
  10.0 432.9 %reduce-scatter.12.cloned.1.call-start = ((), (), s32[]{:S(2)}) async-start(), calls=%async_computation.7 | async-start | bytes 655360 | tf_op jit(solution)/shard_map/reduce_scatter | solution.py:236
  10.7 43.5 %copy-start.162 = (f32[1152]{0:T(1024)}, f32[1152]{0:T(1024)S(1)}, u32[]{:S(2)}) copy-start(f32[1152]{0:T(1024)S(1)} %reduce.1) | copy-start | bytes 13828
  14.3 39.9 %copy-start.152 = (f32[256]{0:T(256)}, f32[256]{0:T(256)S(1)}, u32[]{:S(2)}) copy-start(f32[256]{0:T(256)S(1)} %fusion.242) | copy-start | bytes 3076
  98.5 99.5 %copy-start.154 = (f32[256]{0:T(256)}, f32[256]{0:T(256)S(1)}, u32[]{:S(2)}) copy-start(f32[256]{0:T(256)S(1)} %get-tuple-element.148) | copy-start | bytes 3076
  99.6 89.4 %copy-start.58 = (bf16[256,896]{1,0:T(8,128)(2,1)}, bf16[256,896]{1,0:T(8,128)(2,1)S(1)}, u32[]{:S(2)}) copy-start(bf16[256,896]{1,0:T(8,128)(2,1)S(1)} %multiply_convert_fusion.7) | copy-start | bytes 1376260
  203.2 72.3 %copy-start.17 = (bf16[256,4864]{1,0:T(8,128)(2,1)}, bf16[256,4864]{1,0:T(8,128)(2,1)S(1)}, u32[]{:S(2)}) copy-start(bf16[256,4864]{1,0:T(8,128)(2,1)S(1)} %fusion.71) | copy-start | bytes 7471108
  203.2 86.5 %copy-start.153 = (f32[256]{0:T(256)S(1)}, f32[256]{0:T(256)}, u32[]{:S(2)}) copy-start(f32[256]{0:T(256)} %copy-done.152) | copy-start | bytes 3076
  203.2 87.3 %copy-start.163 = (f32[1152]{0:T(1024)S(1)}, f32[1152]{0:T(1024)}, u32[]{:S(2)}) copy-start(f32[1152]{0:T(1024)} %copy-done.162) | copy-start | bytes 13828
  275.5 14.0 collective-permute-start
  289.5 43.2 %copy-start.31 = (bf16[256,896]{1,0:T(8,128)(2,1)}, bf16[256,896]{1,0:T(8,128)(2,1)S(1)}, u32[]{:S(2)}) copy-start(bf16[256,896]{1,0:T(8,128)(2,1)S(1)} %collective-permute-done) | copy-start | bytes 1376260
  328.8 53.3 %copy-start.144 = (f32[7,256]{1,0:T(8,128)}, f32[7,256]{1,0:T(8,128)S(1)}, u32[]{:S(2)}) copy-start(f32[7,256]{1,0:T(8,128)S(1)} %log_add_fusion.2) | copy-start | bytes 21508
  330.7 51.4 %copy-start.146 = (f32[7,256]{1,0:T(8,128)}, f32[7,256]{1,0:T(8,128)S(1)}, u32[]{:S(2)}) copy-start(f32[7,256]{1,0:T(8,128)S(1)} %log_add_fusion.3) | copy-start | bytes 21508
  423.9 189.1 %reduce-scatter.14.cloned.1.call-start = ((), (), s32[]{:S(2)}) async-start(), calls=%async_computation.8 | async-start | bytes 655360 | tf_op jit(solution)/shard_map/reduce_scatter | solution.py:236
  433.8 10.1 collective-permute-start.1
  443.9 46.6 %copy-start.60 = (bf16[256,896]{1,0:T(8,128)(2,1)}, bf16[256,896]{1,0:T(8,128)(2,1)S(1)}, u32[]{:S(2)}) copy-start(bf16[256,896]{1,0:T(8,128)(2,1)S(1)} %collective-permute-done.1) | copy-start | bytes 1376260
  478.2 46.1 %copy-start.92 = (bf16[256,14,64]{0,2,1:T(8,128)(2,1)}, bf16[256,14,64]{0,2,1:T(8,128)(2,1)S(1)}, u32[]{:S(2)}) copy-start(bf16[256,14,64]{0,2,1:T(8,128)(2,1)S(1)} %get-tuple-element.76) | copy-start | bytes 1376260
  481.4 42.8 %copy-start.44 = (bf16[1024,256]{1,0:T(8,128)(2,1)}, bf16[1024,256]{1,0:T(8,128)(2,1)S(1)}, u32[]{:S(2)}) copy-start(bf16[1024,256]{1,0:T(8,128)(2,1)S(1)} %get-tuple-element.74) | copy-start | bytes 1572868
  491.3 48.7 %copy-start.101 = (f32[256,896]{1,0:T(8,128)}, f32[256,896]{1,0:T(8,128)S(1)}, u32[]{:S(2)}) copy-start(f32[256,896]{1,0:T(8,128)S(1)} %get-tuple-element.162) | copy-start | bytes 2752516
  492.0 36.4 %collective-permute-start.2 = (bf16[256,896]{1,0:T(8,128)(2,1)S(1)}, bf16[256,896]{1,0:T(8,128)(2,1)S(1)}, u32[]{:S(2)}, u32[]{:S(2)}) collective-permute-start(bf16[256,896]{1,0:T(8,128)(2,1)S(1)} %copy-done.132), channel_id=1, source_target_pairs={{16,0},{17,1},{18,2},{19,3},{20,4},{21,5},{22,6},{23,7},{24,8},{25... | collective-permute-start | bytes 1376264 | tf_op jit(solution)/shard_map/ppermute | solution.py:17
  593.9 122.8 %reduce-scatter.16.cloned.1.call-start = ((), (), s32[]{:S(2)}) async-start(), calls=%async_computation.9 | async-start | bytes 655360 | tf_op jit(solution)/shard_map/reduce_scatter | solution.py:236
  620.1 12.4 collective-permute-start.3
  696.9 227.5 %reduce-scatter.24.cloned.1.call-start = ((), (), s32[]{:S(2)}) async-start(), calls=%async_computation.17 | async-start | bytes 3411968
  707.9 216.6 %reduce-scatter.22.cloned.1.call-start = ((), (), s32[]{:S(2)}) async-start(), calls=%async_computation.16 | async-start | bytes 4386816
  724.4 327.7 %reduce-scatter.20.cloned.1.call-start = ((), (), s32[]{:S(2)}) async-start(), calls=%async_computation.15 | async-start | bytes 18522112 | tf_op jit(solution)/shard_map/reduce_scatter | solution.py:269
  770.8 631.4 %reduce-scatter.18.cloned.1.call-start = ((), (), s32[]{:S(2)}) async-start(), calls=%async_computation.14 | async-start | bytes 37044224 | tf_op jit(solution)/shard_map/reduce_scatter | solution.py:268
  857.5 62.6 %copy-start.24 = (f32[256,896]{1,0:T(8,128)S(1)}, f32[256,896]{1,0:T(8,128)}, u32[]{:S(2)}) copy-start(f32[256,896]{1,0:T(8,128)} %copy-done.22) | copy-start | bytes 2752516
  857.5 62.6 %copy-start.34 = (bf16[256,896]{1,0:T(8,128)(2,1)S(1)}, bf16[256,896]{1,0:T(8,128)(2,1)}, u32[]{:S(2)}) copy-start(bf16[256,896]{1,0:T(8,128)(2,1)} %copy-done.31) | copy-start | bytes 1376260
  857.5 62.6 %copy-start.53 = (f32[256,896]{1,0:T(8,128)S(1)}, f32[256,896]{1,0:T(8,128)}, u32[]{:S(2)}) copy-start(f32[256,896]{1,0:T(8,128)} %copy-done.52) | copy-start | bytes 2752516
  (173 other events, 1537.3 us)
Sparse Core Ops, SparseCore 0:
  10.2 43.9 all-gather.8
  56.3 39.9 all-gather.10
  97.9 91.0 all-gather.12
  191.0 76.9 all-gather.14
  424.0 18.8 reduce-scatter.11
  594.0 18.9 reduce-scatter.13
  697.0 19.7 reduce-scatter.15
  721.2 67.4 reduce-scatter.23
  793.2 70.8 reduce-scatter.21
  868.7 183.3 reduce-scatter.19
  1057.0 345.1 reduce-scatter.17
where the time goes:
time: 1420 us; the launch traced here: 1410 us
  waiting for transfers between devices  711 us (50%)
  matrix products  421 us (30%)
  blocking collectives  108 us (8%)
  other arithmetic  97 us (7%)
  local copies, waits for them, and re-layouts  44.6 us (3%)
  between operations  16.9 us (1%)
    reduce_scatter x1, waiting for transfers between devices, reduce_weights(): lax.psum_scatter(weight_terms[2], ('blk', 'fsdp'), scatter_dimension=0, t...  350 us
    reduce_scatter x1, waiting for transfers between devices, reduce_weights(): lax.psum_scatter(weight_terms[3], ('blk', 'fsdp'), scatter_dimension=0, t...  128 us
    all_gather x1, waiting for transfers between devices, shards(): lax.all_gather(w_gate_up[0], ('blk', 'fsdp'), axis=0, tiled=True)  89.4 us
    dot_general x3, matrix products, layer_backward(): lax.dot_general(normed_two, grad_gate_up, over_rows, preferred_element_ty...  76.5 us
    all_gather x1, waiting for transfers between devices, shards(): lax.all_gather(w_down[0], ('blk', 'fsdp'), axis=0, tiled=True)  64.8 us
    psum x1, blocking collectives, shards(): lax.psum((small_totals[0], small_totals[1], small_totals[2]), ('blk', 'fs...  58.7 us
    dot_general x3, matrix products, layer_forward(): jnp.dot(normed_two, weight_gate_up, preferred_element_type=jnp.float32)  51.4 us
    all_gather x3, blocking collectives, layer_forward(): pairs_all = lax.all_gather(pairs, 'blk', axis=0, tiled=True)  49.3 us
  transfers between devices with their start and end apart: 15, of which 11 were waited for; matrix products, arithmetic and copies ran while one was open for 18% of the time, Pallas kernels for 0%

commit v1 on v0

v1 whole, which is shorter than its diff:
```python
import functools
import math

import jax
import jax.numpy as jnp
from jax import lax
from jax.experimental import pallas as pl
from jax.experimental.pallas import tpu as pltpu
from jax.sharding import PartitionSpec as P

H = 14
KVH = 2
HD = 64
GROUP = H // KVH
LONGEST = 512
NEG = -1e30
BF = jnp.bfloat16
F32 = jnp.float32
MESH = pl.DeviceIdType.MESH
VMEM_LIMIT = 60 * 2**20
VM = pl.BlockSpec(memory_space=pltpu.VMEM)
AN = pl.BlockSpec(memory_space=pl.ANY)


def nn(a, b):
    return lax.dot_general(a, b, (((1,), (0,)), ((), ())), preferred_element_type=F32)


def nt(a, b):
    return lax.dot_general(a, b, (((1,), (1,)), ((), ())), preferred_element_type=F32)


def tn(a, b):
    return lax.dot_general(a, b, (((0,), (0,)), ((), ())), preferred_element_type=F32)


def other(f):
    return f + 1 - 2 * (f % 2)


class Place:
    def __init__(self, dims):
        self.ns, self.nb, self.nf = dims
        self.count = self.ns * self.nf
        self.s = lax.axis_index("section")
        self.b = lax.axis_index("blk")
        self.f = lax.axis_index("fsdp")
        self.me = self.s * self.nf + self.f
        self.two_level = self.ns == 2 and self.nf == 4

    def plane(self, e):
        q = (self.me + e) % self.count
        return (q // self.nf, self.b, q % self.nf)

    def slot_from(self, e):
        return (self.me + self.count - e) % self.count

    def along(self, d):
        return (self.s, (self.b + d) % self.nb, self.f)

    def mates(self):
        s, b, f = (self.s, self.b, self.f)
        xf = (f + 2) % 4
        return ((s, b, other(f)), (s, b, xf), (1 - s, b, f))

    def slots(self):
        s, f = (self.s, self.f)
        xf = (f + 2) % 4
        t = 1 - s
        return (
            s * 4 + f,
            s * 4 + other(f),
            s * 4 + xf,
            t * 4 + f,
            s * 4 + other(xf),
            t * 4 + other(f),
            t * 4 + xf,
            t * 4 + other(xf),
        )


def pick(i, values):
    total = 0
    for k, v in enumerate(values):
        total = total + jnp.where(i == k, v, 0)
    return total


def greet(place, plane, along):
    barrier = pltpu.get_barrier_semaphore()
    count = 0
    if plane:
        if place.two_level and plane == "mates":
            targets = list(place.mates())
        else:
            targets = [place.plane(e) for e in range(1, place.count)]
        for t in targets:
            pl.semaphore_signal(barrier, 1, device_id=t, device_id_type=MESH)
        count += len(targets)
    if along:
        for d in range(1, place.nb):
            pl.semaphore_signal(barrier, 1, device_id=place.along(d), device_id_type=MESH)
        count += place.nb - 1
    pl.semaphore_wait(barrier, count)


def remote(src, dst, ssem, rsem, device):
    return pltpu.make_async_remote_copy(
        src_ref=src,
        dst_ref=dst,
        send_sem=ssem,
        recv_sem=rsem,
        device_id=device,
        device_id_type=MESH,
    )


class PlaneGather:
    def __init__(self, place, slot, ssem, rsem):
        self.place, self.slot, self.ssem, self.rsem = (place, slot, ssem, rsem)
        if place.two_level:
            self.order = place.slots()
        else:
            self.order = tuple(place.slot_from(e) for e in range(place.count))

    def copy(self, k, q, device):
        v = self.slot(q)
        return remote(v, v, self.ssem.at[k], self.rsem.at[k], device)

    def start(self):
        pc = self.place
        if pc.two_level:
            core, xm, ym = pc.mates()
            self.copy(1, self.order[0], xm).start()
            self.copy(2, self.order[0], ym).start()
            self.copy(0, self.order[0], core).start()
        else:
            for e in range(1, pc.count):
                self.copy(e - 1, self.order[0], pc.plane(e)).start()

    def waited(self, k):
        self.copy(k, self.order[k + 1], self.place.plane(1)).wait_recv()

    def before(self, step):
        if step == 0:
            return
        pc = self.place
        if not pc.two_level:
            self.waited(step - 1)
            return
        core, xm, ym = pc.mates()
        c = pc.f % 2
        if step == 2:
            self.waited(1)
            self.copy(3, self.order[2], core).start()
            self.waited(2)
            self.copy(4, self.order[3], core).start()
            which = c * self.order[3] + (1 - c) * self.order[2]
            far = (
                c * xm[0] + (1 - c) * ym[0],
                pc.b,
                c * xm[2] + (1 - c) * ym[2],
            )
            self.copy(5, which, far).start()
        elif step == 3:
            return
        elif step == 6:
            self.waited(5)
            self.copy(6, self.order[6], core).start()
        else:
            self.waited(step - 1)

    def finish(self):
        n = self.place.count - 1
        for k in range(n):
            self.copy(k, self.order[0], self.place.plane(1)).wait_send()


class PlaneScatter:
    def __init__(self, place, near, away, back, hop, ssem, rsem):
        self.place = place
        self.near, self.away, self.back, self.hop = (near, away, back, hop)
        self.ssem, self.rsem = (ssem, rsem)

    def put(self, step, value):
        pc = self.place
        if not pc.two_level:
            @pl.when(step == 0)
            def _():
                self.near[0] = value

            @pl.when(step > 0)
            def _():
                e = pc.count - step
                self.away[e - 1] = value.astype(BF)
                q = (pc.me + e) % pc.count
                remote(
                    self.away.at[e - 1],
                    self.back.at[e - 1],
                    self.ssem.at[e - 1],
                    self.rsem.at[e - 1],
                    (q // pc.nf, pc.b, q % pc.nf),
                ).start()
            return
        core, xm, ym = pc.mates()
        here = (step == 0) | (step == 2) | (step == 3) | (step == 6)
        q = pick(step, (0, 0, 1, 2, 1, 2, 3, 3))

        @pl.when(here)
        def _():
            self.near[q] = value

        @pl.when(jnp.logical_not(here))
        def _():
            self.away[q] = value.astype(BF)
            self.core_copy(q).start()

    def core_copy(self, q):
        core = self.place.mates()[0]
        return remote(self.away.at[q], self.back.at[q], self.ssem.at[q], self.rsem.at[q], core)

    def hop_copy(self, k, device):
        return remote(
            self.hop.at[k], self.hop.at[k + 3], self.ssem.at[4 + k], self.rsem.at[4 + k], device
        )

    def targets(self):
        pc = self.place
        core, xm, ym = pc.mates()
        c = pc.f % 2
        first = (c * xm[0] + (1 - c) * ym[0], pc.b, c * xm[2] + (1 - c) * ym[2])
        second = (c * ym[0] + (1 - c) * xm[0], pc.b, c * ym[2] + (1 - c) * xm[2])
        return (first, second)

    def early(self):
        pc = self.place
        if not pc.two_level:
            return
        c = pc.f % 2
        first, second = self.targets()
        self.core_copy(1).wait_recv()
        self.core_copy(2).wait_recv()
        q = c * 1 + (1 - c) * 2
        self.hop[0] = (self.near[q] + self.back[q].astype(F32)).astype(BF)
        self.hop_copy(0, first).start()

    def diagonal(self):
        pc = self.place
        if not pc.two_level:
            return
        first, second = self.targets()
        self.core_copy(3).wait_recv()
        self.hop[1] = (self.near[3] + self.back[3].astype(F32)).astype(BF)
        self.hop_copy(1, first).start()

    def result(self, store):
        pc = self.place
        if not pc.two_level:
            total = self.near[0]
            for e in range(1, pc.count):
                remote(self.away.at[e - 1], self.back.at[e - 1], self.ssem.at[e - 1],
                       self.rsem.at[e - 1], pc.plane(e)).wait()
                total = total + self.back[e - 1].astype(F32)
            store(total)
            return
        c = pc.f % 2
        first, second = self.targets()
        self.hop_copy(1, first).wait_recv()
        q = c * 2 + (1 - c) * 1
        self.hop[2] = (
            self.near[q] + self.back[q].astype(F32) + self.hop[4].astype(F32)
        ).astype(BF)
        self.hop_copy(2, second).start()
        self.core_copy(0).wait_recv()
        self.hop_copy(0, first).wait_recv()
        part = self.near[0] + self.back[0].astype(F32) + self.hop[3].astype(F32)
        self.near[0] = part
        self.hop_copy(2, second).wait_recv()
        store(self.near[0] + self.hop[5].astype(F32))
        for q in range(4):
            self.core_copy(q).wait_send()
        self.hop_copy(0, first).wait_send()
        self.hop_copy(1, first).wait_send()
        self.hop_copy(2, second).wait_send()


def scatter_scratch(dims, rows, cols):
    count = dims[0] * dims[2]
    if dims[0] == 2 and dims[2] == 4:
        near, away, hops, sems = (4, 4, 6, 7)
    else:
        near, away, hops, sems = (1, count - 1, 1, count - 1)
    return [
        pltpu.VMEM((near, rows, cols), F32),
        pltpu.VMEM((away, rows, cols), BF),
        pltpu.VMEM((away, rows, cols), BF),
        pltpu.VMEM((hops, rows, cols), BF),
        pltpu.SemaphoreType.DMA((sems,)),
        pltpu.SemaphoreType.DMA((sems,)),
    ]


def call(kernel, name, cid, outs, out_specs, in_specs, scratch, args):
    params = pltpu.CompilerParams(
        collective_id=cid, has_side_effects=True, vmem_limit_bytes=VMEM_LIMIT
    )
    return pl.pallas_call(
        kernel,
        name=name,
        out_shape=outs,
        in_specs=in_specs,
        out_specs=out_specs,
        scratch_shapes=scratch,
        compiler_params=params,
    )(*args)


def gather_weights_kernel(dims, gu, wd, qo, gu_all, wd_all, qo_all, lsem, ps, pr, zs, zr, qs, qr):
    pc = Place(dims)
    ns, nb, nf = dims
    greet(pc, "all", True)
    local = [
        pltpu.make_async_copy(qo, qo_all.at[pc.s, pc.f, pc.b], lsem.at[0]),
        pltpu.make_async_copy(gu.at[pc.s, pc.f], gu_all.at[pc.s, pc.b, pc.f], lsem.at[1]),
        pltpu.make_async_copy(wd.at[pc.s], wd_all.at[pc.s, pc.b], lsem.at[2]),
    ]
    mine = qo_all.at[pc.s, pc.f, pc.b]
    firsts = [remote(qo, mine, qs.at[d - 1], qr.at[d - 1], pc.along(d)) for d in range(1, nb)]
    for c in firsts:
        c.start()
    for c in local:
        c.start()
    plane = []
    for e in range(1, pc.count):
        t = pc.plane(e)
        plane.append(
            remote(gu.at[t[0], t[2]], gu_all.at[pc.s, pc.b, pc.f], ps.at[e - 1], pr.at[e - 1], t)
        )
    for d in range(1, ns):
        y = (pc.s + d) % ns
        k = pc.count - 1 + d - 1
        plane.append(
            remote(wd.at[y], wd_all.at[pc.s, pc.b], ps.at[k], pr.at[k], (y, pc.b, pc.f))
        )
    for c in plane:
        c.start()
    for c in local:
        c.wait()
    for c in firsts:
        c.wait()
    base = nb - 1
    gather = PlaneGather(
        pc,
        lambda q: qo_all.at[q // nf, q % nf],
        qs.at[pl.ds(base, pc.count - 1)],
        qr.at[pl.ds(base, pc.count - 1)],
    )
    gather.start()
    for c in plane:
        c.wait()
    lines = []
    k = 0
    for d in range(1, nb):
        for l in range(ns):
            for ref in (gu_all, wd_all):
                lines.append(
                    remote(ref.at[l, pc.b], ref.at[l, pc.b], zs.at[k], zr.at[k], pc.along(d))
                )
                k += 1
    for c in lines:
        c.start()
    for step in range(pc.count):
        gather.before(step)
    gather.finish()
    for c in lines:
        c.wait()


def gather_weights(dims, gu, wd, qo):
    ns, nb, nf = dims
    count = ns * nf
    half, width = wd.shape[1:]
    outs = (
        jax.ShapeDtypeStruct((ns, nb) + gu.shape[1:], BF),
        jax.ShapeDtypeStruct((ns, nb, half, width), BF),
        jax.ShapeDtypeStruct((ns, nf, nb) + qo.shape, BF),
    )
    dma = pltpu.SemaphoreType.DMA
    n_plane = count - 1 + ns - 1
    n_line = (nb - 1) * ns * 2
    n_qo = nb - 1 + count - 1
    return call(
        functools.partial(gather_weights_kernel, dims),
        "gather_weights",
        0,
        outs,
        [AN] * 3,
        [AN] * 3,
        [dma((3,)), dma((n_plane,)), dma((n_plane,)), dma((n_line,)), dma((n_line,)),
         dma((n_qo,)), dma((n_qo,))],
        (gu, wd, qo),
    )


def rms(values):
    return lax.rsqrt(jnp.mean(values * values, axis=0, keepdims=True) + 1e-06)


def attention_forward_kernel(
    dims, nk, h_ref, w_ref, wo_ref, bias_ref, g1_ref, g2_ref, cos_ref, sin_ref, mask_ref,
    normed_ref, q_ref, kv_ref, lse_ref, mixed_ref, res_ref, n2_ref,
    joined, ssem, rsem,
):
    pc = Place(dims)
    width, rows = h_ref.shape
    hidden = h_ref[...]
    normed = (hidden * rms(hidden) * g1_ref[...]).astype(BF)
    normed_ref[...] = normed
    joined[...] = tn(w_ref[...], normed) + bias_ref[...]
    cos_part = cos_ref[...]
    sin_part = sin_ref[...]
    half = HD // 2
    greet(pc, None, True)

    def turned(row):
        u1 = joined[pl.ds(row, half), :]
        u2 = joined[pl.ds(row + half, half), :]
        return (u1 * cos_part - u2 * sin_part, u2 * cos_part + u1 * sin_part)

    for g in range(KVH):
        r1, r2 = turned((H + g) * HD)
        kv_ref[0, g, :half, :] = r1.astype(BF)
        kv_ref[0, g, half:, :] = r2.astype(BF)
        v0 = (H + KVH + g) * HD
        kv_ref[0, KVH + g] = joined[v0 : v0 + HD, :].astype(BF)
    sends = [
        remote(kv_ref.at[0], kv_ref.at[j], ssem.at[j - 1], rsem.at[j - 1], pc.along(j))
        for j in range(1, nk)
    ]
    for c in sends:
        c.start()
    scale = HD**-0.5
    for head in range(H):
        r1, r2 = turned(head * HD)
        q_ref[head, :half, :] = (r1 * scale).astype(BF)
        q_ref[head, half:, :] = (r2 * scale).astype(BF)
    for c in sends:
        c.wait()
    for g in range(KVH):
        keys = [kv_ref[j, g].T for j in range(nk)]
        values = [kv_ref[j, KVH + g] for j in range(nk)]

        def one_head(i, carry):
            head = g * GROUP + i
            q = q_ref[head]
            s = [nn(keys[j], q) + mask_ref[j] for j in range(nk)]
            top = s[0].max(axis=0, keepdims=True)
            for j in range(1, nk):
                top = jnp.maximum(top, s[j].max(axis=0, keepdims=True))
            e = [jnp.exp(x - top) for x in s]
            total = e[0].sum(axis=0, keepdims=True)
            for j in range(1, nk):
                total = total + e[j].sum(axis=0, keepdims=True)
            out = nn(values[0], e[0].astype(BF))
            for j in range(1, nk):
                out = out + nn(values[j], e[j].astype(BF))
            lse_ref[head] = top + jnp.log(total)
            mixed_ref[head] = (out / total).astype(BF)
            return carry

        lax.fori_loop(0, GROUP, one_head, 0)
    mixed = mixed_ref[...].reshape(H * HD, rows)
    residual = h_ref[...] + tn(wo_ref[...], mixed)
    res_ref[...] = residual
    n2_ref[...] = (residual * rms(residual) * g2_ref[...]).astype(BF)


def attention_forward(dims, nk, cid, hidden, w, wo, bias, g1, g2, cos_part, sin_part, mask):
    width, rows = hidden.shape
    sds = jax.ShapeDtypeStruct
    outs = (
        sds((width, rows), BF),
        sds((H, HD, rows), BF),
        sds((nk, 2 * KVH, HD, rows), BF),
        sds((H, 1, rows), F32),
        sds((H, HD, rows), BF),
        sds((width, rows), F32),
        sds((width, rows), BF),
    )
    dma = pltpu.SemaphoreType.DMA
    return call(
        functools.partial(attention_forward_kernel, dims, nk),
        "attention_forward",
        cid,
        outs,
        [VM] * 7,
        [VM] * 9,
        [pltpu.VMEM((w.shape[1], rows), F32), dma((nk - 1,)), dma((nk - 1,))],
        (hidden, w, wo, bias, g1, g2, cos_part, sin_part, mask),
    )


def folded(v):
    out = v[:, :128]
    for k in range(1, v.shape[1] // 128):
        out = out + v[:, k * 128 : (k + 1) * 128]
    return out


def attention_backward_kernel(
    dims, nk, g_ref, w_ref, wo_ref, g1_ref, cos_ref, sin_ref, mask_ref,
    h_ref, normed_ref, q_ref, kv_ref, lse_ref, mixed_ref,
    gh_ref, dw_ref, dwo_ref, dg1_ref, db_ref,
    dmix, dkv, out_kv, in_kv, gj, ssem, rsem,
):
    pc = Place(dims)
    width, rows = h_ref.shape
    greet(pc, None, True)
    grl = g_ref[...].astype(BF)
    dmix[...] = nn(wo_ref[...], grl).astype(BF).reshape(dmix.shape)
    dwo_ref[...] = nt(mixed_ref[...].reshape(H * HD, rows), grl).astype(BF)
    cos_part = cos_ref[...]
    sin_part = sin_ref[...]
    half = HD // 2
    scale = HD**-0.5
    dkv[...] = jnp.zeros_like(dkv)

    def unturned(d1, d2):
        return (d1 * cos_part + d2 * sin_part, d2 * cos_part - d1 * sin_part)

    for g in range(KVH):
        keys_t = [kv_ref[j, g] for j in range(nk)]
        keys = [k.T for k in keys_t]
        values = [kv_ref[j, KVH + g].T for j in range(nk)]

        def one_head(i, carry):
            head = g * GROUP + i
            q = q_ref[head]
            do = dmix[head]
            lse = lse_ref[head]
            p = [jnp.exp(nn(keys[j], q) + mask_ref[j] - lse) for j in range(nk)]
            dp = [nn(values[j], do) for j in range(nk)]
            delta = (p[0] * dp[0]).sum(axis=0, keepdims=True)
            for j in range(1, nk):
                delta = delta + (p[j] * dp[j]).sum(axis=0, keepdims=True)
            dq = jnp.zeros((HD, rows), F32)
            for j in range(nk):
                ds = (p[j] * (dp[j] - delta)).astype(BF)
                dkv[j, g] += nt(q, ds)
                dkv[j, KVH + g] += nt(do, p[j].astype(BF))
                dq = dq + nn(keys_t[j], ds)
            dq = dq * scale
            r1, r2 = unturned(dq[:half], dq[half:])
            gj[pl.ds(pl.multiple_of(head * HD, HD), half), :] = r1.astype(BF)
            gj[pl.ds(pl.multiple_of(head * HD + half, half), half), :] = r2.astype(BF)
            return carry

        lax.fori_loop(0, GROUP, one_head, 0)
    for j in range(1, nk):
        out_kv[j - 1] = dkv[j].astype(BF)
    sends = [
        remote(out_kv.at[j - 1], in_kv.at[j - 1], ssem.at[j - 1], rsem.at[j - 1],
               pc.along(pc.nb - j))
        for j in range(1, nk)
    ]
    for c in sends:
        c.start()
    for c in sends:
        c.wait()
    own = dkv[0]
    for j in range(1, nk):
        own = own + in_kv[j - 1].astype(F32)
    for g in range(KVH):
        r1, r2 = unturned(own[g, :half], own[g, half:])
        k0 = (H + g) * HD
        gj[k0 : k0 + half, :] = r1.astype(BF)
        gj[k0 + half : k0 + HD, :] = r2.astype(BF)
        v0 = (H + KVH + g) * HD
        gj[v0 : v0 + HD, :] = own[KVH + g].astype(BF)
    gjv = gj[...]
    db_ref[...] = folded(gjv.astype(F32))
    dw_ref[...] = nt(normed_ref[...], gjv).astype(BF)
    gn = nn(w_ref[...], gjv)
    hidden = h_ref[...]
    scale_one = rms(hidden)
    unit = hidden * scale_one
    dg1_ref[...] = folded(gn * unit)
    u = gn * g1_ref[...]
    gh_ref[...] = g_ref[...] + scale_one * (u - unit * jnp.mean(u * unit, axis=0, keepdims=True))


def attention_backward(dims, nk, cid, g, w, wo, g1, cos_part, sin_part, mask, hidden, normed, q,
                       kv, lse, mixed):
    width, rows = hidden.shape
    sds = jax.ShapeDtypeStruct
    outs = (
        sds((width, rows), F32),
        sds(w.shape, BF),
        sds(wo.shape, BF),
        sds((width, 128), F32),
        sds((w.shape[1], 128), F32),
    )
    dma = pltpu.SemaphoreType.DMA
    block = (2 * KVH, HD, rows)
    return call(
        functools.partial(attention_backward_kernel, dims, nk),
        "attention_backward",
        cid,
        outs,
        [VM] * 5,
        [VM] * 13,
        [
            pltpu.VMEM((H, HD, rows), BF),
            pltpu.VMEM((nk,) + block, F32),
            pltpu.VMEM((nk - 1,) + block, BF),
            pltpu.VMEM((nk - 1,) + block, BF),
            pltpu.VMEM((w.shape[1], rows), BF),
            dma((nk - 1,)),
            dma((nk - 1,)),
        ],
        (g, w, wo, g1, cos_part, sin_part, mask, hidden, normed, q, kv, lse, mixed),
    )


def steps_of(count):
    return (5, count - 1)


def lanes(slot, rows):
    return pl.ds(pl.multiple_of(slot * rows, rows), rows)


def transpose_into(dst, src):
    cols = src.shape[1]
    for c0 in range(0, cols, 128):
        c1 = min(c0 + 128, cols)
        dst[c0:c1, :] = src[:, c0:c1].T


def feed_forward_kernel(
    dims, x_ref, res_ref, wgu_ref, wd_ref,
    out_ref, x_all, gu_all,
    wgu_t, wd_t, gu, inner, near, away, back, hop, ss, sr, gs, gr,
):
    pc = Place(dims)
    width, rows = x_ref.shape
    ff = wd_ref.shape[0]
    greet(pc, "mates", False)
    gather = PlaneGather(pc, lambda q: x_all.at[:, lanes(q, rows)], gs, gr)
    scatter = PlaneScatter(pc, near, away, back, hop, ss, sr)
    x_all[:, lanes(pc.me, rows)] = x_ref[...]
    gather.start()
    transpose_into(wgu_t, wgu_ref)
    transpose_into(wd_t, wd_ref)
    neighbours, last = steps_of(pc.count)
    chunk = 32 if ff % 32 == 0 else 16

    def step_body(step, carry):
        for k in range(pc.count):
            @pl.when(step == k)
            def _():
                gather.before(k)

        slot = pick(step, gather.order)
        sl = lanes(slot, rows)
        gu[...] = nn(wgu_t[...], x_all[:, sl])

        def act(i, c):
            r = pl.multiple_of(i * chunk, chunk)
            gate = gu[pl.ds(r, chunk), :]
            up = gu[pl.ds(ff + r, chunk), :]
            gu_all[pl.ds(r, chunk), sl] = gate.astype(BF)
            gu_all[pl.ds(ff + r, chunk), sl] = up.astype(BF)
            inner[pl.ds(r, chunk), :] = (gate * jax.nn.sigmoid(gate) * up).astype(BF)
            return c

        lax.fori_loop(0, ff // chunk, act, 0)
        scatter.put(step, nn(wd_t[...], inner[...]))

        @pl.when(step == neighbours)
        def _():
            scatter.early()

        return carry

    lax.fori_loop(0, pc.count, step_body, 0)
    scatter.diagonal()

    def store(total):
        out_ref[...] = res_ref[...] + total

    scatter.result(store)
    gather.finish()


def feed_forward(dims, cid, x, residual, wgu, wd):
    width, rows = x.shape
    count = dims[0] * dims[2]
    two_ff, ff = (wgu.shape[1], wd.shape[0])
    sds = jax.ShapeDtypeStruct
    dma = pltpu.SemaphoreType.DMA
    return call(
        functools.partial(feed_forward_kernel, dims),
        "feed_forward",
        cid,
        (
            sds((width, rows), F32),
            sds((width, count * rows), BF),
            sds((two_ff, count * rows), BF),
        ),
        [VM] * 3,
        [VM] * 4,
        [
            pltpu.VMEM((two_ff, width), BF),
            pltpu.VMEM((width, ff), BF),
            pltpu.VMEM((two_ff, rows), F32),
            pltpu.VMEM((ff, rows), BF),
        ]
        + scatter_scratch(dims, width, rows)
        + [dma((count - 1,)), dma((count - 1,))],
        (x, residual, wgu, wd),
    )


def feed_backward_kernel(
    dims, g_ref, res_ref, x_all, gu_all, wgu_ref, wd_ref, g2_ref,
    gr_ref, dwgu_ref, dwd_ref, dg2_ref,
    g_all, inner, ggu, gi, near, away, back, hop, ss, sr, gs, gr,
):
    pc = Place(dims)
    width, rows = g_ref.shape
    ff = wd_ref.shape[0]
    greet(pc, "mates", False)
    gather = PlaneGather(pc, lambda q: g_all.at[:, lanes(q, rows)], gs, gr)
    scatter = PlaneScatter(pc, near, away, back, hop, ss, sr)
    g_all[:, lanes(pc.me, rows)] = g_ref[...].astype(BF)
    gather.start()
    neighbours, last = steps_of(pc.count)
    chunk = 32 if ff % 32 == 0 else 16

    def step_body(step, carry):
        for k in range(pc.count):
            @pl.when(step == k)
            def _():
                gather.before(k)

        slot = pick(step, gather.order)
        sl = lanes(slot, rows)
        gi[...] = nn(wd_ref[...], g_all[:, sl])

        def act(i, c):
            r = pl.multiple_of(i * chunk, chunk)
            gate = gu_all[pl.ds(r, chunk), sl].astype(F32)
            up = gu_all[pl.ds(ff + r, chunk), sl].astype(F32)
            grad = gi[pl.ds(r, chunk), :]
            sig = jax.nn.sigmoid(gate)
            silu = gate * sig
            inner[pl.ds(r, chunk), sl] = (silu * up).astype(BF)
            ggu[pl.ds(r, chunk), sl] = (grad * up * sig * (1.0 + gate * (1.0 - sig))).astype(BF)
            ggu[pl.ds(ff + r, chunk), sl] = (grad * silu).astype(BF)
            return c

        lax.fori_loop(0, ff // chunk, act, 0)
        scatter.put(step, nn(wgu_ref[...], ggu[:, sl]))

        @pl.when(step == neighbours)
        def _():
            scatter.early()

        return carry

    lax.fori_loop(0, pc.count, step_body, 0)
    scatter.diagonal()
    part = width // 2
    for r in range(2):
        dwgu_ref[r * part : (r + 1) * part, :] = nt(
            x_all[r * part : (r + 1) * part, :], ggu[...]
        ).astype(BF)
    dwd_ref[...] = nt(inner[...], g_all[...]).astype(BF)

    def store(total):
        residual = res_ref[...]
        scale_two = rms(residual)
        unit = residual * scale_two
        dg2_ref[...] = folded(total * unit)
        u = total * g2_ref[...]
        gr_ref[...] = g_ref[...] + scale_two * (
            u - unit * jnp.mean(u * unit, axis=0, keepdims=True)
        )

    scatter.result(store)
    gather.finish()


def feed_backward(dims, cid, g, residual, x_all, gu_all, wgu, wd, g2):
    width, rows = g.shape
    count = dims[0] * dims[2]
    two_ff, ff = (wgu.shape[1], wd.shape[0])
    sds = jax.ShapeDtypeStruct
    dma = pltpu.SemaphoreType.DMA
    return call(
        functools.partial(feed_backward_kernel, dims),
        "feed_backward",
        cid,
        (
            sds((width, rows), F32),
            sds(wgu.shape, BF),
            sds(wd.shape, BF),
            sds((width, 128), F32),
        ),
        [VM] * 4,
        [VM] * 7,
        [
            pltpu.VMEM((width, count * rows), BF),
            pltpu.VMEM((ff, count * rows), BF),
            pltpu.VMEM((two_ff, count * rows), BF),
            pltpu.VMEM((ff, rows), F32),
        ]
        + scatter_scratch(dims, width, rows)
        + [dma((count - 1,)), dma((count - 1,))],
        (g, residual, x_all, gu_all, wgu, wd, g2),
    )


def line_exchange_kernel(dims, count, *refs):
    pc = Place(dims)
    ins, outs, (lsem, ss, sr) = (refs[:count], refs[count : 2 * count], refs[2 * count :])
    greet(pc, None, True)
    copies = []
    k = 0
    for i in range(count):
        copies.append(
            pltpu.make_async_copy(ins[i].at[pc.b], outs[i].at[pc.b], lsem.at[i])
        )
        for d in range(1, pc.nb):
            t = pc.along(d)
            copies.append(remote(ins[i].at[t[1]], outs[i].at[pc.b], ss.at[k], sr.at[k], t))
            k += 1
    for c in copies:
        c.start()
    for c in copies:
        c.wait()


def line_exchange(dims, cid, arrays):
    n = len(arrays)
    dma = pltpu.SemaphoreType.DMA
    total = n * (dims[1] - 1)
    return call(
        functools.partial(line_exchange_kernel, dims, n),
        "line_exchange",
        cid,
        tuple(jax.ShapeDtypeStruct(a.shape, a.dtype) for a in arrays),
        [AN] * n,
        [AN] * n,
        [dma((n,)), dma((total,)), dma((total,))],
        tuple(arrays),
    )


def plane_exchange_kernel(dims, gu, wd, gu_out, wd_out, lsem, ss, sr):
    pc = Place(dims)
    greet(pc, "all", False)
    copies = [
        pltpu.make_async_copy(gu.at[pc.me], gu_out.at[pc.me], lsem.at[0]),
        pltpu.make_async_copy(wd.at[pc.s], wd_out.at[pc.s], lsem.at[1]),
    ]
    for e in range(1, pc.count):
        t = pc.plane(e)
        copies.append(
            remote(gu.at[t[0] * pc.nf + t[2]], gu_out.at[pc.me], ss.at[e - 1], sr.at[e - 1], t)
        )
    for d in range(1, pc.ns):
        k = pc.count - 1 + d - 1
        y = (pc.s + d) % pc.ns
        copies.append(remote(wd.at[y], wd_out.at[pc.s], ss.at[k], sr.at[k], (y, pc.b, pc.f)))
    for c in copies:
        c.start()
    for c in copies:
        c.wait()


def plane_exchange(dims, cid, gu, wd):
    dma = pltpu.SemaphoreType.DMA
    total = dims[0] * dims[2] - 1 + dims[0] - 1
    return call(
        functools.partial(plane_exchange_kernel, dims),
        "plane_exchange",
        cid,
        tuple(jax.ShapeDtypeStruct(a.shape, a.dtype) for a in (gu, wd)),
        [AN] * 2,
        [AN] * 2,
        [dma((2,)), dma((total,)), dma((total,))],
        (gu, wd),
    )


def small_reduce_kernel(
    dims, qo_ref, small_ref, qo_out, small_out,
    half_sum, z_out, z_in, sm_in, sm_mid, sm_line, near, away, back, hop, ss, sr, ps, pr, zs, zr, ws, wr,
):
    pc = Place(dims)
    ns, nb, nf = dims
    greet(pc, "all", True)
    smalls = [
        remote(small_ref, sm_in.at[e - 1], ps.at[e - 1], pr.at[e - 1], pc.plane(e))
        for e in range(1, pc.count)
    ]
    for c in smalls:
        c.start()
    scatter = PlaneScatter(pc, near, away, back, hop, ss, sr)
    if pc.two_level:
        order = pc.slots()
    else:
        order = tuple(pc.slot_from(e) for e in range(pc.count))
    neighbours, last = steps_of(pc.count)

    def step_body(step, carry):
        slot = pick(step, order)
        scatter.put(step, qo_ref[slot].astype(F32))

        @pl.when(step == neighbours)
        def _():
            scatter.early()

        return carry

    lax.fori_loop(0, pc.count, step_body, 0)
    scatter.diagonal()
    total = small_ref[...]
    for e, c in enumerate(smalls):
        c.wait()
        total = total + sm_in[e]
    sm_mid[...] = total
    lines = [
        remote(sm_mid, sm_line.at[d - 1], ws.at[d - 1], wr.at[d - 1], pc.along(d))
        for d in range(1, nb)
    ]
    for c in lines:
        c.start()

    def store(value):
        half_sum[...] = value

    scatter.result(store)
    part = half_sum.shape[0] // nb
    z_out[...] = half_sum[...].astype(BF).reshape(z_out.shape)
    sends = []
    for d in range(1, nb):
        t = pc.along(d)
        sends.append(
            remote(z_out.at[t[1]], z_in.at[d - 1], zs.at[d - 1], zr.at[d - 1], t)
        )
    for c in sends:
        c.start()
    mine = z_out[pc.b].astype(F32)
    for d, c in enumerate(sends):
        c.wait()
        mine = mine + z_in[d].astype(F32)
    qo_out[...] = mine
    total = sm_mid[...]
    for d, c in enumerate(lines):
        c.wait()
        total = total + sm_line[d]
    small_out[...] = total


def small_reduce(dims, cid, qo, small, dr):
    ns, nb, nf = dims
    count = ns * nf
    cols = qo.shape[2]
    sds = jax.ShapeDtypeStruct
    dma = pltpu.SemaphoreType.DMA
    return call(
        functools.partial(small_reduce_kernel, dims),
        "small_reduce",
        cid,
        (sds((dr, cols), F32), sds(small.shape, F32)),
        [VM] * 2,
        [VM] * 2,
        [
            pltpu.VMEM((nb * dr, cols), F32),
            pltpu.VMEM((nb, dr, cols), BF),
            pltpu.VMEM((nb - 1, dr, cols), BF),
            pltpu.VMEM((count - 1,) + small.shape, F32),
            pltpu.VMEM(small.shape, F32),
            pltpu.VMEM((nb - 1,) + small.shape, F32),
        ]
        + scatter_scratch(dims, nb * dr, cols)
        + [dma((count - 1,)), dma((count - 1,))]
        + [dma((nb - 1,))] * 4,
        (qo, small),
    )


def shards(
    dims,
    tokens_in,
    positions,
    doc_ids,
    out_grad,
    norm1_gain,
    w_qkv,
    b_qkv,
    w_out,
    norm2_gain,
    w_gate_up,
    w_down,
):
    ns, nb, nf = dims
    seqs, rows, width = tokens_in.shape
    length = doc_ids.shape[1]
    s = lax.axis_index("section")
    b = lax.axis_index("blk")
    dr = w_qkv.shape[1]
    qkv = w_qkv.shape[2]
    fr = w_down.shape[1]
    half = fr // ns
    ff = nb * half
    nk = min(nb, 1 + (LONGEST - 1 + rows - 1) // rows)

    gu = w_gate_up[0].reshape(dr, 2, nb, nf, ns, half).transpose(4, 3, 0, 1, 2, 5)
    gu = gu.reshape(ns, nf, dr, 2 * ff)
    wd = w_down[0].reshape(ns, half, width)
    qo = jnp.concatenate([w_qkv[0], w_out[0]], axis=1)
    gu_all, wd_all, qo_all = gather_weights(dims, gu, wd, qo)
    wgu = gu_all.reshape(ns, width, 2 * ff)
    wdn = wd_all.reshape(ns, ff, width)
    qo_all = qo_all.transpose(0, 2, 1, 3, 4).reshape(ns, width, qkv + width)
    wq = qo_all[:, :, :qkv]
    wo = qo_all[:, :, qkv:]

    small_in = jnp.concatenate([norm1_gain[0], norm2_gain[0], b_qkv[0]])
    small_all = lax.all_gather(small_in, "section", axis=0, tiled=False)
    g1 = small_all[:, :width, None]
    g2 = small_all[:, width : 2 * width, None]
    bias = small_all[:, 2 * width :, None]

    tokens = lax.dynamic_index_in_dim(tokens_in, s, 0, keepdims=False)
    cot = lax.dynamic_index_in_dim(out_grad, s, 0, keepdims=False)
    pos = lax.dynamic_index_in_dim(positions, s, 0, keepdims=False)
    docs = lax.dynamic_index_in_dim(doc_ids, s, 0, keepdims=False)
    freq = jnp.exp(jnp.arange(HD // 2, dtype=F32) * (-2.0 / HD) * math.log(1000000.0))
    phase = freq[:, None] * pos.astype(F32)[None, :]
    cos_part, sin_part = (jnp.cos(phase), jnp.sin(phase))
    query_rows = b * rows + jnp.arange(rows, dtype=jnp.int32)
    query_docs = lax.dynamic_slice_in_dim(docs, b * rows, rows)
    masks = []
    for j in range(nk):
        key_rows = (b - j) * rows + jnp.arange(rows, dtype=jnp.int32)
        start = lax.rem(b - j + nb, nb) * rows
        key_docs = lax.dynamic_slice_in_dim(docs, start, rows)
        live = (
            (key_rows[:, None] >= 0)
            & (key_rows[:, None] <= query_rows[None, :])
            & (key_docs[:, None] == query_docs[None, :])
        )
        masks.append(jnp.where(live, 0.0, NEG).astype(F32))
    mask = jnp.stack(masks)

    hidden = tokens.T.astype(F32)
    saved = []
    outputs = []
    for l in range(ns):
        normed, q, kv, lse, mixed, residual, n2 = attention_forward(
            dims, nk, 1 + l, hidden, wq[l], wo[l], bias[l], g1[l], g2[l], cos_part, sin_part, mask
        )
        out, x_all, gu_saved = feed_forward(dims, 3 + l, n2, residual, wgu[l], wdn[l])
        saved.append((hidden, normed, q, kv, lse, mixed, residual, x_all, gu_saved))
        outputs.append(out)
        hidden = out.astype(BF).astype(F32)
    g = cot.T.astype(F32)
    grads = [None] * ns
    line_in = []
    qo_terms = [None] * ns
    small_terms = [None] * ns
    for l in reversed(range(ns)):
        hidden, normed, q, kv, lse, mixed, residual, x_all, gu_saved = saved[l]
        gres, dwgu, dwd, dg2 = feed_backward(
            dims, 5 + l, g, residual, x_all, gu_saved, wgu[l], wdn[l], g2[l]
        )
        gh, dwq, dwo, dg1, db = attention_backward(
            dims, nk, 7 + l, gres, wq[l], wo[l], g1[l], cos_part, sin_part, mask, hidden, normed, q,
            kv, lse, mixed,
        )
        grads[l] = gh
        g = gh.astype(BF).astype(F32)
        line_in.append((dwgu.reshape(nb, nf * dr, 2 * ff), dwd.reshape(nb, half, width)))
        qo_terms[l] = jnp.concatenate([dwq, dwo], axis=1)
        small_terms[l] = jnp.concatenate([dg1.sum(1), dg2.sum(1), db.sum(1)])
    line_in.reverse()

    got = line_exchange(dims, 9, [a for pair in line_in for a in pair])
    summed = [a.astype(F32).sum(0) for a in got]
    gu_send = jnp.stack([summed[2 * l].reshape(nf, dr, 2 * ff) for l in range(ns)]).astype(BF)
    wd_send = jnp.stack([summed[2 * l + 1] for l in range(ns)]).astype(BF)
    gu_got, wd_got = plane_exchange(dims, 10, gu_send.reshape(ns * nf, dr, 2 * ff), wd_send)
    grad_gu = gu_got.reshape(ns, nf, dr, 2, nb, half).transpose(2, 3, 4, 1, 0, 5)
    grad_gu = grad_gu.reshape(dr, w_gate_up.shape[2]).astype(F32)
    grad_wd = wd_got.reshape(fr, width).astype(F32)
    qo_send = jnp.stack(qo_terms).reshape(ns, nb, nf, dr, qkv + width)
    qo_send = qo_send.transpose(0, 2, 1, 3, 4).reshape(ns * nf, nb * dr, qkv + width)
    small = jnp.stack(small_terms)
    small_size = small.shape[1]
    padded = -(-small_size // 1024) * 1024
    small = jnp.pad(small, ((0, 0), (0, padded - small_size))).reshape(-1, 128)
    grad_qo, small_sum = small_reduce(dims, 11, qo_send, small, dr)
    small_sum = small_sum.reshape(ns, padded)
    mine = lax.dynamic_index_in_dim(small_sum, s, 0, keepdims=False)

    def both(values):
        own = jnp.stack(values)
        keep = lax.dynamic_index_in_dim(own, s, 0, keepdims=False)
        give = lax.dynamic_index_in_dim(own, 1 - s, 0, keepdims=False)
        take = lax.ppermute(give.astype(BF), "section", [(0, 1), (1, 0)]).astype(F32)
        first = jnp.where(s == 0, keep, take).T
        second = jnp.where(s == 0, take, keep).T
        return jnp.stack([first, second])[None]

    return (
        both(outputs),
        both(grads),
        mine[None, :width],
        grad_qo[None, :, :qkv],
        mine[None, 2 * width : 2 * width + qkv],
        grad_qo[None, :, qkv:],
        mine[None, width : 2 * width],
        grad_gu[None],
        grad_wd[None],
    )


def solution(mesh):
    dims = (mesh.shape["section"], mesh.shape["blk"], mesh.shape["fsdp"])
    return jax.shard_map(
        functools.partial(shards, dims),
        mesh=mesh,
        in_specs=(
            P("fsdp", "blk", None),
            P("fsdp", "blk"),
            P("fsdp", None),
            P("fsdp", "blk", None),
            P("section", None),
            P("section", ("blk", "fsdp"), None),
            P("section", None),
            P("section", ("blk", "fsdp"), None),
            P("section", None),
            P("section", ("blk", "fsdp"), None),
            P("section", ("blk", "fsdp"), None),
        ),
        out_specs=(
            P("section", "fsdp", "blk", None),
            P("section", "fsdp", "blk", None),
            P("section", None),
            P("section", ("blk", "fsdp"), None),
            P("section", None),
            P("section", ("blk", "fsdp"), None),
            P("section", None),
            P("section", ("blk", "fsdp"), None),
            P("section", ("blk", "fsdp"), None),
        ),
        check_vma=False,
    )
```

time: 1420 us -> 863 us (0.61)
  Pallas kernels: 0 us -> 736 us
  waiting for transfers between devices: 711 us -> 0.01 us
  matrix products: 421 us -> 0 us
  blocking collectives: 108 us -> 4.4 us
  other arithmetic: 97 us -> 39.3 us
  local copies, waits for them, and re-layouts: 44.6 us -> 68.3 us
  between operations: 16.9 us -> 1.64 us
    pallas_call x0 -> x12, Pallas kernels: none -> 736 us  [call(): pl.pallas_call(kernel, name=name, out_shape=outs, in_specs=in_specs, out_...]
    reduce_scatter x5 -> x0, waiting for transfers between devices: 492 us -> none  [the longest x1 350 us: reduce_weights(): lax.psum_scatter(weight_terms[2], ('blk', 'fsdp'), scatter_dimension=0, t...]
    dot_general x78 -> x0, matrix products: 421 us -> none  [the longest x3 76.5 us: layer_backward(): lax.dot_general(normed_two, grad_gate_up, over_rows, preferred_element_ty...]
    all_gather x4 -> x0, waiting for transfers between devices: 201 us -> none  [the longest x1 89.4 us: shards(): lax.all_gather(w_gate_up[0], ('blk', 'fsdp'), axis=0, tiled=True)]
    psum x1 -> x0, blocking collectives: 58.7 us -> none  [shards(): lax.psum((small_totals[0], small_totals[1], small_totals[2]), ('blk', 'fs...]
    all_gather x3 -> x1, blocking collectives: 49.3 us -> 4.4 us  [shards(): small_all = lax.all_gather(small_in, 'section', axis=0, tiled=False)]
    convert_element_type x13 -> x8, other arithmetic: 49.6 us -> 10.5 us  [the longest x1 2.27 us: shards(): hidden = out.astype(BF).astype(F32)]
    unnamed x380 -> x50, local copies, waits for them, and re-layouts: 22 us -> 4.32 us
  transfers between devices with their start and end apart: 15 -> 2, of which waited for: 11 -> 0; matrix products, arithmetic and copies ran while one was open for 18% -> 7% of each run, Pallas kernels for 0% -> 27%
where the time goes in v1:
time: 863 us; the launch traced here: 851 us
  Pallas kernels  736 us (85%)
  local copies, waits for them, and re-layouts  68.3 us (8%)
  other arithmetic  39.3 us (5%)
    pallas_call x12, Pallas kernels, call(): pl.pallas_call(kernel, name=name, out_shape=outs, in_specs=in_specs, out_...  736 us
    convert_element_type x3, local copies, waits for them, and re-layouts, shards(): grad_gu = grad_gu.reshape(dr, w_gate_up.shape[2]).astype(F32)  19.3 us
  transfers between devices with their start and end apart: 2, of which 0 were waited for; matrix products, arithmetic and copies ran while one was open for 7% of the time, Pallas kernels for 27%

profile of v1, /device:TPU:0, one launch (start us, length us, event | category | flops | bytes accessed | tf_op | source)
XLA Modules:
  0.0 851.3 jit_solution(17840485498488014405)
XLA Ops:
  0.7 8.1 reshape_squeeze.6
  8.9 2.2 copy.73
  11.1 2.8 reshape.526.gu
  14.6 138.4 %gather_weights.1 = (bf16[2,4,4,56,1216]{4,3,2,1,0:T(8,128)(2,1)}, bf16[2,4,152,896]{3,2,1,0:T(8,128)(2,1)}, bf16[2,4,4,56,2048]{4,3,2,1,0:T(8,128)(2,1)}) custom-call(bf16[2,4,56,1216]{3,2,1,0:T(8,128)(2,1)} %reshape.526.gu, bf16[2,152,896]{2,1,0:T(8,128)(2,1)} %bitcast.147, bf16[56,2048]{1,0:T(8,128)(2,1)} %pad_maximum_fusion.6.qo), custom_call_target="tpu_custom_call" | custom-call | tf_op jit(solution)/shard_map/gather_weights/pallas_call | solution.py:307
  153.0 4.5 copy.50
  157.5 2.6 slice_bitcast_fusion
  160.1 2.1 slice_bitcast_fusion.2
  162.3 4.4 all-gather.1
  171.3 4.9 fusion.15
  179.9 60.9 %attention_forward.2 = (bf16[896,256]{1,0:T(8,128)(2,1)}, bf16[14,64,256]{2,1,0:T(8,128)(2,1)}, bf16[3,4,64,256]{3,2,1,0:T(8,128)(2,1)}, f32[14,1,256]{2,1,0:T(1...) custom-call(f32[896,256]{1,0:T(8,128)} %convert_bitcast_fusion.1.h_ref, ...), custom_call_target="tpu_custom_call" | custom-call | tf_op jit(solution)/shard_map/attention_forward/pallas_call | solution.py:307
  240.9 51.7 %feed_forward.2 = (f32[896,256]{1,0:T(8,128)}, bf16[896,2048]{1,0:T(8,128)(2,1)}, bf16[1216,2048]{1,0:T(8,128)(2,1)}) custom-call(bf16[896,256]{1,0:T(8,128)(2,1)} %get-tuple-element.59.x_ref, f32[896,256]{1,0:T(8,128)} %get-tuple-element.60.res_ref, bf16[896,1216]{1,0:T(8,128)(2,1)} %bitcast.116, bf16[608,896]{1,0:T(8,128)(2,1)} %bitcast.123), custom_call_target="tpu_custom_call" | custom-call | tf_op jit(solution)/shard_map/feed_forward/pallas_call | solution.py:307
  292.5 2.3 convert_convert_fusion.1.h_ref
  299.1 24.9 %attention_forward.3 = (bf16[896,256]{1,0:T(8,128)(2,1)}, bf16[14,64,256]{2,1,0:T(8,128)(2,1)}, bf16[3,4,64,256]{3,2,1,0:T(8,128)(2,1)}, f32[14,1,256]{2,1,0:T(1...) custom-call(f32[896,256]{1,0:T(8,128)} %convert_convert_fusion.1.h_ref, ...), custom_call_target="tpu_custom_call" | custom-call | tf_op jit(solution)/shard_map/attention_forward/pallas_call | solution.py:307
  324.0 51.9 %feed_forward.3 = (f32[896,256]{1,0:T(8,128)}, bf16[896,2048]{1,0:T(8,128)(2,1)}, bf16[1216,2048]{1,0:T(8,128)(2,1)}) custom-call(bf16[896,256]{1,0:T(8,128)(2,1)} %get-tuple-element.64.x_ref, f32[896,256]{1,0:T(8,128)} %get-tuple-element.65.res_ref, bf16[896,1216]{1,0:T(8,128)(2,1)} %bitcast.118, bf16[608,896]{1,0:T(8,128)(2,1)} %bitcast.125), custom_call_target="tpu_custom_call" | custom-call | tf_op jit(solution)/shard_map/feed_forward/pallas_call | solution.py:307
  375.9 53.3 %feed_backward.2 = (f32[896,256]{1,0:T(8,128)}, bf16[896,1216]{1,0:T(8,128)(2,1)}, bf16[608,896]{1,0:T(8,128)(2,1)}, f32[896,128]{1,0:T(8,128)}) custom-call(f32[896,256]{1,0:T(8,128)} %convert_bitcast_fusion.g_ref, f32[896,256]{1,0:T(8,128)} %get-tuple-element.65.res_ref, bf16[896,2048]{1,0:T(8,128)(2,1)} %get-tuple-element.67.x_all, ...), custom_call_target="tpu_custom_call" | custom-call | tf_op jit(solution)/shard_map/feed_backward/pallas_call | solution.py:307
  429.2 34.4 %attention_backward.2 = (f32[896,256]{1,0:T(8,128)}, bf16[896,1152]{1,0:T(8,128)(2,1)}, bf16[896,896]{1,0:T(8,128)(2,1)}, f32[896,128]{1,0:T(8,128)}, f32[1152,128]{1,0:T(8,128)}) custom-call(f32[896,256]{1,0:T(8,128)} %get-tuple-element.69.g_ref, bf16[896,1152]{1,0:T(8,128)(2,1)} %get-tuple-element.136.w_ref, bf16[896,896]{1,0:T(8,128)(2,1)} %get-tuple-element.134.wo_ref, ...), custom_call_target="tpu_custom_call" | custom-call | tf_op jit(solution)/shard_map/attention_backward/pallas_call | solution.py:307
  463.6 2.2 convert_convert_fusion.g_ref
  465.8 53.8 %feed_backward.3 = (f32[896,256]{1,0:T(8,128)}, bf16[896,1216]{1,0:T(8,128)(2,1)}, bf16[608,896]{1,0:T(8,128)(2,1)}, f32[896,128]{1,0:T(8,128)}) custom-call(f32[896,256]{1,0:T(8,128)} %convert_convert_fusion.g_ref, f32[896,256]{1,0:T(8,128)} %get-tuple-element.60.res_ref, bf16[896,2048]{1,0:T(8,128)(2,1)} %get-tuple-element.76.x_all, ...), custom_call_target="tpu_custom_call" | custom-call | tf_op jit(solution)/shard_map/feed_backward/pallas_call | solution.py:307
  519.6 33.2 %attention_backward.3 = (f32[896,256]{1,0:T(8,128)}, bf16[896,1152]{1,0:T(8,128)(2,1)}, bf16[896,896]{1,0:T(8,128)(2,1)}, f32[896,128]{1,0:T(8,128)}, f32[1152,128]{1,0:T(8,128)}) custom-call(f32[896,256]{1,0:T(8,128)} %get-tuple-element.78.g_ref, bf16[896,1152]{1,0:T(8,128)(2,1)} %get-tuple-element.137.w_ref, bf16[896,896]{1,0:T(8,128)(2,1)} %get-tuple-element.135.wo_ref, ...), custom_call_target="tpu_custom_call" | custom-call | tf_op jit(solution)/shard_map/attention_backward/pallas_call | solution.py:307
  562.8 2.8 pad_maximum_fusion.1
  566.0 2.3 pad_maximum_fusion.2
  568.3 2.7 pad_maximum_fusion
  571.0 4.3 copy.67
  575.3 63.5 %small_reduce.1 = (f32[56,2048]{1,0:T(8,128)}, f32[48,128]{1,0:T(8,128)}) custom-call(bf16[8,224,2048]{2,1,0:T(8,128)(2,1)} %bitcast.115, f32[48,128]{1,0:T(8,128)} %reshape.529.small_ref), custom_call_target="tpu_custom_call" | custom-call | tf_op jit(solution)/shard_map/small_reduce/pallas_call | solution.py:307
  642.1 148.1 %line_exchange.1 = (bf16[4,224,1216]{2,1,0:T(8,128)(2,1)}, bf16[4,152,896]{2,1,0:T(8,128)(2,1)}, bf16[4,224,1216]{2,1,0:T(8,128)(2,1)}, bf16[4,152,896]{2,1,0:T(8,128)(2,1)}) custom-call(bf16[4,224,1216]{2,1,0:T(8,128)(2,1)} %bitcast.139, bf16[4,152,896]{2,1,0:T(8,128)(2,1)} %bitcast.143, bf16[4,224,1216]{2,1,0:T(8,128)(2,1)} %bitcast.138, ...), custom_call_target="tpu_custom_call" | custom-call | tf_op jit(solution)/shard_map/line_exchange/pallas_call | solution.py:307
  792.7 2.3 reduce
  795.0 2.3 reduce.1
  800.3 21.6 %plane_exchange.1 = (bf16[8,56,1216]{2,1,0:T(8,128)(2,1)}, bf16[2,152,896]{2,1,0:T(8,128)(2,1)}) custom-call(bf16[8,56,1216]{2,1,0:T(8,128)(2,1)} %bitcast.133, bf16[2,152,896]{2,1,0:T(8,128)(2,1)} %pad_maximum_fusion.5.wd), custom_call_target="tpu_custom_call" | custom-call | tf_op jit(solution)/shard_map/plane_exchange/pallas_call | solution.py:307
  821.9 2.2 bitcast_convert_fusion
  824.8 6.9 reshape.539
  831.7 6.7 copy.64
  838.4 5.7 reshape.535
  (109 shorter events, 39.7 us)
Async XLA Ops:
  0.6 166.2 %copy-start = (bf16[2,256,896]{2,1,0:T(8,128)(2,1)S(1)}, bf16[2,256,896]{2,1,0:T(8,128)(2,1)}, u32[]{:S(2)}) copy-start(bf16[2,256,896]{2,1,0:T(8,128)(2,1)} %param.11) | copy-start | bytes 2752516
  11.1 2.8 copy-start.14
  11.1 2.8 copy-start.15
  160.1 2.1 copy-start.17
  160.1 2.1 copy-start.18
  160.1 2.2 copy-start.19
  160.1 6.7 copy-start.21
  171.3 4.9 copy-start.6
  176.2 2.3 copy-start.20
  292.5 5.3 copy-start.13
  519.6 33.2 %copy-start.3 = (f32[896,256]{1,0:T(8,128)S(1)}, f32[896,256]{1,0:T(8,128)}, u32[]{:S(2)}) copy-start(f32[896,256]{1,0:T(8,128)} %get-tuple-element.75) | copy-start | bytes 2752516
  552.8 2.7 copy-start.2
  552.8 2.7 copy-start.4
  552.9 3.9 copy-start.12
  553.8 5.7 copy-start.11
  553.8 291.0 %collective-permute-start.1 = (bf16[896,256]{1,0:T(8,128)(2,1)}, bf16[896,256]{1,0:T(8,128)(2,1)}, u32[]{:S(2)}, u32[]{:S(2)}) collective-permute-start(bf16[896,256]{1,0:T(8,128)(2,1)} %fusion.13), channel_id=1, source_target_pairs={{0,16},{16,0},{1,17},{17,1},{2,18},{18,2},{3,19},{19,3},{4,20},{20... | collective-permute-start | bytes 1376264 | tf_op jit(solution)/shard_map/ppermute | solution.py:1115
  556.4 291.3 %collective-permute-start = (bf16[896,256]{1,0:T(8,128)(2,1)}, bf16[896,256]{1,0:T(8,128)(2,1)}, u32[]{:S(2)}, u32[]{:S(2)}) collective-permute-start(bf16[896,256]{1,0:T(8,128)(2,1)} %fusion.12), channel_id=1, source_target_pairs={{0,16},{16,0},{1,17},{17,1},{2,18},{18,2},{3,19},{19,3},{4,20},{20... | collective-permute-start | bytes 1376264 | tf_op jit(solution)/shard_map/ppermute | solution.py:1115
  562.8 2.8 copy-start.7
  562.8 3.1 copy-start.8
  790.2 1.6 copy-start.10
  795.0 2.3 copy-start.16
  821.9 2.9 copy-start.9
  838.4 6.3 copy-start.5
  849.0 1.8 copy-start.1

commit v2 on v1

--- a/solution.py
+++ b/solution.py
@@ -284,17 +284,81 @@
         self.hop_copy(2, second).wait_send()
 
 
-def scatter_scratch(dims, rows, cols):
+class LineGather:
+    def __init__(self, place, piece, out, sems):
+        lsem, ss, sr = sems
+        own = out.at[place.b]
+        self.copies = [pltpu.make_async_copy(piece, own, lsem)]
+        for d in range(1, place.nb):
+            self.copies.append(remote(piece, own, ss.at[d - 1], sr.at[d - 1], place.along(d)))
+
+    def start(self):
+        for c in self.copies:
+            c.start()
+
+    def finish(self):
+        for c in self.copies:
+            c.wait()
+
+
+class LineExchange(LineGather):
+    def __init__(self, place, parts, out, sems):
+        lsem, ss, sr = sems
+        own = out(place.b)
+        self.copies = [pltpu.make_async_copy(parts(place.b), own, lsem)]
+        for d in range(1, place.nb):
+            t = place.along(d)
+            self.copies.append(remote(parts(t[1]), own, ss.at[d - 1], sr.at[d - 1], t))
+
+
+def line_sems(dims):
+    dma = pltpu.SemaphoreType.DMA
+    return [dma(()), dma((dims[1] - 1,)), dma((dims[1] - 1,))]
+
+
+def riders_of(place, specs, ins, outs, sems):
+    out = []
+    for i, spec in enumerate(specs):
+        mine = sems[3 * i : 3 * i + 3]
+        if spec[0] == "gather":
+            piece = ins[i] if spec[1] is None else ins[i].at[spec[1]]
+            out.append(LineGather(place, piece, outs[i], mine))
+        else:
+            lo, hi = spec[1]
+            out.append(
+                LineExchange(
+                    place,
+                    lambda t, r=ins[i]: r.at[t, lo:hi],
+                    lambda t, r=outs[i]: r.at[t],
+                    mine,
+                )
+            )
+    return out
+
+
+def rider_shapes(dims, specs, arrays):
+    out = []
+    for spec, a in zip(specs, arrays):
+        if spec[0] == "gather":
+            shape = a.shape if spec[1] is None else a.shape[1:]
+            out.append(jax.ShapeDtypeStruct((dims[1],) + shape, a.dtype))
+        else:
+            lo, hi = spec[1]
+            out.append(jax.ShapeDtypeStruct((a.shape[0], hi - lo) + a.shape[2:], a.dtype))
+    return out
+
+
+def scatter_scratch(dims, *block):
     count = dims[0] * dims[2]
     if dims[0] == 2 and dims[2] == 4:
         near, away, hops, sems = (4, 4, 6, 7)
     else:
         near, away, hops, sems = (1, count - 1, 1, count - 1)
     return [
-        pltpu.VMEM((near, rows, cols), F32),
-        pltpu.VMEM((away, rows, cols), BF),
-        pltpu.VMEM((away, rows, cols), BF),
-        pltpu.VMEM((hops, rows, cols), BF),
+        pltpu.VMEM((near,) + block, F32),
+        pltpu.VMEM((away,) + block, BF),
+        pltpu.VMEM((away,) + block, BF),
+        pltpu.VMEM((hops,) + block, BF),
         pltpu.SemaphoreType.DMA((sems,)),
         pltpu.SemaphoreType.DMA((sems,)),
     ]
@@ -315,90 +379,132 @@
     )(*args)
 
 
-def gather_weights_kernel(dims, gu, wd, qo, gu_all, wd_all, qo_all, lsem, ps, pr, zs, zr, qs, qr):
+def column_start(dims, part, b, f, y, half):
+    ns, nb, nf = dims
+    return part * nb * nf * ns * half + ((b * nf + f) * ns + y) * half
+
+
+def gather_weights_kernel(
+    dims, w_ref, wd, qo, small, gup, wdp, gu_first, qo_all, small_all,
+    pack, lsem, ps, pr, zs, zr, qs, qr, ms, mr, *rest
+):
     pc = Place(dims)
     ns, nb, nf = dims
+    half = wd.shape[1]
     greet(pc, "all", True)
+    firsts = []
+    for d in range(1, nb):
+        firsts.append(
+            remote(qo, qo_all.at[pc.s, pc.b, pc.f], zs.at[d - 1], zr.at[d - 1], pc.along(d))
+        )
+        firsts[-1].start()
     local = [
-        pltpu.make_async_copy(qo, qo_all.at[pc.s, pc.f, pc.b], lsem.at[0]),
-        pltpu.make_async_copy(gu.at[pc.s, pc.f], gu_all.at[pc.s, pc.b, pc.f], lsem.at[1]),
-        pltpu.make_async_copy(wd.at[pc.s], wd_all.at[pc.s, pc.b], lsem.at[2]),
+        pltpu.make_async_copy(qo, qo_all.at[pc.s, pc.b, pc.f], lsem.at[0]),
+        pltpu.make_async_copy(wd.at[pc.s], wdp.at[pc.s], lsem.at[1]),
+        pltpu.make_async_copy(small, small_all.at[pc.s], lsem.at[2]),
     ]
-    mine = qo_all.at[pc.s, pc.f, pc.b]
-    firsts = [remote(qo, mine, qs.at[d - 1], qr.at[d - 1], pc.along(d)) for d in range(1, nb)]
-    for c in firsts:
-        c.start()
     for c in local:
         c.start()
+    across = []
+    for d in range(1, ns):
+        y = (pc.s + d) % ns
+        t = (y, pc.b, pc.f)
+        across.append(remote(wd.at[y], wdp.at[pc.s], ms.at[2 * d - 2], mr.at[2 * d - 2], t))
+        across.append(remote(small, small_all.at[pc.s], ms.at[2 * d - 1], mr.at[2 * d - 1], t))
+    for c in across:
+        c.start()
+    for y in range(ns):
+        for f in range(nf):
+            pieces = []
+            for part in range(2):
+                for b in range(nb):
+                    c0 = column_start(dims, part, b, f, y, half)
+                    pieces.append(w_ref[0, :, c0 : c0 + half])
+            pack[y, f] = jnp.concatenate(pieces, axis=1)
+    own = pltpu.make_async_copy(pack.at[pc.s, pc.f], gup.at[pc.s, pc.f], lsem.at[3])
+    own.start()
     plane = []
     for e in range(1, pc.count):
         t = pc.plane(e)
         plane.append(
-            remote(gu.at[t[0], t[2]], gu_all.at[pc.s, pc.b, pc.f], ps.at[e - 1], pr.at[e - 1], t)
-        )
-    for d in range(1, ns):
-        y = (pc.s + d) % ns
-        k = pc.count - 1 + d - 1
-        plane.append(
-            remote(wd.at[y], wd_all.at[pc.s, pc.b], ps.at[k], pr.at[k], (y, pc.b, pc.f))
+            remote(pack.at[t[0], t[2]], gup.at[pc.s, pc.f], ps.at[e - 1], pr.at[e - 1], t)
         )
     for c in plane:
         c.start()
-    for c in local:
-        c.wait()
-    for c in firsts:
-        c.wait()
-    base = nb - 1
-    gather = PlaneGather(
-        pc,
-        lambda q: qo_all.at[q // nf, q % nf],
-        qs.at[pl.ds(base, pc.count - 1)],
-        qr.at[pl.ds(base, pc.count - 1)],
-    )
-    gather.start()
+    n = pc.count - 1
+    gathers = []
+    for d in range(nb):
+        b = (pc.b + nb - d) % nb
+        gathers.append(
+            PlaneGather(
+                pc,
+                lambda q, b=b: qo_all.at[q // nf, b, q % nf],
+                qs.at[pl.ds(d * n, n)],
+                qr.at[pl.ds(d * n, n)],
+            )
+        )
+    local[0].wait()
+    gathers[0].start()
+    own.wait()
     for c in plane:
         c.wait()
-    lines = []
-    k = 0
+    line = LineGather(pc, gup.at[0], gu_first, rest)
+    line.start()
     for d in range(1, nb):
-        for l in range(ns):
-            for ref in (gu_all, wd_all):
-                lines.append(
-                    remote(ref.at[l, pc.b], ref.at[l, pc.b], zs.at[k], zr.at[k], pc.along(d))
-                )
-                k += 1
-    for c in lines:
-        c.start()
-    for step in range(pc.count):
-        gather.before(step)
-    gather.finish()
-    for c in lines:
+        firsts[d - 1].wait()
+        gathers[d].start()
+        for step in range(1, min(6, pc.count)):
+            gathers[d - 1].before(step)
+    for step in range(1, min(6, pc.count)):
+        gathers[nb - 1].before(step)
+    for step in range(min(6, pc.count), pc.count):
+        for g in gathers:
+            g.before(step)
+    for g in gathers:
+        g.finish()
+    for c in local[1:]:
         c.wait()
-
-
-def gather_weights(dims, gu, wd, qo):
+    for c in across:
+        c.wait()
+    line.finish()
+
+
+def gather_weights(dims, w, wd, qo, small):
     ns, nb, nf = dims
     count = ns * nf
     half, width = wd.shape[1:]
+    dr = qo.shape[0]
+    two_ff = 2 * nb * half
+    sds = jax.ShapeDtypeStruct
     outs = (
-        jax.ShapeDtypeStruct((ns, nb) + gu.shape[1:], BF),
-        jax.ShapeDtypeStruct((ns, nb, half, width), BF),
-        jax.ShapeDtypeStruct((ns, nf, nb) + qo.shape, BF),
+        sds((ns, nf, dr, two_ff), BF),
+        sds((ns, half, width), BF),
+        sds((nb, nf, dr, two_ff), BF),
+        sds((ns, nb, nf) + qo.shape, BF),
+        sds((ns,) + small.shape, F32),
     )
     dma = pltpu.SemaphoreType.DMA
-    n_plane = count - 1 + ns - 1
-    n_line = (nb - 1) * ns * 2
-    n_qo = nb - 1 + count - 1
     return call(
         functools.partial(gather_weights_kernel, dims),
         "gather_weights",
         0,
         outs,
-        [AN] * 3,
-        [AN] * 3,
-        [dma((3,)), dma((n_plane,)), dma((n_plane,)), dma((n_line,)), dma((n_line,)),
-         dma((n_qo,)), dma((n_qo,))],
-        (gu, wd, qo),
+        [AN] * 5,
+        [VM, AN, AN, AN],
+        [
+            pltpu.VMEM((ns, nf, dr, two_ff), BF),
+            dma((4,)),
+            dma((count - 1,)),
+            dma((count - 1,)),
+            dma((nb - 1,)),
+            dma((nb - 1,)),
+            dma((nb * (count - 1),)),
+            dma((nb * (count - 1),)),
+            dma((2 * (ns - 1),)),
+            dma((2 * (ns - 1),)),
+        ]
+        + line_sems(dims),
+        (w, wd, qo, small),
     )
 
 
@@ -406,21 +512,84 @@
     return lax.rsqrt(jnp.mean(values * values, axis=0, keepdims=True) + 1e-06)
 
 
+def column(rows_t, first, count):
+    return jnp.concatenate([rows_t[:, k : k + 1] for k in range(first, first + count)], axis=0)
+
+
+def rows_of(values):
+    v = folded(values)
+    return jnp.concatenate(
+        [v[k : k + 128].T.sum(axis=0, keepdims=True) for k in range(0, v.shape[0], 128)], axis=0
+    )
+
+
+def folded(v):
+    out = v[:, :128]
+    for k in range(1, v.shape[1] // 128):
+        out = out + v[:, k * 128 : (k + 1) * 128]
+    return out
+
+
+def fill_masks(pc, mask, meta_t, query_docs):
+    nk, rows = mask.shape[:2]
+    key_i = lax.broadcasted_iota(jnp.int32, (rows, rows), 0)
+    query_i = lax.broadcasted_iota(jnp.int32, (rows, rows), 1)
+    per = rows // 128
+    for j in range(nk):
+        same = column(meta_t, j * per, per) == query_docs
+        if j == 0:
+            live = same & (key_i <= query_i)
+        else:
+            live = same & (key_i < (pc.b - j + 1) * rows)
+        mask[j] = jnp.where(live, 0.0, NEG)
+
+
+def load_qo(qo_all, layer, w, wo, sems):
+    cols = w.shape[1]
+    c1 = pltpu.make_async_copy(qo_all.at[layer, :, 0:cols], w, sems.at[0])
+    c2 = pltpu.make_async_copy(qo_all.at[layer, :, cols : cols + wo.shape[1]], wo, sems.at[1])
+    c1.start()
+    c2.start()
+    return (c1, c2)
+
+
+def gains_of(small_t, width, qkv):
+    n = width // 128
+    return (
+        column(small_t, 0, n),
+        column(small_t, n, n),
+        column(small_t, 2 * n, qkv // 128),
+    )
+
+
+def padded_t(v):
+    n = v.shape[0]
+    return jnp.concatenate([v, jnp.zeros((128 - n, 128), v.dtype)], axis=0).T
+
+
 def attention_forward_kernel(
-    dims, nk, h_ref, w_ref, wo_ref, bias_ref, g1_ref, g2_ref, cos_ref, sin_ref, mask_ref,
-    normed_ref, q_ref, kv_ref, lse_ref, mixed_ref, res_ref, n2_ref,
-    joined, ssem, rsem,
+    dims, nk, layer, specs, h_ref, small_ref, meta_ref, docs_ref, cos_ref, sin_ref, qo_all, *refs
 ):
+    n = len(specs)
+    ins, refs = (refs[:n], refs[n:])
+    normed_ref, q_ref, kv_ref, lse_ref, mixed_ref, res_ref, n2_ref = refs[:7]
+    outs, refs = (refs[7 : 7 + n], refs[7 + n :])
+    w, wo, mask, joined, ssem, rsem, qsem = refs[:7]
     pc = Place(dims)
     width, rows = h_ref.shape
-    hidden = h_ref[...]
-    normed = (hidden * rms(hidden) * g1_ref[...]).astype(BF)
+    loads = load_qo(qo_all, layer, w, wo, qsem)
+    greet(pc, None, True)
+    riders = riders_of(pc, specs, ins, outs, refs[7:])
+    g1, g2, bias = gains_of(padded_t(small_ref[layer]), width, w.shape[1])
+    hidden = h_ref[...].astype(BF).astype(F32)
+    normed = (hidden * rms(hidden) * g1).astype(BF)
     normed_ref[...] = normed
-    joined[...] = tn(w_ref[...], normed) + bias_ref[...]
+    fill_masks(pc, mask, padded_t(meta_ref[...]), docs_ref[...])
+    loads[0].wait()
+    joined[...] = tn(w[...], normed) + bias
     cos_part = cos_ref[...]
     sin_part = sin_ref[...]
     half = HD // 2
-    greet(pc, None, True)
 
     def turned(row):
         u1 = joined[pl.ds(row, half), :]
@@ -439,6 +608,8 @@
     ]
     for c in sends:
         c.start()
+    for r in riders:
+        r.start()
     scale = HD**-0.5
     for head in range(H):
         r1, r2 = turned(head * HD)
@@ -453,7 +624,7 @@
         def one_head(i, carry):
             head = g * GROUP + i
             q = q_ref[head]
-            s = [nn(keys[j], q) + mask_ref[j] for j in range(nk)]
+            s = [nn(keys[j], q) + mask[j] for j in range(nk)]
             top = s[0].max(axis=0, keepdims=True)
             for j in range(1, nk):
                 top = jnp.maximum(top, s[j].max(axis=0, keepdims=True))
@@ -470,15 +641,20 @@
 
         lax.fori_loop(0, GROUP, one_head, 0)
     mixed = mixed_ref[...].reshape(H * HD, rows)
-    residual = h_ref[...] + tn(wo_ref[...], mixed)
+    loads[1].wait()
+    residual = hidden + tn(wo[...], mixed)
     res_ref[...] = residual
-    n2_ref[...] = (residual * rms(residual) * g2_ref[...]).astype(BF)
-
-
-def attention_forward(dims, nk, cid, hidden, w, wo, bias, g1, g2, cos_part, sin_part, mask):
+    n2_ref[...] = (residual * rms(residual) * g2).astype(BF)
+    for r in riders:
+        r.finish()
+
+
+def attention_forward(dims, nk, cid, layer, hidden, small, meta, docs, cos_part, sin_part, qo_all,
+                      specs, riders):
     width, rows = hidden.shape
+    qkv = qo_all.shape[2] - width
     sds = jax.ShapeDtypeStruct
-    outs = (
+    outs = [
         sds((width, rows), BF),
         sds((H, HD, rows), BF),
         sds((nk, 2 * KVH, HD, rows), BF),
@@ -486,39 +662,54 @@
         sds((H, HD, rows), BF),
         sds((width, rows), F32),
         sds((width, rows), BF),
-    )
+    ] + rider_shapes(dims, specs, riders)
     dma = pltpu.SemaphoreType.DMA
-    return call(
-        functools.partial(attention_forward_kernel, dims, nk),
+    n = len(specs)
+    out = call(
+        functools.partial(attention_forward_kernel, dims, nk, layer, specs),
         "attention_forward",
         cid,
-        outs,
-        [VM] * 7,
-        [VM] * 9,
-        [pltpu.VMEM((w.shape[1], rows), F32), dma((nk - 1,)), dma((nk - 1,))],
-        (hidden, w, wo, bias, g1, g2, cos_part, sin_part, mask),
-    )
-
-
-def folded(v):
-    out = v[:, :128]
-    for k in range(1, v.shape[1] // 128):
-        out = out + v[:, k * 128 : (k + 1) * 128]
-    return out
+        tuple(outs),
+        [VM] * 7 + [AN] * n,
+        [VM] * 6 + [AN] * (1 + n),
+        [
+            pltpu.VMEM((width, qkv), BF),
+            pltpu.VMEM((width, width), BF),
+            pltpu.VMEM((nk, rows, rows), F32),
+            pltpu.VMEM((qkv, rows), F32),
+            dma((nk - 1,)),
+            dma((nk - 1,)),
+            dma((2,)),
+        ]
+        + line_sems(dims) * n,
+        (hidden, small, meta, docs, cos_part, sin_part, qo_all, *riders),
+    )
+    return (out[:7], out[7:])
 
 
 def attention_backward_kernel(
-    dims, nk, g_ref, w_ref, wo_ref, g1_ref, cos_ref, sin_ref, mask_ref,
-    h_ref, normed_ref, q_ref, kv_ref, lse_ref, mixed_ref,
-    gh_ref, dw_ref, dwo_ref, dg1_ref, db_ref,
-    dmix, dkv, out_kv, in_kv, gj, ssem, rsem,
+    dims, nk, layer, specs, g_ref, small_ref, meta_ref, docs_ref, cos_ref, sin_ref,
+    h_ref, normed_ref, q_ref, kv_ref, lse_ref, mixed_ref, qo_all, *refs
 ):
+    n = len(specs)
+    ins, refs = (refs[:n], refs[n:])
+    gh_ref, dqo_ref, dsmall_ref = refs[:3]
+    outs, refs = (refs[3 : 3 + n], refs[3 + n :])
+    w, wo, mask, dmix, dkv, out_kv, in_kv, gj, ssem, rsem, qsem = refs[:11]
     pc = Place(dims)
     width, rows = h_ref.shape
+    qkv = w.shape[1]
+    loads = load_qo(qo_all, layer, w, wo, qsem)
     greet(pc, None, True)
+    riders = riders_of(pc, specs, ins, outs, refs[11:])
+    for r in riders:
+        r.start()
+    g1 = column(padded_t(small_ref[layer]), 0, width // 128)
+    fill_masks(pc, mask, padded_t(meta_ref[...]), docs_ref[...])
     grl = g_ref[...].astype(BF)
-    dmix[...] = nn(wo_ref[...], grl).astype(BF).reshape(dmix.shape)
-    dwo_ref[...] = nt(mixed_ref[...].reshape(H * HD, rows), grl).astype(BF)
+    loads[1].wait()
+    dmix[...] = nn(wo[...], grl).astype(BF).reshape(dmix.shape)
+    dqo_ref[:, qkv:] = nt(mixed_ref[...].reshape(H * HD, rows), grl).astype(BF)
     cos_part = cos_ref[...]
     sin_part = sin_ref[...]
     half = HD // 2
@@ -538,7 +729,7 @@
             q = q_ref[head]
             do = dmix[head]
             lse = lse_ref[head]
-            p = [jnp.exp(nn(keys[j], q) + mask_ref[j] - lse) for j in range(nk)]
+            p = [jnp.exp(nn(keys[j], q) + mask[j] - lse) for j in range(nk)]
             dp = [nn(values[j], do) for j in range(nk)]
             delta = (p[0] * dp[0]).sum(axis=0, keepdims=True)
             for j in range(1, nk):
@@ -578,48 +769,59 @@
         v0 = (H + KVH + g) * HD
         gj[v0 : v0 + HD, :] = own[KVH + g].astype(BF)
     gjv = gj[...]
-    db_ref[...] = folded(gjv.astype(F32))
-    dw_ref[...] = nt(normed_ref[...], gjv).astype(BF)
-    gn = nn(w_ref[...], gjv)
-    hidden = h_ref[...]
+    n1 = width // 128
+    dsmall_ref[n1 : n1 + qkv // 128, :] = rows_of(gjv.astype(F32))
+    loads[0].wait()
+    dqo_ref[:, :qkv] = nt(normed_ref[...], gjv).astype(BF)
+    gn = nn(w[...], gjv)
+    hidden = h_ref[...].astype(BF).astype(F32)
     scale_one = rms(hidden)
     unit = hidden * scale_one
-    dg1_ref[...] = folded(gn * unit)
-    u = gn * g1_ref[...]
+    dsmall_ref[:n1, :] = rows_of(gn * unit)
+    u = gn * g1
     gh_ref[...] = g_ref[...] + scale_one * (u - unit * jnp.mean(u * unit, axis=0, keepdims=True))
-
-
-def attention_backward(dims, nk, cid, g, w, wo, g1, cos_part, sin_part, mask, hidden, normed, q,
-                       kv, lse, mixed):
+    for r in riders:
+        r.finish()
+
+
+def attention_backward(dims, nk, cid, layer, g, small, meta, docs, cos_part, sin_part, hidden,
+                       normed, q, kv, lse, mixed, qo_all, specs, riders):
     width, rows = hidden.shape
+    qkv = qo_all.shape[2] - width
     sds = jax.ShapeDtypeStruct
-    outs = (
+    outs = [
         sds((width, rows), F32),
-        sds(w.shape, BF),
-        sds(wo.shape, BF),
-        sds((width, 128), F32),
-        sds((w.shape[1], 128), F32),
-    )
+        sds((width, qkv + width), BF),
+        sds(((width + qkv) // 128, 128), F32),
+    ] + rider_shapes(dims, specs, riders)
     dma = pltpu.SemaphoreType.DMA
     block = (2 * KVH, HD, rows)
-    return call(
-        functools.partial(attention_backward_kernel, dims, nk),
+    n = len(specs)
+    out = call(
+        functools.partial(attention_backward_kernel, dims, nk, layer, specs),
         "attention_backward",
         cid,
-        outs,
-        [VM] * 5,
-        [VM] * 13,
+        tuple(outs),
+        [VM] * 3 + [AN] * n,
+        [VM] * 12 + [AN] * (1 + n),
         [
+            pltpu.VMEM((width, qkv), BF),
+            pltpu.VMEM((width, width), BF),
+            pltpu.VMEM((nk, rows, rows), F32),
             pltpu.VMEM((H, HD, rows), BF),
             pltpu.VMEM((nk,) + block, F32),
             pltpu.VMEM((nk - 1,) + block, BF),
             pltpu.VMEM((nk - 1,) + block, BF),
-            pltpu.VMEM((w.shape[1], rows), BF),
+            pltpu.VMEM((qkv, rows), BF),
             dma((nk - 1,)),
             dma((nk - 1,)),
-        ],
-        (g, w, wo, g1, cos_part, sin_part, mask, hidden, normed, q, kv, lse, mixed),
-    )
+            dma((2,)),
+        ]
+        + line_sems(dims) * n,
+        (g, small, meta, docs, cos_part, sin_part, hidden, normed, q, kv, lse, mixed, qo_all,
+         *riders),
+    )
+    return (out[:3], out[3:])
 
 
 def steps_of(count):
@@ -637,19 +839,23 @@
         dst[c0:c1, :] = src[:, c0:c1].T
 
 
-def feed_forward_kernel(
-    dims, x_ref, res_ref, wgu_ref, wd_ref,
-    out_ref, x_all, gu_all,
-    wgu_t, wd_t, gu, inner, near, away, back, hop, ss, sr, gs, gr,
-):
+def feed_forward_kernel(dims, specs, x_ref, res_ref, wgu_ref, wd_ref, *refs):
+    n = len(specs)
+    ins, refs = (refs[:n], refs[n:])
+    out_ref, x_all, gu_all = refs[:3]
+    outs, refs = (refs[3 : 3 + n], refs[3 + n :])
+    wgu_t, wd_t, gu, inner, near, away, back, hop, ss, sr, gs, gr = refs[:12]
     pc = Place(dims)
     width, rows = x_ref.shape
     ff = wd_ref.shape[0]
-    greet(pc, "mates", False)
+    greet(pc, "mates", n > 0)
+    riders = riders_of(pc, specs, ins, outs, refs[12:])
     gather = PlaneGather(pc, lambda q: x_all.at[:, lanes(q, rows)], gs, gr)
     scatter = PlaneScatter(pc, near, away, back, hop, ss, sr)
     x_all[:, lanes(pc.me, rows)] = x_ref[...]
     gather.start()
+    for r in riders:
+        r.start()
     transpose_into(wgu_t, wgu_ref)
     transpose_into(wd_t, wd_ref)
     neighbours, last = steps_of(pc.count)
@@ -691,25 +897,29 @@
 
     scatter.result(store)
     gather.finish()
-
-
-def feed_forward(dims, cid, x, residual, wgu, wd):
+    for r in riders:
+        r.finish()
+
+
+def feed_forward(dims, cid, x, residual, wgu, wd, specs, riders):
     width, rows = x.shape
     count = dims[0] * dims[2]
     two_ff, ff = (wgu.shape[1], wd.shape[0])
     sds = jax.ShapeDtypeStruct
     dma = pltpu.SemaphoreType.DMA
-    return call(
-        functools.partial(feed_forward_kernel, dims),
+    n = len(specs)
+    out = call(
+        functools.partial(feed_forward_kernel, dims, specs),
         "feed_forward",
         cid,
         (
             sds((width, rows), F32),
             sds((width, count * rows), BF),
             sds((two_ff, count * rows), BF),
+            *rider_shapes(dims, specs, riders),
         ),
-        [VM] * 3,
-        [VM] * 4,
+        [VM] * 3 + [AN] * n,
+        [VM] * 4 + [AN] * n,
         [
             pltpu.VMEM((two_ff, width), BF),
             pltpu.VMEM((width, ff), BF),
@@ -717,24 +927,32 @@
             pltpu.VMEM((ff, rows), BF),
         ]
         + scatter_scratch(dims, width, rows)
-        + [dma((count - 1,)), dma((count - 1,))],
-        (x, residual, wgu, wd),
-    )
+        + [dma((count - 1,)), dma((count - 1,))]
+        + line_sems(dims) * n,
+        (x, residual, wgu, wd, *riders),
+    )
+    return (out[:3], out[3:])
 
 
 def feed_backward_kernel(
-    dims, g_ref, res_ref, x_all, gu_all, wgu_ref, wd_ref, g2_ref,
-    gr_ref, dwgu_ref, dwd_ref, dg2_ref,
-    g_all, inner, ggu, gi, near, away, back, hop, ss, sr, gs, gr,
+    dims, layer, specs, g_ref, res_ref, x_all, gu_all, wgu_ref, wd_ref, small_ref, *refs
 ):
+    n = len(specs)
+    ins, refs = (refs[:n], refs[n:])
+    gr_ref, dwgu_ref, dwd_ref, dsmall_ref = refs[:4]
+    outs, refs = (refs[4 : 4 + n], refs[4 + n :])
+    g_all, inner, ggu, gi, near, away, back, hop, ss, sr, gs, gr = refs[:12]
     pc = Place(dims)
     width, rows = g_ref.shape
     ff = wd_ref.shape[0]
-    greet(pc, "mates", False)
+    greet(pc, "mates", n > 0)
+    riders = riders_of(pc, specs, ins, outs, refs[12:])
     gather = PlaneGather(pc, lambda q: g_all.at[:, lanes(q, rows)], gs, gr)
     scatter = PlaneScatter(pc, near, away, back, hop, ss, sr)
     g_all[:, lanes(pc.me, rows)] = g_ref[...].astype(BF)
     gather.start()
+    for r in riders:
+        r.start()
     neighbours, last = steps_of(pc.count)
     chunk = 32 if ff % 32 == 0 else 16
 
@@ -782,34 +1000,39 @@
         residual = res_ref[...]
         scale_two = rms(residual)
         unit = residual * scale_two
-        dg2_ref[...] = folded(total * unit)
-        u = total * g2_ref[...]
-        gr_ref[...] = g_ref[...] + scale_two * (
+        n1 = width // 128
+        dsmall_ref[...] = rows_of(total * unit)
+        u = total * column(padded_t(small_ref[layer]), n1, n1)
+        gr_ref[...] = g_ref[...].astype(BF).astype(F32) + scale_two * (
             u - unit * jnp.mean(u * unit, axis=0, keepdims=True)
         )
 
     scatter.result(store)
     gather.finish()
-
-
-def feed_backward(dims, cid, g, residual, x_all, gu_all, wgu, wd, g2):
+    for r in riders:
+        r.finish()
+
+
+def feed_backward(dims, cid, layer, g, residual, x_all, gu_all, wgu, wd, small, specs, riders):
     width, rows = g.shape
     count = dims[0] * dims[2]
     two_ff, ff = (wgu.shape[1], wd.shape[0])
     sds = jax.ShapeDtypeStruct
     dma = pltpu.SemaphoreType.DMA
-    return call(
-        functools.partial(feed_backward_kernel, dims),
+    n = len(specs)
+    out = call(
+        functools.partial(feed_backward_kernel, dims, layer, specs),
         "feed_backward",
         cid,
         (
             sds((width, rows), F32),
             sds(wgu.shape, BF),
             sds(wd.shape, BF),
-            sds((width, 128), F32),
+            sds((width // 128, 128), F32),
+            *rider_shapes(dims, specs, riders),
         ),
-        [VM] * 4,
-        [VM] * 7,
+        [VM] * 4 + [AN] * n,
+        [VM] * 7 + [AN] * n,
         [
             pltpu.VMEM((width, count * rows), BF),
             pltpu.VMEM((ff, count * rows), BF),
@@ -817,93 +1040,42 @@
             pltpu.VMEM((ff, rows), F32),
         ]
         + scatter_scratch(dims, width, rows)
-        + [dma((count - 1,)), dma((count - 1,))],
-        (g, residual, x_all, gu_all, wgu, wd, g2),
-    )
-
-
-def line_exchange_kernel(dims, count, *refs):
-    pc = Place(dims)
-    ins, outs, (lsem, ss, sr) = (refs[:count], refs[count : 2 * count], refs[2 * count :])
-    greet(pc, None, True)
-    copies = []
-    k = 0
-    for i in range(count):
-        copies.append(
-            pltpu.make_async_copy(ins[i].at[pc.b], outs[i].at[pc.b], lsem.at[i])
-        )
-        for d in range(1, pc.nb):
-            t = pc.along(d)
-            copies.append(remote(ins[i].at[t[1]], outs[i].at[pc.b], ss.at[k], sr.at[k], t))
-            k += 1
-    for c in copies:
-        c.start()
-    for c in copies:
-        c.wait()
-
-
-def line_exchange(dims, cid, arrays):
-    n = len(arrays)
-    dma = pltpu.SemaphoreType.DMA
-    total = n * (dims[1] - 1)
-    return call(
-        functools.partial(line_exchange_kernel, dims, n),
-        "line_exchange",
-        cid,
-        tuple(jax.ShapeDtypeStruct(a.shape, a.dtype) for a in arrays),
-        [AN] * n,
-        [AN] * n,
-        [dma((n,)), dma((total,)), dma((total,))],
-        tuple(arrays),
-    )
-
-
-def plane_exchange_kernel(dims, gu, wd, gu_out, wd_out, lsem, ss, sr):
-    pc = Place(dims)
-    greet(pc, "all", False)
-    copies = [
-        pltpu.make_async_copy(gu.at[pc.me], gu_out.at[pc.me], lsem.at[0]),
-        pltpu.make_async_copy(wd.at[pc.s], wd_out.at[pc.s], lsem.at[1]),
-    ]
-    for e in range(1, pc.count):
-        t = pc.plane(e)
-        copies.append(
-            remote(gu.at[t[0] * pc.nf + t[2]], gu_out.at[pc.me], ss.at[e - 1], sr.at[e - 1], t)
-        )
-    for d in range(1, pc.ns):
-        k = pc.count - 1 + d - 1
-        y = (pc.s + d) % pc.ns
-        copies.append(remote(wd.at[y], wd_out.at[pc.s], ss.at[k], sr.at[k], (y, pc.b, pc.f)))
-    for c in copies:
-        c.start()
-    for c in copies:
-        c.wait()
-
-
-def plane_exchange(dims, cid, gu, wd):
-    dma = pltpu.SemaphoreType.DMA
-    total = dims[0] * dims[2] - 1 + dims[0] - 1
-    return call(
-        functools.partial(plane_exchange_kernel, dims),
-        "plane_exchange",
-        cid,
-        tuple(jax.ShapeDtypeStruct(a.shape, a.dtype) for a in (gu, wd)),
-        [AN] * 2,
-        [AN] * 2,
-        [dma((2,)), dma((total,)), dma((total,))],
-        (gu, wd),
-    )
-
-
-def small_reduce_kernel(
-    dims, qo_ref, small_ref, qo_out, small_out,
-    half_sum, z_out, z_in, sm_in, sm_mid, sm_line, near, away, back, hop, ss, sr, ps, pr, zs, zr, ws, wr,
+        + [dma((count - 1,)), dma((count - 1,))]
+        + line_sems(dims) * n,
+        (g, residual, x_all, gu_all, wgu, wd, small, *riders),
+    )
+    return (out[:4], out[4:])
+
+
+def reduce_kernel(
+    dims, cut, qo0, qo1, sa0, sa1, sb0, sb1, gu1, wd1, wd0, gu0a, gu0,
+    qo_out, small_out, gu_got, wd_got,
+    buf1, bufa, buf0, bufw, gsum, wsum, small, sm_in, sm_mid, sm_line, z_out, z_in, half_sum,
+    lsem, ps, pr, gs, gr, ws, wr, ls, lr, zs, zr, near, away, back, hop, ss, sr, *rest
 ):
     pc = Place(dims)
     ns, nb, nf = dims
     greet(pc, "all", True)
+    line = LineExchange(pc, lambda t: gu0.at[t, cut:nf], lambda t: buf0.at[t], rest)
+    line.start()
+    loads = [
+        pltpu.make_async_copy(gu1, buf1, lsem.at[0]),
+        pltpu.make_async_copy(gu0a, bufa, lsem.at[1]),
+        pltpu.make_async_copy(wd0, bufw.at[0], lsem.at[2]),
+        pltpu.make_async_copy(wd1, bufw.at[1], lsem.at[3]),
+    ]
+    for c in loads:
+        c.start()
+    n1 = sb0.shape[0]
+    per = small.shape[0] // ns
+    nr = sa0.shape[0] + n1
+    small[...] = jnp.zeros_like(small)
+    for l, (a, g) in enumerate(((sa0, sb0), (sa1, sb1))):
+        small[l * per : l * per + n1] = a[0:n1]
+        small[l * per + n1 : l * per + 2 * n1] = g[...]
+        small[l * per + 2 * n1 : l * per + nr] = a[n1 : a.shape[0]]
     smalls = [
-        remote(small_ref, sm_in.at[e - 1], ps.at[e - 1], pr.at[e - 1], pc.plane(e))
+        remote(small, sm_in.at[e - 1], ls.at[e - 1], lr.at[e - 1], pc.plane(e))
         for e in range(1, pc.count)
     ]
     for c in smalls:
@@ -917,7 +1089,11 @@
 
     def step_body(step, carry):
         slot = pick(step, order)
-        scatter.put(step, qo_ref[slot].astype(F32))
+        f = slot % nf
+        for l, ref in enumerate((qo0, qo1)):
+            @pl.when(slot // nf == l)
+            def _():
+                scatter.put(step, ref[:, f].astype(F32))
 
         @pl.when(step == neighbours)
         def _():
@@ -927,13 +1103,55 @@
 
     lax.fori_loop(0, pc.count, step_body, 0)
     scatter.diagonal()
-    total = small_ref[...]
+
+    def send_rows(l, f):
+        e = (l * nf + f - pc.me + pc.count) % pc.count
+
+        @pl.when(e != 0)
+        def _():
+            remote(
+                gsum.at[l, f], gu_got.at[pc.me], ps.at[e - 1], pr.at[e - 1], (l, pc.b, f)
+            ).start()
+
+        @pl.when(e == 0)
+        def _():
+            pltpu.make_async_copy(gsum.at[l, f], gu_got.at[pc.me], lsem.at[4]).start()
+
+    def total_of(buf):
+        total = buf[0].astype(F32)
+        for t in range(1, nb):
+            total = total + buf[t].astype(F32)
+        return total.astype(BF)
+
+    loads[0].wait()
+    for f in range(nf):
+        gsum[1, f] = total_of(buf1.at[:, f])
+        send_rows(1, f)
+    loads[2].wait()
+    loads[3].wait()
+    wsum[0] = total_of(bufw.at[0])
+    wsum[1] = total_of(bufw.at[1])
+    own = pltpu.make_async_copy(wsum.at[pc.s], wd_got.at[pc.s], lsem.at[5])
+    own.start()
+    across = []
+    for d in range(1, ns):
+        y = (pc.s + d) % ns
+        across.append(
+            remote(wsum.at[y], wd_got.at[pc.s], ws.at[d - 1], wr.at[d - 1], (y, pc.b, pc.f))
+        )
+        across[-1].start()
+    loads[1].wait()
+    for f in range(cut):
+        gsum[0, f] = total_of(bufa.at[:, f])
+        send_rows(0, f)
+    total = small[...]
     for e, c in enumerate(smalls):
         c.wait()
         total = total + sm_in[e]
     sm_mid[...] = total
+    m = nb - 1
     lines = [
-        remote(sm_mid, sm_line.at[d - 1], ws.at[d - 1], wr.at[d - 1], pc.along(d))
+        remote(sm_mid, sm_line.at[d - 1], zs.at[m + d - 1], zr.at[m + d - 1], pc.along(d))
         for d in range(1, nb)
     ]
     for c in lines:
@@ -943,16 +1161,17 @@
         half_sum[...] = value
 
     scatter.result(store)
-    part = half_sum.shape[0] // nb
-    z_out[...] = half_sum[...].astype(BF).reshape(z_out.shape)
+    z_out[...] = half_sum[...].astype(BF)
     sends = []
     for d in range(1, nb):
         t = pc.along(d)
-        sends.append(
-            remote(z_out.at[t[1]], z_in.at[d - 1], zs.at[d - 1], zr.at[d - 1], t)
-        )
+        sends.append(remote(z_out.at[t[1]], z_in.at[d - 1], zs.at[d - 1], zr.at[d - 1], t))
     for c in sends:
         c.start()
+    line.finish()
+    for f in range(cut, nf):
+        gsum[0, f] = total_of(buf0.at[:, f - cut])
+        send_rows(0, f)
     mine = z_out[pc.b].astype(F32)
     for d, c in enumerate(sends):
         c.wait()
@@ -963,34 +1182,133 @@
         c.wait()
         total = total + sm_line[d]
     small_out[...] = total
-
-
-def small_reduce(dims, cid, qo, small, dr):
+    for k in range(pc.count - 1):
+        c = remote(gsum.at[0, 0], gu_got.at[pc.me], ps.at[k], pr.at[k], pc.plane(1))
+        c.wait()
+    pltpu.make_async_copy(gsum.at[0, 0], gu_got.at[pc.me], lsem.at[4]).wait()
+    own.wait()
+    for c in across:
+        c.wait()
+
+
+def reduce_gradients(dims, cid, cut, qo0, qo1, smalls, gu1, wd1, wd0, gu0a, gu0):
     ns, nb, nf = dims
     count = ns * nf
-    cols = qo.shape[2]
+    dr, cols = qo0.shape[2:]
+    two_ff = gu0.shape[3]
+    half, width = wd0.shape[1:]
+    rows = smalls[0].shape[0] + smalls[2].shape[0]
+    small = (ns * (-(-rows // 8) * 8), 128)
     sds = jax.ShapeDtypeStruct
     dma = pltpu.SemaphoreType.DMA
     return call(
-        functools.partial(small_reduce_kernel, dims),
-        "small_reduce",
+        functools.partial(reduce_kernel, dims, cut),
+        "reduce_gradients",
         cid,
-        (sds((dr, cols), F32), sds(small.shape, F32)),
-        [VM] * 2,
-        [VM] * 2,
+        (
+            sds((dr, cols), F32),
+            sds(small, F32),
+            sds((count, dr, two_ff), BF),
+            sds((ns, half, width), BF),
+        ),
+        [VM] * 4,
+        [VM] * 6 + [AN] * 5,
         [
-            pltpu.VMEM((nb * dr, cols), F32),
+            pltpu.VMEM((nb, nf, dr, two_ff), BF),
+            pltpu.VMEM((nb, cut, dr, two_ff), BF),
+            pltpu.VMEM((nb, nf - cut, dr, two_ff), BF),
+            pltpu.VMEM((ns, nb, half, width), BF),
+            pltpu.VMEM((ns, nf, dr, two_ff), BF),
+            pltpu.VMEM((ns, half, width), BF),
+            pltpu.VMEM(small, F32),
+            pltpu.VMEM((count - 1,) + small, F32),
+            pltpu.VMEM(small, F32),
+            pltpu.VMEM((nb - 1,) + small, F32),
             pltpu.VMEM((nb, dr, cols), BF),
             pltpu.VMEM((nb - 1, dr, cols), BF),
-            pltpu.VMEM((count - 1,) + small.shape, F32),
-            pltpu.VMEM(small.shape, F32),
-            pltpu.VMEM((nb - 1,) + small.shape, F32),
+            pltpu.VMEM((nb, dr, cols), F32),
+            dma((6,)),
+            dma((count - 1,)),
+            dma((count - 1,)),
+            dma((1,)),
+            dma((1,)),
+            dma((ns - 1,)),
+            dma((ns - 1,)),
+            dma((count - 1,)),
+            dma((count - 1,)),
+            dma((2 * (nb - 1),)),
+            dma((2 * (nb - 1),)),
         ]
-        + scatter_scratch(dims, nb * dr, cols)
-        + [dma((count - 1,)), dma((count - 1,))]
-        + [dma((nb - 1,))] * 4,
-        (qo, small),
-    )
+        + scatter_scratch(dims, nb, dr, cols)
+        + line_sems(dims),
+        (qo0, qo1, *smalls, gu1, wd1, wd0, gu0a, gu0),
+    )
+
+
+def lay_out_kernel(
+    dims, gu, wd, qo, small, out0, out1, gh0, gh1, take_out, take_grad,
+    block_out, input_grad, g1, wqkv, bqkv, wout, g2, wgu, wdn
+):
+    ns, nb, nf = dims
+    half = wd.shape[1]
+    s = lax.axis_index("section")
+    qkv = wqkv.shape[2]
+    width = wout.shape[2]
+    wqkv[0] = qo[:, :qkv]
+    wout[0] = qo[:, qkv:]
+    for y in range(ns):
+        wdn[0, y * half : (y + 1) * half, :] = wd[y].astype(F32)
+        for f in range(nf):
+            got = gu[y * nf + f].astype(F32)
+            for part in range(2):
+                for b in range(nb):
+                    c0 = column_start(dims, part, b, f, y, half)
+                    k0 = (part * nb + b) * half
+                    wgu[0, :, c0 : c0 + half] = got[:, k0 : k0 + half]
+    n1 = width // 128
+    per = small.shape[0] // ns
+    rows = small[pl.ds(pl.multiple_of(s * per, 8), per), :]
+    for k in range(n1):
+        g1[0:1, k * 128 : (k + 1) * 128] = rows[k : k + 1]
+        g2[0:1, k * 128 : (k + 1) * 128] = rows[n1 + k : n1 + k + 1]
+    for k in range(qkv // 128):
+        bqkv[0:1, k * 128 : (k + 1) * 128] = rows[2 * n1 + k : 2 * n1 + k + 1]
+    for out, pair, take in (
+        (block_out, (out0, out1), take_out),
+        (input_grad, (gh0, gh1), take_grad),
+    ):
+        for l in range(ns):
+            @pl.when(s == l)
+            def _():
+                out[0, l] = pair[l][...].T
+                out[0, 1 - l] = take[...].T.astype(F32)
+
+
+def lay_out(dims, qkv, args):
+    ns, nb, nf = dims
+    gu, wd, qo = args[:3]
+    width, rows = args[4].shape
+    dr = qo.shape[0]
+    sds = jax.ShapeDtypeStruct
+    tokens = sds((1, ns, rows, width), F32)
+    return pl.pallas_call(
+        functools.partial(lay_out_kernel, dims),
+        name="lay_out",
+        out_shape=(
+            tokens,
+            tokens,
+            sds((1, width), F32),
+            sds((1, dr, qkv), F32),
+            sds((1, qkv), F32),
+            sds((1, dr, width), F32),
+            sds((1, width), F32),
+            sds((1, dr, gu.shape[0] * gu.shape[2]), F32),
+            sds((1, ns * wd.shape[1], width), F32),
+        ),
+        in_specs=[VM] * len(args),
+        out_specs=[VM] * 9,
+        compiler_params=pltpu.CompilerParams(vmem_limit_bytes=VMEM_LIMIT),
+    )(*args)
 
 
 def shards(
@@ -1009,7 +1327,6 @@
 ):
     ns, nb, nf = dims
     seqs, rows, width = tokens_in.shape
-    length = doc_ids.shape[1]
     s = lax.axis_index("section")
     b = lax.axis_index("blk")
     dr = w_qkv.shape[1]
@@ -1019,114 +1336,73 @@
     ff = nb * half
     nk = min(nb, 1 + (LONGEST - 1 + rows - 1) // rows)
 
-    gu = w_gate_up[0].reshape(dr, 2, nb, nf, ns, half).transpose(4, 3, 0, 1, 2, 5)
-    gu = gu.reshape(ns, nf, dr, 2 * ff)
-    wd = w_down[0].reshape(ns, half, width)
-    qo = jnp.concatenate([w_qkv[0], w_out[0]], axis=1)
-    gu_all, wd_all, qo_all = gather_weights(dims, gu, wd, qo)
-    wgu = gu_all.reshape(ns, width, 2 * ff)
-    wdn = wd_all.reshape(ns, ff, width)
-    qo_all = qo_all.transpose(0, 2, 1, 3, 4).reshape(ns, width, qkv + width)
-    wq = qo_all[:, :, :qkv]
-    wo = qo_all[:, :, qkv:]
-
-    small_in = jnp.concatenate([norm1_gain[0], norm2_gain[0], b_qkv[0]])
-    small_all = lax.all_gather(small_in, "section", axis=0, tiled=False)
-    g1 = small_all[:, :width, None]
-    g2 = small_all[:, width : 2 * width, None]
-    bias = small_all[:, 2 * width :, None]
-
     tokens = lax.dynamic_index_in_dim(tokens_in, s, 0, keepdims=False)
     cot = lax.dynamic_index_in_dim(out_grad, s, 0, keepdims=False)
     pos = lax.dynamic_index_in_dim(positions, s, 0, keepdims=False)
-    docs = lax.dynamic_index_in_dim(doc_ids, s, 0, keepdims=False)
+    docs = lax.dynamic_index_in_dim(doc_ids, s, 0, keepdims=False).astype(F32)
     freq = jnp.exp(jnp.arange(HD // 2, dtype=F32) * (-2.0 / HD) * math.log(1000000.0))
     phase = freq[:, None] * pos.astype(F32)[None, :]
     cos_part, sin_part = (jnp.cos(phase), jnp.sin(phase))
-    query_rows = b * rows + jnp.arange(rows, dtype=jnp.int32)
-    query_docs = lax.dynamic_slice_in_dim(docs, b * rows, rows)
-    masks = []
-    for j in range(nk):
-        key_rows = (b - j) * rows + jnp.arange(rows, dtype=jnp.int32)
-        start = lax.rem(b - j + nb, nb) * rows
-        key_docs = lax.dynamic_slice_in_dim(docs, start, rows)
-        live = (
-            (key_rows[:, None] >= 0)
-            & (key_rows[:, None] <= query_rows[None, :])
-            & (key_docs[:, None] == query_docs[None, :])
-        )
-        masks.append(jnp.where(live, 0.0, NEG).astype(F32))
-    mask = jnp.stack(masks)
-
+    docs = docs.reshape(nb, rows)
+    picked = (b - jnp.arange(nk) + nb) % nb
+    meta = jnp.take(docs, picked, axis=0).reshape(nk * rows // 128, 128)
+    query_docs = lax.dynamic_slice_in_dim(docs, b, 1)
     hidden = tokens.T.astype(F32)
-    saved = []
-    outputs = []
-    for l in range(ns):
-        normed, q, kv, lse, mixed, residual, n2 = attention_forward(
-            dims, nk, 1 + l, hidden, wq[l], wo[l], bias[l], g1[l], g2[l], cos_part, sin_part, mask
-        )
-        out, x_all, gu_saved = feed_forward(dims, 3 + l, n2, residual, wgu[l], wdn[l])
-        saved.append((hidden, normed, q, kv, lse, mixed, residual, x_all, gu_saved))
-        outputs.append(out)
-        hidden = out.astype(BF).astype(F32)
     g = cot.T.astype(F32)
-    grads = [None] * ns
-    line_in = []
-    qo_terms = [None] * ns
-    small_terms = [None] * ns
-    for l in reversed(range(ns)):
-        hidden, normed, q, kv, lse, mixed, residual, x_all, gu_saved = saved[l]
-        gres, dwgu, dwd, dg2 = feed_backward(
-            dims, 5 + l, g, residual, x_all, gu_saved, wgu[l], wdn[l], g2[l]
-        )
-        gh, dwq, dwo, dg1, db = attention_backward(
-            dims, nk, 7 + l, gres, wq[l], wo[l], g1[l], cos_part, sin_part, mask, hidden, normed, q,
-            kv, lse, mixed,
-        )
-        grads[l] = gh
-        g = gh.astype(BF).astype(F32)
-        line_in.append((dwgu.reshape(nb, nf * dr, 2 * ff), dwd.reshape(nb, half, width)))
-        qo_terms[l] = jnp.concatenate([dwq, dwo], axis=1)
-        small_terms[l] = jnp.concatenate([dg1.sum(1), dg2.sum(1), db.sum(1)])
-    line_in.reverse()
-
-    got = line_exchange(dims, 9, [a for pair in line_in for a in pair])
-    summed = [a.astype(F32).sum(0) for a in got]
-    gu_send = jnp.stack([summed[2 * l].reshape(nf, dr, 2 * ff) for l in range(ns)]).astype(BF)
-    wd_send = jnp.stack([summed[2 * l + 1] for l in range(ns)]).astype(BF)
-    gu_got, wd_got = plane_exchange(dims, 10, gu_send.reshape(ns * nf, dr, 2 * ff), wd_send)
-    grad_gu = gu_got.reshape(ns, nf, dr, 2, nb, half).transpose(2, 3, 4, 1, 0, 5)
-    grad_gu = grad_gu.reshape(dr, w_gate_up.shape[2]).astype(F32)
-    grad_wd = wd_got.reshape(fr, width).astype(F32)
-    qo_send = jnp.stack(qo_terms).reshape(ns, nb, nf, dr, qkv + width)
-    qo_send = qo_send.transpose(0, 2, 1, 3, 4).reshape(ns * nf, nb * dr, qkv + width)
-    small = jnp.stack(small_terms)
-    small_size = small.shape[1]
-    padded = -(-small_size // 1024) * 1024
-    small = jnp.pad(small, ((0, 0), (0, padded - small_size))).reshape(-1, 128)
-    grad_qo, small_sum = small_reduce(dims, 11, qo_send, small, dr)
-    small_sum = small_sum.reshape(ns, padded)
-    mine = lax.dynamic_index_in_dim(small_sum, s, 0, keepdims=False)
-
-    def both(values):
-        own = jnp.stack(values)
-        keep = lax.dynamic_index_in_dim(own, s, 0, keepdims=False)
-        give = lax.dynamic_index_in_dim(own, 1 - s, 0, keepdims=False)
-        take = lax.ppermute(give.astype(BF), "section", [(0, 1), (1, 0)]).astype(F32)
-        first = jnp.where(s == 0, keep, take).T
-        second = jnp.where(s == 0, take, keep).T
-        return jnp.stack([first, second])[None]
-
-    return (
-        both(outputs),
-        both(grads),
-        mine[None, :width],
-        grad_qo[None, :, :qkv],
-        mine[None, 2 * width : 2 * width + qkv],
-        grad_qo[None, :, qkv:],
-        mine[None, width : 2 * width],
-        grad_gu[None],
-        grad_wd[None],
+
+    wd = w_down[0].reshape(ns, half, width)
+    qo = jnp.concatenate([w_qkv[0], w_out[0]], axis=1)
+    small = jnp.concatenate([norm1_gain[0], norm2_gain[0], b_qkv[0]])
+    total = -(-small.shape[0] // 1024) * 1024
+    small = jnp.pad(small, (0, total - small.shape[0])).reshape(-1, 128)
+    gup, wdp, gu_first, qo_all, small_all = gather_weights(dims, w_gate_up, wd, qo, small)
+    qo_all = qo_all.reshape(ns, width, qkv + width)
+    wide = (width, 2 * ff)
+
+    common = (small_all, meta, query_docs, cos_part, sin_part, qo_all)
+    a0, (wd0,) = attention_forward(dims, nk, 1, 0, hidden, *common, (("gather", 0),), (wdp,))
+    wd0 = wd0.reshape(ff, width)
+    wgu0 = gu_first.reshape(wide)
+    f0, (gu1,) = feed_forward(dims, 3, a0[6], a0[5], wgu0, wd0, (("gather", 1),), (gup,))
+    wgu1 = gu1.reshape(wide)
+    a1, (wd1,) = attention_forward(dims, nk, 2, 1, f0[0], *common, (("gather", 1),), (wdp,))
+    wd1 = wd1.reshape(ff, width)
+    f1, _ = feed_forward(dims, 4, a1[6], a1[5], wgu1, wd1, (), ())
+
+    line_gu = (nb, nf, dr, 2 * ff)
+    line_wd = (nb, half, width)
+    everything = (0, half)
+    cut = max(1, nf // 4)
+    b1, _ = feed_backward(dims, 5, 1, g, a1[5], f1[1], f1[2], wgu1, wd1, small_all, (), ())
+    ab1, (dwd1,) = attention_backward(
+        dims, nk, 7, 1, b1[0], *common[:5], f0[0], *a1[:5], qo_all,
+        (("exchange", everything),), (b1[2].reshape(line_wd),),
+    )
+    b0, (dgu1,) = feed_backward(
+        dims, 6, 0, ab1[0], a0[5], f0[1], f0[2], wgu0, wd0, small_all,
+        (("exchange", (0, nf)),), (b1[1].reshape(line_gu),),
+    )
+    dgu0 = b0[1].reshape(line_gu)
+    ab0, (dwd0, dgu0a) = attention_backward(
+        dims, nk, 8, 0, b0[0], *common[:5], hidden, *a0[:5], qo_all,
+        (("exchange", everything), ("exchange", (0, cut))), (b0[2].reshape(line_wd), dgu0),
+    )
+
+    def swapped(values):
+        give = jnp.where(s == 0, values[1], values[0]).astype(BF)
+        return lax.ppermute(give, "section", [(0, 1), (1, 0)])
+
+    take_out = swapped((f0[0], f1[0]))
+    take_grad = swapped((ab0[0], ab1[0]))
+    line_qo = (nb, nf, dr, qkv + width)
+    grad_qo, small_sum, gu_got, wd_got = reduce_gradients(
+        dims, 9, cut, ab0[1].reshape(line_qo), ab1[1].reshape(line_qo),
+        (ab0[2], ab1[2], b0[3], b1[3]), dgu1, dwd1, dwd0, dgu0a, dgu0,
+    )
+    return lay_out(
+        dims,
+        qkv,
+        (gu_got, wd_got, grad_qo, small_sum, f0[0], f1[0], ab0[0], ab1[0], take_out, take_grad),
     )
 
 

time: 863 us -> 585 us (0.68)
  the two profiles are of different devices: /device:TPU:0 before, /device:TPU:12 now
where the time goes in v2:
time: 585 us; the launch traced here: 582 us
  Pallas kernels  565 us (97%)
  other arithmetic  9.8 us (2%)
    pallas_call x10, Pallas kernels, call(): pl.pallas_call(kernel, name=name, out_shape=outs, in_specs=in_specs, out_...  558 us
  transfers between devices with their start and end apart: 2, of which 0 were waited for; matrix products, arithmetic and copies ran while one was open for 0% of the time, Pallas kernels for 50%

profile of v2, /device:TPU:12, one launch (start us, length us, event | category | flops | bytes accessed | tf_op | source)
XLA Modules:
  0.0 581.6 jit_solution(2196184965195345640)
XLA Ops:
  0.8 0.1 broadcast_in_dim.17
  0.9 0.8 fusion.1
  1.7 0.7 convert_reduce_fusion
  2.4 0.6 gather_fusion
  3.0 0.6 constant_dynamic-slice_fusion.1.docs_ref
  3.6 0.7 reduce
  4.3 0.7 reduce.1
  5.0 0.7 reduce.2
  5.7 0.2 copy.23
  5.9 1.0 convert_bitcast_fusion.h_ref
  6.9 0.7 broadcast_select_fusion.meta_ref
  7.6 0.8 multiply_sine_fusion
  8.4 0.7 pad_maximum_fusion.qo
  9.1 0.6 fusion.small
  9.7 75.0 %gather_weights.1 = (bf16[2,4,56,1216]{3,2,1,0:T(8,128)(2,1)}, bf16[2,152,896]{2,1,0:T(8,128)(2,1)}, bf16[4,4,56,1216]{3,2,1,0:T(8,128)(2,1)}, bf16[2,4,4,56,2048]{4,3,2,1,0:T(8,128)(2,1)}, f32[2,24,128]{2,1,0:T(8,128)}) custom-call(bf16[1,56,9728]{2,1,0:T(8,128)(2,1)} %w_ref.1, bf16[2,152,896]{2,1,0:T(8,128)(2,1)} %bitcast.48, ...), custom_call_target="tpu_custom_call" | custom-call | tf_op jit(solution)/shard_map/gather_weights/pallas_call | solution.py:371
  84.8 40.8 %attention_forward.2 = (bf16[896,256]{1,0:T(8,128)(2,1)}, bf16[14,64,256]{2,1,0:T(8,128)(2,1)}, bf16[3,4,64,256]{3,2,1,0:T(8,128)(2,1)}, f32[14,1,256]{2,1,0:T(1...) custom-call(f32[896,256]{1,0:T(8,128)} %convert_bitcast_fusion.h_ref, ...), custom_call_target="tpu_custom_call" | custom-call | tf_op jit(solution)/shard_map/attention_forward/pallas_call | solution.py:371
  125.5 58.8 %feed_forward.2 = (f32[896,256]{1,0:T(8,128)}, bf16[896,2048]{1,0:T(8,128)(2,1)}, bf16[1216,2048]{1,0:T(8,128)(2,1)}, bf16[4,4,56,1216]{3,2,1,0:T(8,128)(2,1)}) custom-call(bf16[896,256]{1,0:T(8,128)(2,1)} %get-tuple-element.62.x_ref, f32[896,256]{1,0:T(8,128)} %get-tuple-element.63.res_ref, bf16[896,1216]{1,0:T(8,128)(2,1)} %bitcast.37, ...), custom_call_target="tpu_custom_call" | custom-call | tf_op jit(solution)/shard_map/feed_forward/pallas_call | solution.py:371
  184.3 38.4 %attention_forward.3 = (bf16[896,256]{1,0:T(8,128)(2,1)}, bf16[14,64,256]{2,1,0:T(8,128)(2,1)}, bf16[3,4,64,256]{3,2,1,0:T(8,128)(2,1)}, f32[14,1,256]{2,1,0:T(1...) custom-call(f32[896,256]{1,0:T(8,128)} %get-tuple-element.67.h_ref.o, ...), custom_call_target="tpu_custom_call" | custom-call | tf_op jit(solution)/shard_map/attention_forward/pallas_call | solution.py:371
  222.7 52.5 %feed_forward.3 = (f32[896,256]{1,0:T(8,128)}, bf16[896,2048]{1,0:T(8,128)(2,1)}, bf16[1216,2048]{1,0:T(8,128)(2,1)}) custom-call(bf16[896,256]{1,0:T(8,128)(2,1)} %get-tuple-element.69.x_ref, f32[896,256]{1,0:T(8,128)} %get-tuple-element.68.res_ref, bf16[896,1216]{1,0:T(8,128)(2,1)} %bitcast.35, bf16[608,896]{1,0:T(8,128)(2,1)} %bitcast.41), custom_call_target="tpu_custom_call" | custom-call | tf_op jit(solution)/shard_map/feed_forward/pallas_call | solution.py:371
  275.2 0.1 select_convert_fusion.1
  275.3 2.8 collective-permute-start
  278.2 0.2 copy.22
  278.4 1.0 convert_bitcast_fusion.1.g_ref
  279.4 53.8 %feed_backward.2 = (f32[896,256]{1,0:T(8,128)}, bf16[896,1216]{1,0:T(8,128)(2,1)}, bf16[608,896]{1,0:T(8,128)(2,1)}, f32[7,128]{1,0:T(8,128)}) custom-call(f32[896,256]{1,0:T(8,128)} %convert_bitcast_fusion.1.g_ref, f32[896,256]{1,0:T(8,128)} %get-tuple-element.68.res_ref, bf16[896,2048]{1,0:T(8,128)(2,1)} %get-tuple-element.72.x_all, ...), custom_call_target="tpu_custom_call" | custom-call | tf_op jit(solution)/shard_map/feed_backward/pallas_call | solution.py:371
  333.1 40.3 %attention_backward.2 = (f32[896,256]{1,0:T(8,128)}, bf16[896,2048]{1,0:T(8,128)(2,1)}, f32[16,128]{1,0:T(8,128)}, bf16[4,152,896]{2,1,0:T(8,128)(2,1)}) custom-call(f32[896,256]{1,0:T(8,128)} %get-tuple-element.74.g_ref, f32[2,24,128]{2,1,0:T(8,128)} %get-tuple-element.59.small_ref, f32[6,128]{1,0:T(8,128)} %broadcast_select_fusion.meta_ref, ...), custom_call_target="tpu_custom_call" | custom-call | tf_op jit(solution)/shard_map/attention_backward/pallas_call | solution.py:371
  373.5 61.7 %feed_backward.3 = (f32[896,256]{1,0:T(8,128)}, bf16[896,1216]{1,0:T(8,128)(2,1)}, bf16[608,896]{1,0:T(8,128)(2,1)}, f32[7,128]{1,0:T(8,128)}, bf16[4,4,56,1216]{3,2,1,0:T(8,128)(2,1)}) custom-call(f32[896,256]{1,0:T(8,128)} %get-tuple-element.81.g_ref.gh1, f32[896,256]{1,0:T(8,128)} %get-tuple-element.63.res_ref, ...), custom_call_target="tpu_custom_call" | custom-call | tf_op jit(solution)/shard_map/feed_backward/pallas_call | solution.py:371
  435.2 50.9 %attention_backward.3 = (f32[896,256]{1,0:T(8,128)}, bf16[896,2048]{1,0:T(8,128)(2,1)}, f32[16,128]{1,0:T(8,128)}, bf16[4,152,896]{2,1,0:T(8,128)(2,1)}, bf16[4,1,56,1216]{3,2,1,0:T(8,128)(2,1)}) custom-call(f32[896,256]{1,0:T(8,128)} %get-tuple-element.85.g_ref, f32[2,24,128]{2,1,0:T(8,128)} %get-tuple-element.59.small_ref, ...), custom_call_target="tpu_custom_call" | custom-call | tf_op jit(solution)/shard_map/attention_backward/pallas_call | solution.py:371
  486.2 1.3 select_convert_fusion
  487.5 85.4 %reduce_gradients.1 = (f32[56,2048]{1,0:T(8,128)}, f32[48,128]{1,0:T(8,128)}, bf16[8,56,1216]{2,1,0:T(8,128)(2,1)}, bf16[2,152,896]{2,1,0:T(8,128)(2,1)}) custom-call(bf16[4,4,56,2048]{3,2,1,0:T(8,128)(2,1)} %bitcast.44, bf16[4,4,56,2048]{3,2,1,0:T(8,128)(2,1)} %bitcast.43, f32[16,128]{1,0:T(8,128)} %get-tuple-element.95.sa0, ...), custom_call_target="tpu_custom_call" | custom-call | tf_op jit(solution)/shard_map/reduce_gradients/pallas_call | solution.py:371
  573.0 0.7 copy-done.4
  573.8 0.1 copy-done.5
  573.9 7.4 %lay_out.1 = (f32[1,2,256,896]{3,2,1,0:T(8,128)}, f32[1,2,256,896]{3,2,1,0:T(8,128)}, f32[1,896]{1,0:T(1,128)}, f32[1,56,1152]{2,1,0:T(8,128)}, f32[1,1152]{1,0:...) custom-call(bf16[8,56,1216]{2,1,0:T(8,128)(2,1)} %get-tuple-element.103.gu, ...), custom_call_target="tpu_custom_call" | custom-call | tf_op jit(solution)/shard_map/lay_out/pallas_call | solution.py:1294
  (28 shorter events, 0.3 us)
Async XLA Ops:
  0.6 5.0 copy-start
  0.7 7.8 %copy-start.8 = (bf16[1,56,896]{2,1,0:T(8,128)(2,1)S(1)}, bf16[1,56,896]{2,1,0:T(8,128)(2,1)}, u32[]{:S(2)}) copy-start(bf16[1,56,896]{2,1,0:T(8,128)(2,1)} %param.18) | copy-start | bytes 301060
  0.7 7.8 %copy-start.7 = (bf16[1,56,1152]{2,1,0:T(8,128)(2,1)S(1)}, bf16[1,56,1152]{2,1,0:T(8,128)(2,1)}, u32[]{:S(2)}) copy-start(bf16[1,56,1152]{2,1,0:T(8,128)(2,1)} %param.16) | copy-start | bytes 387076
  222.7 52.5 %copy-start.2 = (f32[896,256]{1,0:T(8,128)S(1)}, f32[896,256]{1,0:T(8,128)}, u32[]{:S(2)}) copy-start(f32[896,256]{1,0:T(8,128)} %get-tuple-element.67.h_ref.out0) | copy-start | bytes 2752516
  275.2 2.9 copy-start.6
  275.3 297.7 %collective-permute-start = (bf16[896,256]{1,0:T(8,128)(2,1)S(1)}, bf16[896,256]{1,0:T(8,128)(2,1)S(1)}, u32[]{:S(2)}, u32[]{:S(2)}) collective-permute-start(bf16[896,256]{1,0:T(8,128)(2,1)S(1)} %select_convert_fusion.1), channel_id=1, source_target_pairs={{0,16},{16,0},{1,17},{17,1},{2,18},{18,2},{3,19},{19,3},{4,20},{20... | collective-permute-start | bytes 1376264 | tf_op jit(solution)/shard_map/ppermute | solution.py:1393
  435.2 51.0 %copy-start.3 = (f32[896,256]{1,0:T(8,128)S(1)}, f32[896,256]{1,0:T(8,128)}, u32[]{:S(2)}) copy-start(f32[896,256]{1,0:T(8,128)} %get-tuple-element.81.g_ref.gh1) | copy-start | bytes 2752516
  487.5 85.6 %collective-permute-start.1 = (bf16[896,256]{1,0:T(8,128)(2,1)S(1)}, bf16[896,256]{1,0:T(8,128)(2,1)S(1)}, u32[]{:S(2)}, u32[]{:S(2)}) collective-permute-start(bf16[896,256]{1,0:T(8,128)(2,1)S(1)} %select_convert_fusion), channel_id=1, source_target_pairs={{0,16},{16,0},{1,17},{17,1},{2,18},{18,2},{3,19},{19,3},{4,20},{20... | collective-permute-start | bytes 1376264 | tf_op jit(solution)/shard_map/ppermute | solution.py:1393
  573.0 0.8 copy-start.4
  573.0 0.9 copy-start.5
  573.0 8.3 %copy-start.1 = (bf16[2,256,896]{2,1,0:T(8,128)(2,1)S(1)}, bf16[2,256,896]{2,1,0:T(8,128)(2,1)}, u32[]{:S(2)}) copy-start(bf16[2,256,896]{2,1,0:T(8,128)(2,1)} %param.11) | copy-start | bytes 2752516

commit v3 on v2

--- a/solution.py
+++ b/solution.py
@@ -219,6 +219,10 @@
         core = self.place.mates()[0]
         return remote(self.away.at[q], self.back.at[q], self.ssem.at[q], self.rsem.at[q], core)
 
+    def far_copy(self, e):
+        return remote(self.away.at[e - 1], self.back.at[e - 1], self.ssem.at[e - 1],
+                      self.rsem.at[e - 1], self.place.plane(e))
+
     def hop_copy(self, k, device):
         return remote(
             self.hop.at[k], self.hop.at[k + 3], self.ssem.at[4 + k], self.rsem.at[4 + k], device
@@ -241,7 +245,7 @@
         self.core_copy(1).wait_recv()
         self.core_copy(2).wait_recv()
         q = c * 1 + (1 - c) * 2
-        self.hop[0] = (self.near[q] + self.back[q].astype(F32)).astype(BF)
+        self.hop[0] = (self.mine(q) + self.back[q].astype(F32)).astype(BF)
         self.hop_copy(0, first).start()
 
     def diagonal(self):
@@ -250,38 +254,88 @@
             return
         first, second = self.targets()
         self.core_copy(3).wait_recv()
-        self.hop[1] = (self.near[3] + self.back[3].astype(F32)).astype(BF)
+        self.hop[1] = (self.mine(3) + self.back[3].astype(F32)).astype(BF)
         self.hop_copy(1, first).start()
 
+    def mine(self, q):
+        return self.near[q]
+
     def result(self, store):
+        self.late()
+        self.finish(store)
+
+    def late(self):
         pc = self.place
         if not pc.two_level:
-            total = self.near[0]
-            for e in range(1, pc.count):
-                remote(self.away.at[e - 1], self.back.at[e - 1], self.ssem.at[e - 1],
-                       self.rsem.at[e - 1], pc.plane(e)).wait()
-                total = total + self.back[e - 1].astype(F32)
-            store(total)
             return
         c = pc.f % 2
         first, second = self.targets()
         self.hop_copy(1, first).wait_recv()
         q = c * 2 + (1 - c) * 1
         self.hop[2] = (
-            self.near[q] + self.back[q].astype(F32) + self.hop[4].astype(F32)
+            self.mine(q) + self.back[q].astype(F32) + self.hop[4].astype(F32)
         ).astype(BF)
         self.hop_copy(2, second).start()
+
+    def finish(self, store):
+        pc = self.place
+        if not pc.two_level:
+            total = self.mine(0)
+            for e in range(1, pc.count):
+                self.far_copy(e).wait()
+                total = total + self.back[e - 1].astype(F32)
+            store(total)
+            return
+        first, second = self.targets()
         self.core_copy(0).wait_recv()
         self.hop_copy(0, first).wait_recv()
-        part = self.near[0] + self.back[0].astype(F32) + self.hop[3].astype(F32)
-        self.near[0] = part
         self.hop_copy(2, second).wait_recv()
-        store(self.near[0] + self.hop[5].astype(F32))
+        store(
+            self.mine(0)
+            + self.back[0].astype(F32)
+            + self.hop[3].astype(F32)
+            + self.hop[5].astype(F32)
+        )
         for q in range(4):
             self.core_copy(q).wait_send()
         self.hop_copy(0, first).wait_send()
         self.hop_copy(1, first).wait_send()
         self.hop_copy(2, second).wait_send()
+
+
+class ReadyScatter(PlaneScatter):
+    def __init__(self, place, parts, back, hop, ssem, rsem):
+        super().__init__(place, None, None, back, hop, ssem, rsem)
+        self.parts = parts
+        if place.two_level:
+            o = place.slots()
+            self.here = (o[0], o[2], o[3], o[6])
+            self.gone = (o[1], o[4], o[5], o[7])
+
+    def mine(self, q):
+        if not self.place.two_level:
+            return self.parts[self.place.me].astype(F32)
+        return self.parts[pick(q, self.here)].astype(F32)
+
+    def core_copy(self, q):
+        core = self.place.mates()[0]
+        v = self.parts.at[self.gone[q]]
+        return remote(v, self.back.at[q], self.ssem.at[q], self.rsem.at[q], core)
+
+    def far_copy(self, e):
+        pc = self.place
+        v = self.parts.at[(pc.me + e) % pc.count]
+        return remote(v, self.back.at[e - 1], self.ssem.at[e - 1], self.rsem.at[e - 1],
+                      pc.plane(e))
+
+    def start(self):
+        pc = self.place
+        if pc.two_level:
+            for q in (2, 1, 3, 0):
+                self.core_copy(q).start()
+        else:
+            for e in range(1, pc.count):
+                self.far_copy(e).start()
 
 
 class LineGather:
@@ -568,18 +622,29 @@
 
 
 def attention_forward_kernel(
-    dims, nk, layer, specs, h_ref, small_ref, meta_ref, docs_ref, cos_ref, sin_ref, qo_all, *refs
+    dims, nk, layer, specs, carry, h_ref, small_ref, meta_ref, docs_ref, cos_ref, sin_ref, qo_all,
+    *refs
 ):
     n = len(specs)
+    if carry:
+        block_ref, refs = (refs[0], refs[1:])
     ins, refs = (refs[:n], refs[n:])
     normed_ref, q_ref, kv_ref, lse_ref, mixed_ref, res_ref, n2_ref = refs[:7]
     outs, refs = (refs[7 : 7 + n], refs[7 + n :])
+    if carry:
+        block_all, refs = (refs[0], refs[1:])
     w, wo, mask, joined, ssem, rsem, qsem = refs[:7]
+    refs = refs[7:]
     pc = Place(dims)
     width, rows = h_ref.shape
     loads = load_qo(qo_all, layer, w, wo, qsem)
-    greet(pc, None, True)
-    riders = riders_of(pc, specs, ins, outs, refs[7:])
+    greet(pc, "mates" if carry else None, True)
+    riders = riders_of(pc, specs, ins, outs, refs[: 3 * n])
+    gather = None
+    if carry:
+        gather = PlaneGather(pc, lambda q: block_all.at[:, lanes(q, rows)], *refs[3 * n :])
+        block_all[:, lanes(pc.me, rows)] = block_ref[...]
+        gather.start()
     g1, g2, bias = gains_of(padded_t(small_ref[layer]), width, w.shape[1])
     hidden = h_ref[...].astype(BF).astype(F32)
     normed = (hidden * rms(hidden) * g1).astype(BF)
@@ -608,8 +673,6 @@
     ]
     for c in sends:
         c.start()
-    for r in riders:
-        r.start()
     scale = HD**-0.5
     for head in range(H):
         r1, r2 = turned(head * HD)
@@ -617,11 +680,13 @@
         q_ref[head, half:, :] = (r2 * scale).astype(BF)
     for c in sends:
         c.wait()
+    for r in riders:
+        r.start()
     for g in range(KVH):
         keys = [kv_ref[j, g].T for j in range(nk)]
         values = [kv_ref[j, KVH + g] for j in range(nk)]
 
-        def one_head(i, carry):
+        def one_head(i, carried):
             head = g * GROUP + i
             q = q_ref[head]
             s = [nn(keys[j], q) + mask[j] for j in range(nk)]
@@ -637,21 +702,30 @@
                 out = out + nn(values[j], e[j].astype(BF))
             lse_ref[head] = top + jnp.log(total)
             mixed_ref[head] = (out / total).astype(BF)
-            return carry
+            return carried
 
         lax.fori_loop(0, GROUP, one_head, 0)
+        if carry and g == 0:
+            for step in range(1, min(6, pc.count)):
+                gather.before(step)
     mixed = mixed_ref[...].reshape(H * HD, rows)
     loads[1].wait()
     residual = hidden + tn(wo[...], mixed)
     res_ref[...] = residual
     n2_ref[...] = (residual * rms(residual) * g2).astype(BF)
+    if carry:
+        for step in range(min(6, pc.count), pc.count):
+            gather.before(step)
+        gather.finish()
     for r in riders:
         r.finish()
 
 
 def attention_forward(dims, nk, cid, layer, hidden, small, meta, docs, cos_part, sin_part, qo_all,
-                      specs, riders):
+                      specs, riders, block=None):
     width, rows = hidden.shape
+    count = dims[0] * dims[2]
+    carry = block is not None
     qkv = qo_all.shape[2] - width
     sds = jax.ShapeDtypeStruct
     outs = [
@@ -665,13 +739,15 @@
     ] + rider_shapes(dims, specs, riders)
     dma = pltpu.SemaphoreType.DMA
     n = len(specs)
+    if carry:
+        outs.append(sds((width, count * rows), BF))
     out = call(
-        functools.partial(attention_forward_kernel, dims, nk, layer, specs),
+        functools.partial(attention_forward_kernel, dims, nk, layer, specs, carry),
         "attention_forward",
         cid,
         tuple(outs),
-        [VM] * 7 + [AN] * n,
-        [VM] * 6 + [AN] * (1 + n),
+        [VM] * 7 + [AN] * n + [VM] * carry,
+        [VM] * 6 + [AN] + [VM] * carry + [AN] * n,
         [
             pltpu.VMEM((width, qkv), BF),
             pltpu.VMEM((width, width), BF),
@@ -681,27 +757,37 @@
             dma((nk - 1,)),
             dma((2,)),
         ]
-        + line_sems(dims) * n,
-        (hidden, small, meta, docs, cos_part, sin_part, qo_all, *riders),
+        + line_sems(dims) * n
+        + [dma((count - 1,))] * (2 * carry),
+        (hidden, small, meta, docs, cos_part, sin_part, qo_all, *([block] * carry), *riders),
     )
     return (out[:7], out[7:])
 
 
 def attention_backward_kernel(
-    dims, nk, layer, specs, g_ref, small_ref, meta_ref, docs_ref, cos_ref, sin_ref,
+    dims, nk, layer, specs, carry, g_ref, small_ref, meta_ref, docs_ref, cos_ref, sin_ref,
     h_ref, normed_ref, q_ref, kv_ref, lse_ref, mixed_ref, qo_all, *refs
 ):
     n = len(specs)
+    if carry:
+        parts_ref, res_ref, refs = (refs[0], refs[1], refs[2:])
     ins, refs = (refs[:n], refs[n:])
     gh_ref, dqo_ref, dsmall_ref = refs[:3]
     outs, refs = (refs[3 : 3 + n], refs[3 + n :])
+    if carry:
+        out_ref, refs = (refs[0], refs[1:])
     w, wo, mask, dmix, dkv, out_kv, in_kv, gj, ssem, rsem, qsem = refs[:11]
+    refs = refs[11:]
     pc = Place(dims)
     width, rows = h_ref.shape
     qkv = w.shape[1]
     loads = load_qo(qo_all, layer, w, wo, qsem)
-    greet(pc, None, True)
-    riders = riders_of(pc, specs, ins, outs, refs[11:])
+    greet(pc, "mates" if carry else None, True)
+    riders = riders_of(pc, specs, ins, outs, refs[: 3 * n])
+    scatter = None
+    if carry:
+        scatter = ReadyScatter(pc, parts_ref, *refs[3 * n :])
+        scatter.start()
     for r in riders:
         r.start()
     g1 = column(padded_t(small_ref[layer]), 0, width // 128)
@@ -710,6 +796,9 @@
     loads[1].wait()
     dmix[...] = nn(wo[...], grl).astype(BF).reshape(dmix.shape)
     dqo_ref[:, qkv:] = nt(mixed_ref[...].reshape(H * HD, rows), grl).astype(BF)
+    if carry:
+        scatter.early()
+        scatter.diagonal()
     cos_part = cos_ref[...]
     sin_part = sin_ref[...]
     half = HD // 2
@@ -724,7 +813,7 @@
         keys = [k.T for k in keys_t]
         values = [kv_ref[j, KVH + g].T for j in range(nk)]
 
-        def one_head(i, carry):
+        def one_head(i, carried):
             head = g * GROUP + i
             q = q_ref[head]
             do = dmix[head]
@@ -744,9 +833,11 @@
             r1, r2 = unturned(dq[:half], dq[half:])
             gj[pl.ds(pl.multiple_of(head * HD, HD), half), :] = r1.astype(BF)
             gj[pl.ds(pl.multiple_of(head * HD + half, half), half), :] = r2.astype(BF)
-            return carry
+            return carried
 
         lax.fori_loop(0, GROUP, one_head, 0)
+        if carry and g == 0:
+            scatter.late()
     for j in range(1, nk):
         out_kv[j - 1] = dkv[j].astype(BF)
     sends = [
@@ -780,13 +871,20 @@
     dsmall_ref[:n1, :] = rows_of(gn * unit)
     u = gn * g1
     gh_ref[...] = g_ref[...] + scale_one * (u - unit * jnp.mean(u * unit, axis=0, keepdims=True))
+    if carry:
+
+        def store(total):
+            out_ref[...] = res_ref[...] + total
+
+        scatter.finish(store)
     for r in riders:
         r.finish()
 
 
 def attention_backward(dims, nk, cid, layer, g, small, meta, docs, cos_part, sin_part, hidden,
-                       normed, q, kv, lse, mixed, qo_all, specs, riders):
+                       normed, q, kv, lse, mixed, qo_all, specs, riders, late=()):
     width, rows = hidden.shape
+    carry = len(late) > 0
     qkv = qo_all.shape[2] - width
     sds = jax.ShapeDtypeStruct
     outs = [
@@ -797,13 +895,15 @@
     dma = pltpu.SemaphoreType.DMA
     block = (2 * KVH, HD, rows)
     n = len(specs)
+    if carry:
+        outs.append(sds((width, rows), F32))
     out = call(
-        functools.partial(attention_backward_kernel, dims, nk, layer, specs),
+        functools.partial(attention_backward_kernel, dims, nk, layer, specs, carry),
         "attention_backward",
         cid,
         tuple(outs),
-        [VM] * 3 + [AN] * n,
-        [VM] * 12 + [AN] * (1 + n),
+        [VM] * 3 + [AN] * n + [VM] * carry,
+        [VM] * 12 + [AN] + [VM] * len(late) + [AN] * n,
         [
             pltpu.VMEM((width, qkv), BF),
             pltpu.VMEM((width, width), BF),
@@ -817,9 +917,10 @@
             dma((nk - 1,)),
             dma((2,)),
         ]
-        + line_sems(dims) * n,
+        + line_sems(dims) * n
+        + (scatter_scratch(dims, width, rows)[2:] if carry else []),
         (g, small, meta, docs, cos_part, sin_part, hidden, normed, q, kv, lse, mixed, qo_all,
-         *riders),
+         *late, *riders),
     )
     return (out[:3], out[3:])
 
@@ -989,12 +1090,13 @@
 
     lax.fori_loop(0, pc.count, step_body, 0)
     scatter.diagonal()
+    dwd_ref[...] = nt(inner[...], g_all[...]).astype(BF)
+    scatter.late()
     part = width // 2
     for r in range(2):
         dwgu_ref[r * part : (r + 1) * part, :] = nt(
             x_all[r * part : (r + 1) * part, :], ggu[...]
         ).astype(BF)
-    dwd_ref[...] = nt(inner[...], g_all[...]).astype(BF)
 
     def store(total):
         residual = res_ref[...]
@@ -1007,7 +1109,7 @@
             u - unit * jnp.mean(u * unit, axis=0, keepdims=True)
         )
 
-    scatter.result(store)
+    scatter.finish(store)
     gather.finish()
     for r in riders:
         r.finish()
@@ -1045,6 +1147,119 @@
         (g, residual, x_all, gu_all, wgu, wd, small, *riders),
     )
     return (out[:4], out[4:])
+
+
+def feed_both_kernel(
+    dims, layer, x_ref, res_ref, g_ref, g_all, wgu_ref, wd_ref, small_ref,
+    gr_ref, dwgu_ref, dwd_ref, dsmall_ref, parts_ref,
+    x_all, inner, ggu, wgu_t, wd_t, gu, gi, near, away, back, hop, ss, sr, gs, gr,
+):
+    pc = Place(dims)
+    width, rows = g_ref.shape
+    ff = wd_ref.shape[0]
+    greet(pc, "mates", False)
+    gather = PlaneGather(pc, lambda q: x_all.at[:, lanes(q, rows)], gs, gr)
+    scatter = PlaneScatter(pc, near, away, back, hop, ss, sr)
+    x_all[:, lanes(pc.me, rows)] = x_ref[...]
+    gather.start()
+    transpose_into(wgu_t, wgu_ref)
+    transpose_into(wd_t, wd_ref)
+    neighbours, last = steps_of(pc.count)
+    chunk = 32 if ff % 32 == 0 else 16
+
+    def step_body(step, carry):
+        for k in range(pc.count):
+            @pl.when(step == k)
+            def _():
+                gather.before(k)
+
+        slot = pick(step, gather.order)
+        sl = lanes(slot, rows)
+        gu[...] = nn(wgu_t[...], x_all[:, sl])
+        gi[...] = nn(wd_ref[...], g_all[:, sl])
+
+        def act(i, c):
+            r = pl.multiple_of(i * chunk, chunk)
+            gate = gu[pl.ds(r, chunk), :]
+            up = gu[pl.ds(ff + r, chunk), :]
+            grad = gi[pl.ds(r, chunk), :]
+            sig = jax.nn.sigmoid(gate)
+            silu = gate * sig
+            inner[pl.ds(r, chunk), sl] = (silu * up).astype(BF)
+            ggu[pl.ds(r, chunk), sl] = (grad * up * sig * (1.0 + gate * (1.0 - sig))).astype(BF)
+            ggu[pl.ds(ff + r, chunk), sl] = (grad * silu).astype(BF)
+            return c
+
+        lax.fori_loop(0, ff // chunk, act, 0)
+        scatter.put(step, nn(wgu_ref[...], ggu[:, sl]))
+
+        @pl.when(step == neighbours)
+        def _():
+            scatter.early()
+
+        @pl.when(step == last)
+        def _():
+            scatter.diagonal()
+
+        parts_ref[slot] = nn(wd_t[...], inner[:, sl]).astype(BF)
+        return carry
+
+    lax.fori_loop(0, pc.count, step_body, 0)
+    dwd_ref[...] = nt(inner[...], g_all[...]).astype(BF)
+    scatter.late()
+    part = width // 2
+    for r in range(2):
+        dwgu_ref[r * part : (r + 1) * part, :] = nt(
+            x_all[r * part : (r + 1) * part, :], ggu[...]
+        ).astype(BF)
+
+    def store(total):
+        residual = res_ref[...]
+        scale_two = rms(residual)
+        unit = residual * scale_two
+        n1 = width // 128
+        dsmall_ref[...] = rows_of(total * unit)
+        u = total * column(padded_t(small_ref[layer]), n1, n1)
+        gr_ref[...] = g_ref[...].astype(BF).astype(F32) + scale_two * (
+            u - unit * jnp.mean(u * unit, axis=0, keepdims=True)
+        )
+
+    scatter.finish(store)
+    gather.finish()
+
+
+def feed_both(dims, cid, layer, x, residual, g, g_all, wgu, wd, small):
+    width, rows = g.shape
+    count = dims[0] * dims[2]
+    two_ff, ff = (wgu.shape[1], wd.shape[0])
+    sds = jax.ShapeDtypeStruct
+    dma = pltpu.SemaphoreType.DMA
+    return call(
+        functools.partial(feed_both_kernel, dims, layer),
+        "feed_both",
+        cid,
+        (
+            sds((width, rows), F32),
+            sds(wgu.shape, BF),
+            sds(wd.shape, BF),
+            sds((width // 128, 128), F32),
+            sds((count, width, rows), BF),
+        ),
+        [VM] * 5,
+        [VM] * 7,
+        [
+            pltpu.VMEM((width, count * rows), BF),
+            pltpu.VMEM((ff, count * rows), BF),
+            pltpu.VMEM((two_ff, count * rows), BF),
+            pltpu.VMEM((two_ff, width), BF),
+            pltpu.VMEM((width, ff), BF),
+            pltpu.VMEM((two_ff, rows), F32),
+            pltpu.VMEM((ff, rows), F32),
+        ]
+        + scatter_scratch(dims, width, rows)
+        + [dma((count - 1,)), dma((count - 1,))],
+        (x, residual, g, g_all, wgu, wd, small),
+    )
 
 
 def reduce_kernel(
@@ -1365,18 +1580,19 @@
     wgu0 = gu_first.reshape(wide)
     f0, (gu1,) = feed_forward(dims, 3, a0[6], a0[5], wgu0, wd0, (("gather", 1),), (gup,))
     wgu1 = gu1.reshape(wide)
-    a1, (wd1,) = attention_forward(dims, nk, 2, 1, f0[0], *common, (("gather", 1),), (wdp,))
+    a1, (wd1, g_all) = attention_forward(
+        dims, nk, 2, 1, f0[0], *common, (("gather", 1),), (wdp,), cot.T
+    )
     wd1 = wd1.reshape(ff, width)
-    f1, _ = feed_forward(dims, 4, a1[6], a1[5], wgu1, wd1, (), ())
 
     line_gu = (nb, nf, dr, 2 * ff)
     line_wd = (nb, half, width)
     everything = (0, half)
     cut = max(1, nf // 4)
-    b1, _ = feed_backward(dims, 5, 1, g, a1[5], f1[1], f1[2], wgu1, wd1, small_all, (), ())
-    ab1, (dwd1,) = attention_backward(
+    b1 = feed_both(dims, 4, 1, a1[6], a1[5], g, g_all, wgu1, wd1, small_all)
+    ab1, (dwd1, out1) = attention_backward(
         dims, nk, 7, 1, b1[0], *common[:5], f0[0], *a1[:5], qo_all,
-        (("exchange", everything),), (b1[2].reshape(line_wd),),
+        (("exchange", everything),), (b1[2].reshape(line_wd),), (b1[4], a1[5]),
     )
     b0, (dgu1,) = feed_backward(
         dims, 6, 0, ab1[0], a0[5], f0[1], f0[2], wgu0, wd0, small_all,
@@ -1392,7 +1608,7 @@
         give = jnp.where(s == 0, values[1], values[0]).astype(BF)
         return lax.ppermute(give, "section", [(0, 1), (1, 0)])
 
-    take_out = swapped((f0[0], f1[0]))
+    take_out = swapped((f0[0], out1))
     take_grad = swapped((ab0[0], ab1[0]))
     line_qo = (nb, nf, dr, qkv + width)
     grad_qo, small_sum, gu_got, wd_got = reduce_gradients(
@@ -1402,7 +1618,7 @@
     return lay_out(
         dims,
         qkv,
-        (gu_got, wd_got, grad_qo, small_sum, f0[0], f1[0], ab0[0], ab1[0], take_out, take_grad),
+        (gu_got, wd_got, grad_qo, small_sum, f0[0], out1, ab0[0], ab1[0], take_out, take_grad),
     )
 
 

time: 585 us -> 547 us (0.935)
  Pallas kernels: 565 us -> 526 us
    pallas_call x10 -> x9, Pallas kernels: 558 us -> 518 us  [call(): pl.pallas_call(kernel, name=name, out_shape=outs, in_specs=in_specs, out_...]
  transfers between devices with their start and end apart: 2 -> 2, of which waited for: 0 -> 0; matrix products, arithmetic and copies ran while one was open for 0% -> 0% of each run, Pallas kernels for 50% -> 37%
where the time goes in v3:
time: 547 us; the launch traced here: 543 us
  Pallas kernels  526 us (96%)
  other arithmetic  9.71 us (2%)
    pallas_call x9, Pallas kernels, call(): pl.pallas_call(kernel, name=name, out_shape=outs, in_specs=in_specs, out_...  518 us
  transfers between devices with their start and end apart: 2, of which 0 were waited for; matrix products, arithmetic and copies ran while one was open for 0% of the time, Pallas kernels for 37%

profile of v3, /device:TPU:12, one launch (start us, length us, event | category | flops | bytes accessed | tf_op | source)
XLA Modules:
  0.0 543.2 jit_solution(15135965932782980228)
XLA Ops:
  0.8 0.1 broadcast_in_dim.17
  0.9 0.7 fusion.1
  1.6 0.7 convert_reduce_fusion
  2.3 0.6 gather_fusion
  2.9 0.6 constant_dynamic-slice_fusion.2.docs_ref
  3.4 0.7 reduce
  4.1 0.7 reduce.1
  4.8 0.7 reduce.2
  5.5 1.2 constant_dynamic-slice_fusion
  6.8 0.2 copy.21
  7.0 0.2 copy.22
  7.3 1.0 convert_bitcast_fusion.h_ref
  8.2 1.0 bitcast_convert_fusion.g_ref
  9.2 0.7 broadcast_select_fusion.meta_ref
  9.9 0.8 multiply_sine_fusion
  10.7 0.7 pad_maximum_fusion.qo
  11.4 0.6 fusion.small
  12.0 75.0 %gather_weights.1 = (bf16[2,4,56,1216]{3,2,1,0:T(8,128)(2,1)}, bf16[2,152,896]{2,1,0:T(8,128)(2,1)}, bf16[4,4,56,1216]{3,2,1,0:T(8,128)(2,1)}, bf16[2,4,4,56,2048]{4,3,2,1,0:T(8,128)(2,1)}, f32[2,24,128]{2,1,0:T(8,128)}) custom-call(bf16[1,56,9728]{2,1,0:T(8,128)(2,1)} %w_ref.1, bf16[2,152,896]{2,1,0:T(8,128)(2,1)} %bitcast.46, ...), custom_call_target="tpu_custom_call" | custom-call | tf_op jit(solution)/shard_map/gather_weights/pallas_call | solution.py:425
  87.1 40.7 %attention_forward.2 = (bf16[896,256]{1,0:T(8,128)(2,1)}, bf16[14,64,256]{2,1,0:T(8,128)(2,1)}, bf16[3,4,64,256]{3,2,1,0:T(8,128)(2,1)}, f32[14,1,256]{2,1,0:T(1...) custom-call(f32[896,256]{1,0:T(8,128)} %convert_bitcast_fusion.h_ref, ...), custom_call_target="tpu_custom_call" | custom-call | tf_op jit(solution)/shard_map/attention_forward/pallas_call | solution.py:425
  127.8 58.1 %feed_forward.1 = (f32[896,256]{1,0:T(8,128)}, bf16[896,2048]{1,0:T(8,128)(2,1)}, bf16[1216,2048]{1,0:T(8,128)(2,1)}, bf16[4,4,56,1216]{3,2,1,0:T(8,128)(2,1)}) custom-call(bf16[896,256]{1,0:T(8,128)(2,1)} %get-tuple-element.62.x_ref, f32[896,256]{1,0:T(8,128)} %get-tuple-element.63.res_ref, bf16[896,1216]{1,0:T(8,128)(2,1)} %bitcast.34, ...), custom_call_target="tpu_custom_call" | custom-call | tf_op jit(solution)/shard_map/feed_forward/pallas_call | solution.py:425
  185.9 40.3 %attention_forward.3 = (bf16[896,256]{1,0:T(8,128)(2,1)}, bf16[14,64,256]{2,1,0:T(8,128)(2,1)}, bf16[3,4,64,256]{3,2,1,0:T(8,128)(2,1)}, f32[14,1,256]{2,1,0:T(1...) custom-call(f32[896,256]{1,0:T(8,128)} %get-tuple-element.67.h_ref.o, ...), custom_call_target="tpu_custom_call" | custom-call | tf_op jit(solution)/shard_map/attention_forward/pallas_call | solution.py:425
  226.1 63.3 %feed_both.1 = (f32[896,256]{1,0:T(8,128)}, bf16[896,1216]{1,0:T(8,128)(2,1)}, bf16[608,896]{1,0:T(8,128)(2,1)}, f32[7,128]{1,0:T(8,128)}, bf16[8,896,256]{2,1,0:T(8,128)(2,1)}) custom-call(bf16[896,256]{1,0:T(8,128)(2,1)} %get-tuple-element.68.x_ref, f32[896,256]{1,0:T(8,128)} %get-tuple-element.69.res_ref.refs_1_, f32[896,256]{1,0:T(8,128)} %bitcast_convert_fusion.g_ref, ...), custom_call_target="tpu_custom_call" | custom-call | tf_op jit(solution)/shard_map/feed_both/pallas_call | solution.py:425
  289.5 42.7 %attention_backward.2 = (f32[896,256]{1,0:T(8,128)}, bf16[896,2048]{1,0:T(8,128)(2,1)}, f32[16,128]{1,0:T(8,128)}, bf16[4,152,896]{2,1,0:T(8,128)(2,1)}, f32[896,256]{1,0:T(8,128)}) custom-call(f32[896,256]{1,0:T(8,128)} %get-tuple-element.73.g_ref, f32[2,24,128]{2,1,0:T(8,128)} %get-tuple-element.59.small_ref, f32[6,128]{1,0:T(8,128)} %broadcast_select_fusion.meta_ref, ...), custom_call_target="tpu_custom_call" | custom-call | tf_op jit(solution)/shard_map/attention_backward/pallas_call | solution.py:425
  332.2 0.1 select_convert_fusion.1
  332.3 2.4 collective-permute-start
  334.8 61.2 %feed_backward.1 = (f32[896,256]{1,0:T(8,128)}, bf16[896,1216]{1,0:T(8,128)(2,1)}, bf16[608,896]{1,0:T(8,128)(2,1)}, f32[7,128]{1,0:T(8,128)}, bf16[4,4,56,1216]{3,2,1,0:T(8,128)(2,1)}) custom-call(f32[896,256]{1,0:T(8,128)} %get-tuple-element.81.g_ref.gh1, f32[896,256]{1,0:T(8,128)} %get-tuple-element.63.res_ref, ...), custom_call_target="tpu_custom_call" | custom-call | tf_op jit(solution)/shard_map/feed_backward/pallas_call | solution.py:425
  396.0 51.3 %attention_backward.3 = (f32[896,256]{1,0:T(8,128)}, bf16[896,2048]{1,0:T(8,128)(2,1)}, f32[16,128]{1,0:T(8,128)}, bf16[4,152,896]{2,1,0:T(8,128)(2,1)}, bf16[4,1,56,1216]{3,2,1,0:T(8,128)(2,1)}) custom-call(f32[896,256]{1,0:T(8,128)} %get-tuple-element.85.g_ref, f32[2,24,128]{2,1,0:T(8,128)} %get-tuple-element.59.small_ref, ...), custom_call_target="tpu_custom_call" | custom-call | tf_op jit(solution)/shard_map/attention_backward/pallas_call | solution.py:425
  447.3 1.3 select_convert_fusion
  448.6 85.9 %reduce_gradients.1 = (f32[56,2048]{1,0:T(8,128)}, f32[48,128]{1,0:T(8,128)}, bf16[8,56,1216]{2,1,0:T(8,128)(2,1)}, bf16[2,152,896]{2,1,0:T(8,128)(2,1)}) custom-call(bf16[4,4,56,2048]{3,2,1,0:T(8,128)(2,1)} %bitcast.40, bf16[4,4,56,2048]{3,2,1,0:T(8,128)(2,1)} %bitcast.39, f32[16,128]{1,0:T(8,128)} %get-tuple-element.95.sa0, ...), custom_call_target="tpu_custom_call" | custom-call | tf_op jit(solution)/shard_map/reduce_gradients/pallas_call | solution.py:425
  534.6 0.8 copy-done.3
  535.4 0.2 copy-done.4
  535.5 7.4 %lay_out.1 = (f32[1,2,256,896]{3,2,1,0:T(8,128)}, f32[1,2,256,896]{3,2,1,0:T(8,128)}, f32[1,896]{1,0:T(1,128)}, f32[1,56,1152]{2,1,0:T(8,128)}, f32[1,1152]{1,0:...) custom-call(bf16[8,56,1216]{2,1,0:T(8,128)(2,1)} %get-tuple-element.103.gu, ...), custom_call_target="tpu_custom_call" | custom-call | tf_op jit(solution)/shard_map/lay_out/pallas_call | solution.py:1509
  (22 shorter events, 0.2 us)
Async XLA Ops:
  6.8 3.9 copy-start.5
  6.8 3.9 copy-start.6
  7.0 80.0 %copy-start.2 = (bf16[1,256,896]{1,2,0:T(8,128)(2,1)}, bf16[1,256,896]{1,2,0:T(8,128)(2,1)S(1)}, u32[]{:S(2)}) copy-start(bf16[1,256,896]{1,2,0:T(8,128)(2,1)S(1)} %copy.21) | copy-start | bytes 1376260
  289.5 42.8 %copy-start = (f32[896,256]{1,0:T(8,128)S(1)}, f32[896,256]{1,0:T(8,128)}, u32[]{:S(2)}) copy-start(f32[896,256]{1,0:T(8,128)} %get-tuple-element.67.h_ref.out0) | copy-start | bytes 2752516
  332.3 202.2 %collective-permute-start = (bf16[896,256]{1,0:T(8,128)(2,1)S(1)}, bf16[896,256]{1,0:T(8,128)(2,1)S(1)}, u32[]{:S(2)}, u32[]{:S(2)}) collective-permute-start(bf16[896,256]{1,0:T(8,128)(2,1)S(1)} %select_convert_fusion.1), channel_id=1, source_target_pairs={{0,16},{16,0},{1,17},{17,1},{2,18},{18,2},{3,19},{19,3},{4,20},{20... | collective-permute-start | bytes 1376264 | tf_op jit(solution)/shard_map/ppermute | solution.py:1609
  396.0 51.3 %copy-start.1 = (f32[896,256]{1,0:T(8,128)S(1)}, f32[896,256]{1,0:T(8,128)}, u32[]{:S(2)}) copy-start(f32[896,256]{1,0:T(8,128)} %get-tuple-element.81.g_ref.gh1) | copy-start | bytes 2752516
  448.5 86.0 %collective-permute-start.1 = (bf16[896,256]{1,0:T(8,128)(2,1)S(1)}, bf16[896,256]{1,0:T(8,128)(2,1)S(1)}, u32[]{:S(2)}, u32[]{:S(2)}) collective-permute-start(bf16[896,256]{1,0:T(8,128)(2,1)S(1)} %select_convert_fusion), channel_id=1, source_target_pairs={{0,16},{16,0},{1,17},{17,1},{2,18},{18,2},{3,19},{19,3},{4,20},{20... | collective-permute-start | bytes 1376264 | tf_op jit(solution)/shard_map/ppermute | solution.py:1609
  534.6 0.8 copy-start.3
  534.6 0.9 copy-start.4

commit v4 on v3

--- a/solution.py
+++ b/solution.py
@@ -340,66 +340,206 @@
 
 class LineGather:
     def __init__(self, place, piece, out, sems):
-        lsem, ss, sr = sems
-        own = out.at[place.b]
-        self.copies = [pltpu.make_async_copy(piece, own, lsem)]
-        for d in range(1, place.nb):
-            self.copies.append(remote(piece, own, ss.at[d - 1], sr.at[d - 1], place.along(d)))
+        self.place, self.piece, self.out = (place, piece, out)
+        self.lsem, self.ss, self.sr = sems
+        self.k = 0
+
+    def local(self):
+        return pltpu.make_async_copy(self.piece, self.out.at[self.place.b], self.lsem)
+
+    def hop(self, way, k, came):
+        pc = self.place
+        t = pc.b - way * (k - (0 if came else 1))
+        src = self.piece if k == 1 and not came else self.out.at[t]
+        i = k - 1 + (0 if way == 1 else pc.nb - 1)
+        return remote(
+            src, self.out.at[t], self.ss.at[i], self.sr.at[i], (pc.s, pc.b + way, pc.f)
+        )
+
+    def sends(self, way, k):
+        b, nb = (self.place.b, self.place.nb)
+        return (b >= k - 1) & (b < nb - 1) if way == 1 else (b <= nb - k) & (b > 0)
+
+    def comes(self, way, k):
+        b, nb = (self.place.b, self.place.nb)
+        return b >= k if way == 1 else b <= nb - 1 - k
+
+    def arrived(self, k):
+        for way in (1, -1):
+            @pl.when(self.comes(way, k))
+            def _():
+                self.hop(way, k, True).wait_recv()
 
     def start(self):
-        for c in self.copies:
-            c.start()
+        self.local().start()
+        self.service()
+
+    def service(self):
+        if self.k == self.place.nb - 1:
+            return
+        self.k += 1
+        if self.k > 1:
+            self.arrived(self.k - 1)
+        for way in (1, -1):
+            @pl.when(self.sends(way, self.k))
+            def _():
+                self.hop(way, self.k, False).start()
 
     def finish(self):
-        for c in self.copies:
-            c.wait()
-
-
-class LineExchange(LineGather):
-    def __init__(self, place, parts, out, sems):
-        lsem, ss, sr = sems
-        own = out(place.b)
-        self.copies = [pltpu.make_async_copy(parts(place.b), own, lsem)]
-        for d in range(1, place.nb):
-            t = place.along(d)
-            self.copies.append(remote(parts(t[1]), own, ss.at[d - 1], sr.at[d - 1], t))
-
-
-def line_sems(dims):
+        last = self.place.nb - 1
+        while self.k < last:
+            self.service()
+        self.arrived(last)
+        for k in range(1, last + 1):
+            for way in (1, -1):
+                @pl.when(self.sends(way, k))
+                def _():
+                    self.hop(way, k, False).wait_send()
+        self.local().wait()
+
+
+class LineReduce:
+    def __init__(self, place, terms, store, sems):
+        self.place, self.terms, self.store = (place, terms, store)
+        self.out, self.came, self.ss, self.sr = sems
+        self.k = 0
+
+    def index(self, way, k):
+        return k - 1 + (0 if way == 1 else self.place.nb - 1)
+
+    def hop(self, way, k):
+        pc = self.place
+        i = self.index(way, k)
+        return remote(
+            self.out.at[i], self.came.at[i], self.ss.at[i], self.sr.at[i],
+            (pc.s, pc.b + way, pc.f),
+        )
+
+    def rank(self, way):
+        pc = self.place
+        return pc.b if way == 1 else pc.nb - 1 - pc.b
+
+    def sends(self, way, k):
+        r = self.rank(way)
+        return (r < k) & (r < self.place.nb - 1)
+
+    def start(self):
+        self.service()
+
+    def service(self):
+        nb = self.place.nb
+        if self.k == nb - 1:
+            return
+        self.k += 1
+        k = self.k
+        for way in (1, -1):
+            r = self.rank(way)
+            t = nb - k + r if way == 1 else k - 1 - r
+            i = self.index(way, k)
+
+            @pl.when(self.sends(way, k) & (r == 0))
+            def _():
+                self.out[i] = self.terms(t)
+
+            if k > 1:
+                @pl.when(self.sends(way, k) & (r > 0))
+                def _():
+                    self.hop(way, k - 1).wait_recv()
+                    total = self.terms(t).astype(F32) + self.came[i - 1].astype(F32)
+                    self.out[i] = total.astype(BF)
+
+            @pl.when(self.sends(way, k))
+            def _():
+                self.hop(way, k).start()
+
+    def finish(self):
+        pc = self.place
+        last = pc.nb - 1
+        while self.k < last:
+            self.service()
+        right, left = (self.index(1, last), self.index(-1, last))
+
+        @pl.when(pc.b == 0)
+        def _():
+            self.hop(-1, last).wait_recv()
+            self.store(self.terms(pc.b).astype(F32) + self.came[left].astype(F32))
+
+        @pl.when(pc.b == last)
+        def _():
+            self.hop(1, last).wait_recv()
+            self.store(self.terms(pc.b).astype(F32) + self.came[right].astype(F32))
+
+        @pl.when((pc.b > 0) & (pc.b < last))
+        def _():
+            self.hop(1, last).wait_recv()
+            self.hop(-1, last).wait_recv()
+            self.store(
+                self.terms(pc.b).astype(F32)
+                + self.came[right].astype(F32)
+                + self.came[left].astype(F32)
+            )
+
+        for k in range(1, last + 1):
+            for way in (1, -1):
+                @pl.when(self.sends(way, k))
+                def _():
+                    self.hop(way, k).wait_send()
+
+
+def gather_scratch(dims):
     dma = pltpu.SemaphoreType.DMA
-    return [dma(()), dma((dims[1] - 1,)), dma((dims[1] - 1,))]
-
-
-def riders_of(place, specs, ins, outs, sems):
-    out = []
-    for i, spec in enumerate(specs):
-        mine = sems[3 * i : 3 * i + 3]
-        if spec[0] == "gather":
-            piece = ins[i] if spec[1] is None else ins[i].at[spec[1]]
-            out.append(LineGather(place, piece, outs[i], mine))
-        else:
-            lo, hi = spec[1]
-            out.append(
-                LineExchange(
-                    place,
-                    lambda t, r=ins[i]: r.at[t, lo:hi],
-                    lambda t, r=outs[i]: r.at[t],
-                    mine,
+    return [dma(()), dma((2 * (dims[1] - 1),)), dma((2 * (dims[1] - 1),))]
+
+
+def reduce_scratch(dims, *block):
+    dma = pltpu.SemaphoreType.DMA
+    n = 2 * (dims[1] - 1)
+    return [pltpu.VMEM((n,) + block, BF), pltpu.VMEM((n,) + block, BF), dma((n,)), dma((n,))]
+
+
+class Riders:
+    def __init__(self, dims, specs, arrays):
+        self.dims, self.specs, self.arrays = (dims, specs, arrays)
+        self.shapes = []
+        self.places = []
+        self.scratch = []
+        self.sizes = []
+        for spec, a in zip(specs, arrays):
+            if spec[0] == "gather":
+                shape = (dims[1],) + a.shape[1:]
+                self.places.append(AN)
+                scratch = gather_scratch(dims)
+            else:
+                lo, hi = spec[1]
+                shape = (hi - lo,) + a.shape[2:]
+                self.places.append(VM)
+                scratch = reduce_scratch(dims, *shape)
+            self.shapes.append(jax.ShapeDtypeStruct(shape, a.dtype))
+            self.scratch += scratch
+            self.sizes.append(len(scratch))
+        self.count = len(specs)
+
+    def board(self, place, ins, outs, scratch):
+        out = []
+        for spec, size, a, o in zip(self.specs, self.sizes, ins, outs):
+            mine, scratch = (scratch[:size], scratch[size:])
+            if spec[0] == "gather":
+                out.append(LineGather(place, a.at[spec[1]], o, mine))
+            else:
+                lo, hi = spec[1]
+
+                def store(value, o=o):
+                    o[...] = value.astype(BF)
+
+                out.append(
+                    LineReduce(place, lambda t, a=a, lo=lo, hi=hi: a[t, lo:hi], store, mine)
                 )
-            )
-    return out
-
-
-def rider_shapes(dims, specs, arrays):
-    out = []
-    for spec, a in zip(specs, arrays):
-        if spec[0] == "gather":
-            shape = a.shape if spec[1] is None else a.shape[1:]
-            out.append(jax.ShapeDtypeStruct((dims[1],) + shape, a.dtype))
-        else:
-            lo, hi = spec[1]
-            out.append(jax.ShapeDtypeStruct((a.shape[0], hi - lo) + a.shape[2:], a.dtype))
-    return out
+        return (out, scratch)
+
+
+def each(riders, what):
+    for r in riders:
+        getattr(r, what)()
 
 
 def scatter_scratch(dims, *block):
@@ -509,8 +649,10 @@
         gathers[d].start()
         for step in range(1, min(6, pc.count)):
             gathers[d - 1].before(step)
+    line.service()
     for step in range(1, min(6, pc.count)):
         gathers[nb - 1].before(step)
+    line.service()
     for step in range(min(6, pc.count), pc.count):
         for g in gathers:
             g.before(step)
@@ -557,7 +699,7 @@
             dma((2 * (ns - 1),)),
             dma((2 * (ns - 1),)),
         ]
-        + line_sems(dims),
+        + gather_scratch(dims),
         (w, wd, qo, small),
     )
 
@@ -622,10 +764,10 @@
 
 
 def attention_forward_kernel(
-    dims, nk, layer, specs, carry, h_ref, small_ref, meta_ref, docs_ref, cos_ref, sin_ref, qo_all,
+    dims, nk, layer, plan, carry, h_ref, small_ref, meta_ref, docs_ref, cos_ref, sin_ref, qo_all,
     *refs
 ):
-    n = len(specs)
+    n = plan.count
     if carry:
         block_ref, refs = (refs[0], refs[1:])
     ins, refs = (refs[:n], refs[n:])
@@ -639,10 +781,10 @@
     width, rows = h_ref.shape
     loads = load_qo(qo_all, layer, w, wo, qsem)
     greet(pc, "mates" if carry else None, True)
-    riders = riders_of(pc, specs, ins, outs, refs[: 3 * n])
+    riders, refs = plan.board(pc, ins, outs, refs)
     gather = None
     if carry:
-        gather = PlaneGather(pc, lambda q: block_all.at[:, lanes(q, rows)], *refs[3 * n :])
+        gather = PlaneGather(pc, lambda q: block_all.at[:, lanes(q, rows)], *refs)
         block_all[:, lanes(pc.me, rows)] = block_ref[...]
         gather.start()
     g1, g2, bias = gains_of(padded_t(small_ref[layer]), width, w.shape[1])
@@ -680,8 +822,7 @@
         q_ref[head, half:, :] = (r2 * scale).astype(BF)
     for c in sends:
         c.wait()
-    for r in riders:
-        r.start()
+    each(riders, "start")
     for g in range(KVH):
         keys = [kv_ref[j, g].T for j in range(nk)]
         values = [kv_ref[j, KVH + g] for j in range(nk)]
@@ -705,6 +846,7 @@
             return carried
 
         lax.fori_loop(0, GROUP, one_head, 0)
+        each(riders, "service")
         if carry and g == 0:
             for step in range(1, min(6, pc.count)):
                 gather.before(step)
@@ -717,12 +859,11 @@
         for step in range(min(6, pc.count), pc.count):
             gather.before(step)
         gather.finish()
-    for r in riders:
-        r.finish()
+    each(riders, "finish")
 
 
 def attention_forward(dims, nk, cid, layer, hidden, small, meta, docs, cos_part, sin_part, qo_all,
-                      specs, riders, block=None):
+                      plan, block=None):
     width, rows = hidden.shape
     count = dims[0] * dims[2]
     carry = block is not None
@@ -736,18 +877,17 @@
         sds((H, HD, rows), BF),
         sds((width, rows), F32),
         sds((width, rows), BF),
-    ] + rider_shapes(dims, specs, riders)
+    ] + plan.shapes
     dma = pltpu.SemaphoreType.DMA
-    n = len(specs)
     if carry:
         outs.append(sds((width, count * rows), BF))
     out = call(
-        functools.partial(attention_forward_kernel, dims, nk, layer, specs, carry),
+        functools.partial(attention_forward_kernel, dims, nk, layer, plan, carry),
         "attention_forward",
         cid,
         tuple(outs),
-        [VM] * 7 + [AN] * n + [VM] * carry,
-        [VM] * 6 + [AN] + [VM] * carry + [AN] * n,
+        [VM] * 7 + plan.places + [VM] * carry,
+        [VM] * 6 + [AN] + [VM] * carry + plan.places,
         [
             pltpu.VMEM((width, qkv), BF),
             pltpu.VMEM((width, width), BF),
@@ -757,18 +897,18 @@
             dma((nk - 1,)),
             dma((2,)),
         ]
-        + line_sems(dims) * n
+        + plan.scratch
         + [dma((count - 1,))] * (2 * carry),
-        (hidden, small, meta, docs, cos_part, sin_part, qo_all, *([block] * carry), *riders),
+        (hidden, small, meta, docs, cos_part, sin_part, qo_all, *([block] * carry), *plan.arrays),
     )
     return (out[:7], out[7:])
 
 
 def attention_backward_kernel(
-    dims, nk, layer, specs, carry, g_ref, small_ref, meta_ref, docs_ref, cos_ref, sin_ref,
+    dims, nk, layer, plan, carry, g_ref, small_ref, meta_ref, docs_ref, cos_ref, sin_ref,
     h_ref, normed_ref, q_ref, kv_ref, lse_ref, mixed_ref, qo_all, *refs
 ):
-    n = len(specs)
+    n = plan.count
     if carry:
         parts_ref, res_ref, refs = (refs[0], refs[1], refs[2:])
     ins, refs = (refs[:n], refs[n:])
@@ -783,13 +923,12 @@
     qkv = w.shape[1]
     loads = load_qo(qo_all, layer, w, wo, qsem)
     greet(pc, "mates" if carry else None, True)
-    riders = riders_of(pc, specs, ins, outs, refs[: 3 * n])
+    riders, refs = plan.board(pc, ins, outs, refs)
     scatter = None
     if carry:
-        scatter = ReadyScatter(pc, parts_ref, *refs[3 * n :])
+        scatter = ReadyScatter(pc, parts_ref, *refs)
         scatter.start()
-    for r in riders:
-        r.start()
+    each(riders, "start")
     g1 = column(padded_t(small_ref[layer]), 0, width // 128)
     fill_masks(pc, mask, padded_t(meta_ref[...]), docs_ref[...])
     grl = g_ref[...].astype(BF)
@@ -836,6 +975,7 @@
             return carried
 
         lax.fori_loop(0, GROUP, one_head, 0)
+        each(riders, "service")
         if carry and g == 0:
             scatter.late()
     for j in range(1, nk):
@@ -877,12 +1017,11 @@
             out_ref[...] = res_ref[...] + total
 
         scatter.finish(store)
-    for r in riders:
-        r.finish()
+    each(riders, "finish")
 
 
 def attention_backward(dims, nk, cid, layer, g, small, meta, docs, cos_part, sin_part, hidden,
-                       normed, q, kv, lse, mixed, qo_all, specs, riders, late=()):
+                       normed, q, kv, lse, mixed, qo_all, plan, late=()):
     width, rows = hidden.shape
     carry = len(late) > 0
     qkv = qo_all.shape[2] - width
@@ -891,19 +1030,18 @@
         sds((width, rows), F32),
         sds((width, qkv + width), BF),
         sds(((width + qkv) // 128, 128), F32),
-    ] + rider_shapes(dims, specs, riders)
+    ] + plan.shapes
     dma = pltpu.SemaphoreType.DMA
     block = (2 * KVH, HD, rows)
-    n = len(specs)
     if carry:
         outs.append(sds((width, rows), F32))
     out = call(
-        functools.partial(attention_backward_kernel, dims, nk, layer, specs, carry),
+        functools.partial(attention_backward_kernel, dims, nk, layer, plan, carry),
         "attention_backward",
         cid,
         tuple(outs),
-        [VM] * 3 + [AN] * n + [VM] * carry,
-        [VM] * 12 + [AN] + [VM] * len(late) + [AN] * n,
+        [VM] * 3 + plan.places + [VM] * carry,
+        [VM] * 12 + [AN] + [VM] * len(late) + plan.places,
         [
             pltpu.VMEM((width, qkv), BF),
             pltpu.VMEM((width, width), BF),
@@ -917,10 +1055,10 @@
             dma((nk - 1,)),
             dma((2,)),
         ]
-        + line_sems(dims) * n
+        + plan.scratch
         + (scatter_scratch(dims, width, rows)[2:] if carry else []),
         (g, small, meta, docs, cos_part, sin_part, hidden, normed, q, kv, lse, mixed, qo_all,
-         *late, *riders),
+         *late, *plan.arrays),
     )
     return (out[:3], out[3:])
 
@@ -940,8 +1078,8 @@
         dst[c0:c1, :] = src[:, c0:c1].T
 
 
-def feed_forward_kernel(dims, specs, x_ref, res_ref, wgu_ref, wd_ref, *refs):
-    n = len(specs)
+def feed_forward_kernel(dims, plan, x_ref, res_ref, wgu_ref, wd_ref, *refs):
+    n = plan.count
     ins, refs = (refs[:n], refs[n:])
     out_ref, x_all, gu_all = refs[:3]
     outs, refs = (refs[3 : 3 + n], refs[3 + n :])
@@ -950,13 +1088,12 @@
     width, rows = x_ref.shape
     ff = wd_ref.shape[0]
     greet(pc, "mates", n > 0)
-    riders = riders_of(pc, specs, ins, outs, refs[12:])
+    riders, _ = plan.board(pc, ins, outs, refs[12:])
     gather = PlaneGather(pc, lambda q: x_all.at[:, lanes(q, rows)], gs, gr)
     scatter = PlaneScatter(pc, near, away, back, hop, ss, sr)
     x_all[:, lanes(pc.me, rows)] = x_ref[...]
     gather.start()
-    for r in riders:
-        r.start()
+    each(riders, "start")
     transpose_into(wgu_t, wgu_ref)
     transpose_into(wd_t, wd_ref)
     neighbours, last = steps_of(pc.count)
@@ -984,6 +1121,10 @@
         lax.fori_loop(0, ff // chunk, act, 0)
         scatter.put(step, nn(wd_t[...], inner[...]))
 
+        @pl.when(step == 3)
+        def _():
+            each(riders, "service")
+
         @pl.when(step == neighbours)
         def _():
             scatter.early()
@@ -992,35 +1133,34 @@
 
     lax.fori_loop(0, pc.count, step_body, 0)
     scatter.diagonal()
+    each(riders, "service")
 
     def store(total):
         out_ref[...] = res_ref[...] + total
 
     scatter.result(store)
     gather.finish()
-    for r in riders:
-        r.finish()
-
-
-def feed_forward(dims, cid, x, residual, wgu, wd, specs, riders):
+    each(riders, "finish")
+
+
+def feed_forward(dims, cid, x, residual, wgu, wd, plan):
     width, rows = x.shape
     count = dims[0] * dims[2]
     two_ff, ff = (wgu.shape[1], wd.shape[0])
     sds = jax.ShapeDtypeStruct
     dma = pltpu.SemaphoreType.DMA
-    n = len(specs)
     out = call(
-        functools.partial(feed_forward_kernel, dims, specs),
+        functools.partial(feed_forward_kernel, dims, plan),
         "feed_forward",
         cid,
         (
             sds((width, rows), F32),
             sds((width, count * rows), BF),
             sds((two_ff, count * rows), BF),
-            *rider_shapes(dims, specs, riders),
+            *plan.shapes,
         ),
-        [VM] * 3 + [AN] * n,
-        [VM] * 4 + [AN] * n,
+        [VM] * 3 + plan.places,
+        [VM] * 4 + plan.places,
         [
             pltpu.VMEM((two_ff, width), BF),
             pltpu.VMEM((width, ff), BF),
@@ -1029,16 +1169,16 @@
         ]
         + scatter_scratch(dims, width, rows)
         + [dma((count - 1,)), dma((count - 1,))]
-        + line_sems(dims) * n,
-        (x, residual, wgu, wd, *riders),
+        + plan.scratch,
+        (x, residual, wgu, wd, *plan.arrays),
     )
     return (out[:3], out[3:])
 
 
 def feed_backward_kernel(
-    dims, layer, specs, g_ref, res_ref, x_all, gu_all, wgu_ref, wd_ref, small_ref, *refs
+    dims, layer, plan, g_ref, res_ref, x_all, gu_all, wgu_ref, wd_ref, small_ref, *refs
 ):
-    n = len(specs)
+    n = plan.count
     ins, refs = (refs[:n], refs[n:])
     gr_ref, dwgu_ref, dwd_ref, dsmall_ref = refs[:4]
     outs, refs = (refs[4 : 4 + n], refs[4 + n :])
@@ -1047,13 +1187,12 @@
     width, rows = g_ref.shape
     ff = wd_ref.shape[0]
     greet(pc, "mates", n > 0)
-    riders = riders_of(pc, specs, ins, outs, refs[12:])
+    riders, _ = plan.board(pc, ins, outs, refs[12:])
     gather = PlaneGather(pc, lambda q: g_all.at[:, lanes(q, rows)], gs, gr)
     scatter = PlaneScatter(pc, near, away, back, hop, ss, sr)
     g_all[:, lanes(pc.me, rows)] = g_ref[...].astype(BF)
     gather.start()
-    for r in riders:
-        r.start()
+    each(riders, "start")
     neighbours, last = steps_of(pc.count)
     chunk = 32 if ff % 32 == 0 else 16
 
@@ -1082,6 +1221,10 @@
         lax.fori_loop(0, ff // chunk, act, 0)
         scatter.put(step, nn(wgu_ref[...], ggu[:, sl]))
 
+        @pl.when(step == 3)
+        def _():
+            each(riders, "service")
+
         @pl.when(step == neighbours)
         def _():
             scatter.early()
@@ -1090,6 +1233,7 @@
 
     lax.fori_loop(0, pc.count, step_body, 0)
     scatter.diagonal()
+    each(riders, "service")
     dwd_ref[...] = nt(inner[...], g_all[...]).astype(BF)
     scatter.late()
     part = width // 2
@@ -1111,19 +1255,17 @@
 
     scatter.finish(store)
     gather.finish()
-    for r in riders:
-        r.finish()
-
-
-def feed_backward(dims, cid, layer, g, residual, x_all, gu_all, wgu, wd, small, specs, riders):
+    each(riders, "finish")
+
+
+def feed_backward(dims, cid, layer, g, residual, x_all, gu_all, wgu, wd, small, plan):
     width, rows = g.shape
     count = dims[0] * dims[2]
     two_ff, ff = (wgu.shape[1], wd.shape[0])
     sds = jax.ShapeDtypeStruct
     dma = pltpu.SemaphoreType.DMA
-    n = len(specs)
     out = call(
-        functools.partial(feed_backward_kernel, dims, layer, specs),
+        functools.partial(feed_backward_kernel, dims, layer, plan),
         "feed_backward",
         cid,
         (
@@ -1131,10 +1273,10 @@
             sds(wgu.shape, BF),
             sds(wd.shape, BF),
             sds((width // 128, 128), F32),
-            *rider_shapes(dims, specs, riders),
+            *plan.shapes,
         ),
-        [VM] * 4 + [AN] * n,
-        [VM] * 7 + [AN] * n,
+        [VM] * 4 + plan.places,
+        [VM] * 7 + plan.places,
         [
             pltpu.VMEM((width, count * rows), BF),
             pltpu.VMEM((ff, count * rows), BF),
@@ -1143,8 +1285,8 @@
         ]
         + scatter_scratch(dims, width, rows)
         + [dma((count - 1,)), dma((count - 1,))]
-        + line_sems(dims) * n,
-        (g, residual, x_all, gu_all, wgu, wd, small, *riders),
+        + plan.scratch,
+        (g, residual, x_all, gu_all, wgu, wd, small, *plan.arrays),
     )
     return (out[:4], out[4:])
 
@@ -1265,22 +1407,21 @@
 def reduce_kernel(
     dims, cut, qo0, qo1, sa0, sa1, sb0, sb1, gu1, wd1, wd0, gu0a, gu0,
     qo_out, small_out, gu_got, wd_got,
-    buf1, bufa, buf0, bufw, gsum, wsum, small, sm_in, sm_mid, sm_line, z_out, z_in, half_sum,
-    lsem, ps, pr, gs, gr, ws, wr, ls, lr, zs, zr, near, away, back, hop, ss, sr, *rest
+    gsum, small, sm_in, sm_mid, sm_line, z_out,
+    lsem, ps, pr, ws, wr, ls, lr, zs, zr, *rest
 ):
     pc = Place(dims)
     ns, nb, nf = dims
+    line_qo = rest[:4]
+    line_gu = rest[4:8]
+    near, away, back, hop, ss, sr = rest[8:]
     greet(pc, "all", True)
-    line = LineExchange(pc, lambda t: gu0.at[t, cut:nf], lambda t: buf0.at[t], rest)
+
+    def keep(value):
+        gsum[...] = value.astype(BF)
+
+    line = LineReduce(pc, lambda t: gu0[t, cut:nf], keep, line_gu)
     line.start()
-    loads = [
-        pltpu.make_async_copy(gu1, buf1, lsem.at[0]),
-        pltpu.make_async_copy(gu0a, bufa, lsem.at[1]),
-        pltpu.make_async_copy(wd0, bufw.at[0], lsem.at[2]),
-        pltpu.make_async_copy(wd1, bufw.at[1], lsem.at[3]),
-    ]
-    for c in loads:
-        c.start()
     n1 = sb0.shape[0]
     per = small.shape[0] // ns
     nr = sa0.shape[0] + n1
@@ -1293,8 +1434,6 @@
         remote(small, sm_in.at[e - 1], ls.at[e - 1], lr.at[e - 1], pc.plane(e))
         for e in range(1, pc.count)
     ]
-    for c in smalls:
-        c.start()
     scatter = PlaneScatter(pc, near, away, back, hop, ss, sr)
     if pc.two_level:
         order = pc.slots()
@@ -1318,92 +1457,72 @@
 
     lax.fori_loop(0, pc.count, step_body, 0)
     scatter.diagonal()
-
-    def send_rows(l, f):
+    for c in smalls:
+        c.start()
+
+    def send_rows(l, f, src):
         e = (l * nf + f - pc.me + pc.count) % pc.count
 
         @pl.when(e != 0)
         def _():
-            remote(
-                gsum.at[l, f], gu_got.at[pc.me], ps.at[e - 1], pr.at[e - 1], (l, pc.b, f)
-            ).start()
+            remote(src, gu_got.at[pc.me], ps.at[e - 1], pr.at[e - 1], (l, pc.b, f)).start()
 
         @pl.when(e == 0)
         def _():
-            pltpu.make_async_copy(gsum.at[l, f], gu_got.at[pc.me], lsem.at[4]).start()
-
-    def total_of(buf):
-        total = buf[0].astype(F32)
-        for t in range(1, nb):
-            total = total + buf[t].astype(F32)
-        return total.astype(BF)
-
-    loads[0].wait()
+            pltpu.make_async_copy(src, gu_got.at[pc.me], lsem.at[0]).start()
+
+    line.service()
     for f in range(nf):
-        gsum[1, f] = total_of(buf1.at[:, f])
-        send_rows(1, f)
-    loads[2].wait()
-    loads[3].wait()
-    wsum[0] = total_of(bufw.at[0])
-    wsum[1] = total_of(bufw.at[1])
-    own = pltpu.make_async_copy(wsum.at[pc.s], wd_got.at[pc.s], lsem.at[5])
-    own.start()
-    across = []
-    for d in range(1, ns):
-        y = (pc.s + d) % ns
-        across.append(
-            remote(wsum.at[y], wd_got.at[pc.s], ws.at[d - 1], wr.at[d - 1], (y, pc.b, pc.f))
-        )
-        across[-1].start()
-    loads[1].wait()
+        send_rows(1, f, gu1.at[f])
     for f in range(cut):
-        gsum[0, f] = total_of(bufa.at[:, f])
-        send_rows(0, f)
+        send_rows(0, f, gu0a.at[f])
+    for l, ref in ((0, wd0), (1, wd1)):
+        @pl.when(pc.s == l)
+        def _():
+            pltpu.make_async_copy(ref, wd_got.at[l], lsem.at[1]).start()
+
+        @pl.when(pc.s != l)
+        def _():
+            remote(ref, wd_got.at[pc.s], ws.at[0], wr.at[0], (l, pc.b, pc.f)).start()
+
+    scatter.late()
     total = small[...]
     for e, c in enumerate(smalls):
         c.wait()
         total = total + sm_in[e]
     sm_mid[...] = total
-    m = nb - 1
     lines = [
-        remote(sm_mid, sm_line.at[d - 1], zs.at[m + d - 1], zr.at[m + d - 1], pc.along(d))
+        remote(sm_mid, sm_line.at[d - 1], zs.at[d - 1], zr.at[d - 1], pc.along(d))
         for d in range(1, nb)
     ]
     for c in lines:
         c.start()
+    line.service()
 
     def store(value):
-        half_sum[...] = value
-
-    scatter.result(store)
-    z_out[...] = half_sum[...].astype(BF)
-    sends = []
-    for d in range(1, nb):
-        t = pc.along(d)
-        sends.append(remote(z_out.at[t[1]], z_in.at[d - 1], zs.at[d - 1], zr.at[d - 1], t))
-    for c in sends:
-        c.start()
+        z_out[...] = value.astype(BF)
+
+    scatter.finish(store)
+
+    def leave(value):
+        qo_out[...] = value
+
+    ends = LineReduce(pc, lambda t: z_out[t], leave, line_qo)
+    ends.start()
     line.finish()
     for f in range(cut, nf):
-        gsum[0, f] = total_of(buf0.at[:, f - cut])
-        send_rows(0, f)
-    mine = z_out[pc.b].astype(F32)
-    for d, c in enumerate(sends):
-        c.wait()
-        mine = mine + z_in[d].astype(F32)
-    qo_out[...] = mine
+        send_rows(0, f, gsum.at[f - cut])
     total = sm_mid[...]
     for d, c in enumerate(lines):
         c.wait()
         total = total + sm_line[d]
     small_out[...] = total
+    ends.finish()
     for k in range(pc.count - 1):
-        c = remote(gsum.at[0, 0], gu_got.at[pc.me], ps.at[k], pr.at[k], pc.plane(1))
-        c.wait()
-    pltpu.make_async_copy(gsum.at[0, 0], gu_got.at[pc.me], lsem.at[4]).wait()
-    own.wait()
-    for c in across:
-        c.wait()
+        remote(gsum.at[0], gu_got.at[pc.me], ps.at[k], pr.at[k], pc.plane(1)).wait()
+    pltpu.make_async_copy(gsum.at[0], gu_got.at[pc.me], lsem.at[0]).wait()
+    pltpu.make_async_copy(wd0, wd_got.at[pc.s], lsem.at[1]).wait()
+    remote(wd0, wd_got.at[pc.s], ws.at[0], wr.at[0], pc.plane(1)).wait()
 
 
 def reduce_gradients(dims, cid, cut, qo0, qo1, smalls, gu1, wd1, wd0, gu0a, gu0):
@@ -1411,7 +1530,7 @@
     count = ns * nf
     dr, cols = qo0.shape[2:]
     two_ff = gu0.shape[3]
-    half, width = wd0.shape[1:]
+    half, width = wd0.shape
     rows = smalls[0].shape[0] + smalls[2].shape[0]
     small = (ns * (-(-rows // 8) * 8), 128)
     sds = jax.ShapeDtypeStruct
@@ -1427,35 +1546,27 @@
             sds((ns, half, width), BF),
         ),
         [VM] * 4,
-        [VM] * 6 + [AN] * 5,
+        [VM] * 11,
         [
-            pltpu.VMEM((nb, nf, dr, two_ff), BF),
-            pltpu.VMEM((nb, cut, dr, two_ff), BF),
-            pltpu.VMEM((nb, nf - cut, dr, two_ff), BF),
-            pltpu.VMEM((ns, nb, half, width), BF),
-            pltpu.VMEM((ns, nf, dr, two_ff), BF),
-            pltpu.VMEM((ns, half, width), BF),
+            pltpu.VMEM((nf - cut, dr, two_ff), BF),
             pltpu.VMEM(small, F32),
             pltpu.VMEM((count - 1,) + small, F32),
             pltpu.VMEM(small, F32),
             pltpu.VMEM((nb - 1,) + small, F32),
             pltpu.VMEM((nb, dr, cols), BF),
-            pltpu.VMEM((nb - 1, dr, cols), BF),
-            pltpu.VMEM((nb, dr, cols), F32),
-            dma((6,)),
+            dma((2,)),
             dma((count - 1,)),
             dma((count - 1,)),
-            dma((1,)),
-            dma((1,)),
             dma((ns - 1,)),
             dma((ns - 1,)),
             dma((count - 1,)),
             dma((count - 1,)),
-            dma((2 * (nb - 1),)),
-            dma((2 * (nb - 1),)),
+            dma((nb - 1,)),
+            dma((nb - 1,)),
         ]
-        + scatter_scratch(dims, nb, dr, cols)
-        + line_sems(dims),
+        + reduce_scratch(dims, dr, cols)
+        + reduce_scratch(dims, nf - cut, dr, two_ff)
+        + scatter_scratch(dims, nb, dr, cols),
         (qo0, qo1, *smalls, gu1, wd1, wd0, gu0a, gu0),
     )
 
@@ -1575,33 +1686,36 @@
     wide = (width, 2 * ff)
 
     common = (small_all, meta, query_docs, cos_part, sin_part, qo_all)
-    a0, (wd0,) = attention_forward(dims, nk, 1, 0, hidden, *common, (("gather", 0),), (wdp,))
+    def ride(*pairs):
+        return Riders(dims, tuple(a for a, _ in pairs), tuple(v for _, v in pairs))
+
+    a0, (wd0,) = attention_forward(dims, nk, 1, 0, hidden, *common, ride((("gather", 0), wdp)))
     wd0 = wd0.reshape(ff, width)
     wgu0 = gu_first.reshape(wide)
-    f0, (gu1,) = feed_forward(dims, 3, a0[6], a0[5], wgu0, wd0, (("gather", 1),), (gup,))
+    f0, (gu1,) = feed_forward(dims, 3, a0[6], a0[5], wgu0, wd0, ride((("gather", 1), gup)))
     wgu1 = gu1.reshape(wide)
     a1, (wd1, g_all) = attention_forward(
-        dims, nk, 2, 1, f0[0], *common, (("gather", 1),), (wdp,), cot.T
+        dims, nk, 2, 1, f0[0], *common, ride((("gather", 1), wdp)), cot.T
     )
     wd1 = wd1.reshape(ff, width)
 
     line_gu = (nb, nf, dr, 2 * ff)
     line_wd = (nb, half, width)
     everything = (0, half)
-    cut = max(1, nf // 4)
+    cut = nf // 2
     b1 = feed_both(dims, 4, 1, a1[6], a1[5], g, g_all, wgu1, wd1, small_all)
     ab1, (dwd1, out1) = attention_backward(
         dims, nk, 7, 1, b1[0], *common[:5], f0[0], *a1[:5], qo_all,
-        (("exchange", everything),), (b1[2].reshape(line_wd),), (b1[4], a1[5]),
+        ride((("reduce", everything), b1[2].reshape(line_wd))), (b1[4], a1[5]),
     )
     b0, (dgu1,) = feed_backward(
         dims, 6, 0, ab1[0], a0[5], f0[1], f0[2], wgu0, wd0, small_all,
-        (("exchange", (0, nf)),), (b1[1].reshape(line_gu),),
+        ride((("reduce", (0, nf)), b1[1].reshape(line_gu))),
     )
     dgu0 = b0[1].reshape(line_gu)
     ab0, (dwd0, dgu0a) = attention_backward(
         dims, nk, 8, 0, b0[0], *common[:5], hidden, *a0[:5], qo_all,
-        (("exchange", everything), ("exchange", (0, cut))), (b0[2].reshape(line_wd), dgu0),
+        ride((("reduce", everything), b0[2].reshape(line_wd)), (("reduce", (0, cut)), dgu0)),
     )
 
     def swapped(values):

time: 547 us -> 539 us (0.985)
  the two profiles are of different devices: /device:TPU:12 before, /device:TPU:0 now
where the time goes in v4:
time: 539 us; the launch traced here: 528 us
  Pallas kernels  511 us (95%)
  other arithmetic  9.71 us (2%)
    pallas_call x9, Pallas kernels, call(): pl.pallas_call(kernel, name=name, out_shape=outs, in_specs=in_specs, out_...  503 us
  transfers between devices with their start and end apart: 2, of which 0 were waited for; matrix products, arithmetic and copies ran while one was open for 0% of the time, Pallas kernels for 35%

profile of v4, /device:TPU:0, one launch (start us, length us, event | category | flops | bytes accessed | tf_op | source)
XLA Modules:
  0.0 528.1 jit_solution(14762814242233246106)
XLA Ops:
  0.8 0.1 broadcast_in_dim.17
  0.9 0.7 fusion.1
  1.6 0.7 convert_reduce_fusion
  2.3 0.6 gather_fusion
  2.9 0.6 constant_dynamic-slice_fusion.2.docs_ref
  3.4 0.7 reduce
  4.1 0.7 reduce.1
  4.8 0.7 reduce.2
  5.5 1.2 constant_dynamic-slice_fusion
  6.8 0.2 copy.21
  7.0 0.2 copy.22
  7.3 1.0 convert_bitcast_fusion.h_ref
  8.2 1.0 bitcast_convert_fusion.g_ref
  9.2 0.7 broadcast_select_fusion.meta_ref
  9.9 0.8 multiply_sine_fusion
  10.7 0.7 pad_maximum_fusion.qo
  11.4 0.6 fusion.small
  12.0 75.9 %gather_weights.1 = (bf16[2,4,56,1216]{3,2,1,0:T(8,128)(2,1)}, bf16[2,152,896]{2,1,0:T(8,128)(2,1)}, bf16[4,4,56,1216]{3,2,1,0:T(8,128)(2,1)}, bf16[2,4,4,56,2048]{4,3,2,1,0:T(8,128)(2,1)}, f32[2,24,128]{2,1,0:T(8,128)}) custom-call(bf16[1,56,9728]{2,1,0:T(8,128)(2,1)} %w_ref.1, bf16[2,152,896]{2,1,0:T(8,128)(2,1)} %bitcast.46, ...), custom_call_target="tpu_custom_call" | custom-call | tf_op jit(solution)/shard_map/gather_weights/pallas_call | solution.py:565
  87.9 36.5 %attention_forward.2 = (bf16[896,256]{1,0:T(8,128)(2,1)}, bf16[14,64,256]{2,1,0:T(8,128)(2,1)}, bf16[3,4,64,256]{3,2,1,0:T(8,128)(2,1)}, f32[14,1,256]{2,1,0:T(1...) custom-call(f32[896,256]{1,0:T(8,128)} %convert_bitcast_fusion.h_ref, ...), custom_call_target="tpu_custom_call" | custom-call | tf_op jit(solution)/shard_map/attention_forward/pallas_call | solution.py:565
  124.4 52.7 %feed_forward.1 = (f32[896,256]{1,0:T(8,128)}, bf16[896,2048]{1,0:T(8,128)(2,1)}, bf16[1216,2048]{1,0:T(8,128)(2,1)}, bf16[4,4,56,1216]{3,2,1,0:T(8,128)(2,1)}) custom-call(bf16[896,256]{1,0:T(8,128)(2,1)} %get-tuple-element.62.x_ref, f32[896,256]{1,0:T(8,128)} %get-tuple-element.63.res_ref, bf16[896,1216]{1,0:T(8,128)(2,1)} %bitcast.34, ...), custom_call_target="tpu_custom_call" | custom-call | tf_op jit(solution)/shard_map/feed_forward/pallas_call | solution.py:565
  177.2 40.0 %attention_forward.3 = (bf16[896,256]{1,0:T(8,128)(2,1)}, bf16[14,64,256]{2,1,0:T(8,128)(2,1)}, bf16[3,4,64,256]{3,2,1,0:T(8,128)(2,1)}, f32[14,1,256]{2,1,0:T(1...) custom-call(f32[896,256]{1,0:T(8,128)} %get-tuple-element.67.h_ref.o, ...), custom_call_target="tpu_custom_call" | custom-call | tf_op jit(solution)/shard_map/attention_forward/pallas_call | solution.py:565
  217.1 63.1 %feed_both.1 = (f32[896,256]{1,0:T(8,128)}, bf16[896,1216]{1,0:T(8,128)(2,1)}, bf16[608,896]{1,0:T(8,128)(2,1)}, f32[7,128]{1,0:T(8,128)}, bf16[8,896,256]{2,1,0:T(8,128)(2,1)}) custom-call(bf16[896,256]{1,0:T(8,128)(2,1)} %get-tuple-element.68.x_ref, f32[896,256]{1,0:T(8,128)} %get-tuple-element.69.res_ref.refs_1_, f32[896,256]{1,0:T(8,128)} %bitcast_convert_fusion.g_ref, ...), custom_call_target="tpu_custom_call" | custom-call | tf_op jit(solution)/shard_map/feed_both/pallas_call | solution.py:565
  280.3 48.7 %attention_backward.2 = (f32[896,256]{1,0:T(8,128)}, bf16[896,2048]{1,0:T(8,128)(2,1)}, f32[16,128]{1,0:T(8,128)}, bf16[152,896]{1,0:T(8,128)(2,1)}, f32[896,256]{1,0:T(8,128)}) custom-call(f32[896,256]{1,0:T(8,128)} %get-tuple-element.73.g_ref, f32[2,24,128]{2,1,0:T(8,128)} %get-tuple-element.59.small_ref, f32[6,128]{1,0:T(8,128)} %broadcast_select_fusion.meta_ref, ...), custom_call_target="tpu_custom_call" | custom-call | tf_op jit(solution)/shard_map/attention_backward/pallas_call | solution.py:565
  329.0 1.3 select_convert_fusion.1
  330.4 58.1 %feed_backward.1 = (f32[896,256]{1,0:T(8,128)}, bf16[896,1216]{1,0:T(8,128)(2,1)}, bf16[608,896]{1,0:T(8,128)(2,1)}, f32[7,128]{1,0:T(8,128)}, bf16[4,56,1216]{2,1,0:T(8,128)(2,1)}) custom-call(f32[896,256]{1,0:T(8,128)} %get-tuple-element.81.g_ref.gh1, f32[896,256]{1,0:T(8,128)} %get-tuple-element.63.res_ref, bf16[896,2048]{1,0:T(8,128)(2,1)} %get-tuple-element.82.x_all, ...), custom_call_target="tpu_custom_call" | custom-call | tf_op jit(solution)/shard_map/feed_backward/pallas_call | solution.py:565
  388.5 50.2 %attention_backward.3 = (f32[896,256]{1,0:T(8,128)}, bf16[896,2048]{1,0:T(8,128)(2,1)}, f32[16,128]{1,0:T(8,128)}, bf16[152,896]{1,0:T(8,128)(2,1)}, bf16[2,56,1216]{2,1,0:T(8,128)(2,1)}) custom-call(f32[896,256]{1,0:T(8,128)} %get-tuple-element.85.g_ref, f32[2,24,128]{2,1,0:T(8,128)} %get-tuple-element.59.small_ref, ...), custom_call_target="tpu_custom_call" | custom-call | tf_op jit(solution)/shard_map/attention_backward/pallas_call | solution.py:565
  438.7 0.1 select_convert_fusion
  438.8 2.4 collective-permute-start.1
  441.2 78.3 %reduce_gradients.1 = (f32[56,2048]{1,0:T(8,128)}, f32[48,128]{1,0:T(8,128)}, bf16[8,56,1216]{2,1,0:T(8,128)(2,1)}, bf16[2,152,896]{2,1,0:T(8,128)(2,1)}) custom-call(bf16[4,4,56,2048]{3,2,1,0:T(8,128)(2,1)} %bitcast.40, bf16[4,4,56,2048]{3,2,1,0:T(8,128)(2,1)} %bitcast.39, f32[16,128]{1,0:T(8,128)} %get-tuple-element.95.sa0, ...), custom_call_target="tpu_custom_call" | custom-call | tf_op jit(solution)/shard_map/reduce_gradients/pallas_call | solution.py:565
  519.5 0.7 copy-done.3
  520.3 0.2 copy-done.4
  520.4 7.4 %lay_out.1 = (f32[1,2,256,896]{3,2,1,0:T(8,128)}, f32[1,2,256,896]{3,2,1,0:T(8,128)}, f32[1,896]{1,0:T(1,128)}, f32[1,56,1152]{2,1,0:T(8,128)}, f32[1,1152]{1,0:...) custom-call(bf16[8,56,1216]{2,1,0:T(8,128)(2,1)} %get-tuple-element.103.gu, ...), custom_call_target="tpu_custom_call" | custom-call | tf_op jit(solution)/shard_map/lay_out/pallas_call | solution.py:1620
  (22 shorter events, 0.2 us)
Async XLA Ops:
  6.8 3.9 copy-start.5
  6.8 3.9 copy-start.6
  7.0 80.9 %copy-start.2 = (bf16[1,256,896]{1,2,0:T(8,128)(2,1)}, bf16[1,256,896]{1,2,0:T(8,128)(2,1)S(1)}, u32[]{:S(2)}) copy-start(bf16[1,256,896]{1,2,0:T(8,128)(2,1)S(1)} %copy.21) | copy-start | bytes 1376260
  280.3 48.7 %copy-start = (f32[896,256]{1,0:T(8,128)S(1)}, f32[896,256]{1,0:T(8,128)}, u32[]{:S(2)}) copy-start(f32[896,256]{1,0:T(8,128)} %get-tuple-element.67.h_ref.out0) | copy-start | bytes 2752516
  330.3 189.2 %collective-permute-start = (bf16[896,256]{1,0:T(8,128)(2,1)S(1)}, bf16[896,256]{1,0:T(8,128)(2,1)S(1)}, u32[]{:S(2)}, u32[]{:S(2)}) collective-permute-start(bf16[896,256]{1,0:T(8,128)(2,1)S(1)} %select_convert_fusion.1), channel_id=1, source_target_pairs={{0,16},{16,0},{1,17},{17,1},{2,18},{18,2},{3,19},{19,3},{4,20},{20... | collective-permute-start | bytes 1376264 | tf_op jit(solution)/shard_map/ppermute | solution.py:1723
  388.5 50.2 %copy-start.1 = (f32[896,256]{1,0:T(8,128)S(1)}, f32[896,256]{1,0:T(8,128)}, u32[]{:S(2)}) copy-start(f32[896,256]{1,0:T(8,128)} %get-tuple-element.81.g_ref.gh1) | copy-start | bytes 2752516
  438.8 80.7 %collective-permute-start.1 = (bf16[896,256]{1,0:T(8,128)(2,1)S(1)}, bf16[896,256]{1,0:T(8,128)(2,1)S(1)}, u32[]{:S(2)}, u32[]{:S(2)}) collective-permute-start(bf16[896,256]{1,0:T(8,128)(2,1)S(1)} %select_convert_fusion), channel_id=1, source_target_pairs={{0,16},{16,0},{1,17},{17,1},{2,18},{18,2},{3,19},{19,3},{4,20},{20... | collective-permute-start | bytes 1376264 | tf_op jit(solution)/shard_map/ppermute | solution.py:1723
  519.5 0.8 copy-start.3
  519.5 0.9 copy-start.4

commit v5 on v4

--- a/solution.py
+++ b/solution.py
@@ -304,9 +304,9 @@
 
 
 class ReadyScatter(PlaneScatter):
-    def __init__(self, place, parts, back, hop, ssem, rsem):
+    def __init__(self, place, part, back, hop, ssem, rsem):
         super().__init__(place, None, None, back, hop, ssem, rsem)
-        self.parts = parts
+        self.part = part
         if place.two_level:
             o = place.slots()
             self.here = (o[0], o[2], o[3], o[6])
@@ -314,28 +314,77 @@
 
     def mine(self, q):
         if not self.place.two_level:
-            return self.parts[self.place.me].astype(F32)
-        return self.parts[pick(q, self.here)].astype(F32)
+            return self.part(self.place.me)[...].astype(F32)
+        return self.part(pick(q, self.here))[...].astype(F32)
 
     def core_copy(self, q):
         core = self.place.mates()[0]
-        v = self.parts.at[self.gone[q]]
+        v = self.part(self.gone[q])
         return remote(v, self.back.at[q], self.ssem.at[q], self.rsem.at[q], core)
 
     def far_copy(self, e):
         pc = self.place
-        v = self.parts.at[(pc.me + e) % pc.count]
+        v = self.part((pc.me + e) % pc.count)
         return remote(v, self.back.at[e - 1], self.ssem.at[e - 1], self.rsem.at[e - 1],
                       pc.plane(e))
 
     def start(self):
         pc = self.place
         if pc.two_level:
-            for q in (2, 1, 3, 0):
+            for q in (3, 2, 1, 0):
                 self.core_copy(q).start()
         else:
             for e in range(1, pc.count):
                 self.far_copy(e).start()
+
+
+class RowSends:
+    def __init__(self, place, layer, out, sems):
+        self.place, self.layer, self.out = (place, layer, out)
+        self.lsem, self.ss, self.sr = sems
+
+    def copies(self, f, src):
+        pc = self.place
+        e = (self.layer * pc.nf + f - pc.me + pc.count) % pc.count
+        own = self.out.at[pc.me]
+        k = (e + pc.count - 1) % pc.count
+        away = remote(src, own, self.ss.at[f], self.sr.at[k], (self.layer, pc.b, f))
+        return (e, away, pltpu.make_async_copy(src, own, self.lsem))
+
+    def start(self, f, src):
+        e, away, local = self.copies(f, src)
+
+        @pl.when(e != 0)
+        def _():
+            away.start()
+
+        @pl.when(e == 0)
+        def _():
+            local.start()
+
+    def finish(self, src):
+        pc = self.place
+        for f in range(pc.nf):
+            e, away, local = self.copies(f, src)
+
+            @pl.when(e != 0)
+            def _():
+                away.wait_send()
+
+            @pl.when(e == 0)
+            def _():
+                local.wait()
+
+        @pl.when(pc.s == self.layer)
+        def _():
+            for e in range(1, pc.count):
+                q = pc.slot_from(e)
+                remote(src, self.out.at[q], self.ss.at[0], self.sr.at[e - 1], pc.plane(e)).wait_recv()
+
+
+def row_scratch(dims):
+    dma = pltpu.SemaphoreType.DMA
+    return [dma(()), dma((dims[2],)), dma((dims[0] * dims[2],))]
 
 
 class LineGather:
@@ -578,105 +627,123 @@
     return part * nb * nf * ns * half + ((b * nf + f) * ns + y) * half
 
 
+def columns_of(ref, q, nf, wide):
+    return ref.at[:, q % nf, :, pl.ds(pl.multiple_of((q // nf) * wide, wide), wide)]
+
+
 def gather_weights_kernel(
-    dims, w_ref, wd, qo, small, gup, wdp, gu_first, qo_all, small_all,
-    pack, lsem, ps, pr, zs, zr, qs, qr, ms, mr, *rest
+    dims, w_ref, wq_ref, wo_ref, wd, small, gup, wdp, gu_first, qo_first, qz, small_all,
+    pack, qcol, qh, lsem, ps, pr, ms, mr, qs, qr, *rest
 ):
     pc = Place(dims)
     ns, nb, nf = dims
     half = wd.shape[1]
+    wide = qh.shape[2]
     greet(pc, "all", True)
-    firsts = []
-    for d in range(1, nb):
-        firsts.append(
-            remote(qo, qo_all.at[pc.s, pc.b, pc.f], zs.at[d - 1], zr.at[d - 1], pc.along(d))
-        )
-        firsts[-1].start()
-    local = [
-        pltpu.make_async_copy(qo, qo_all.at[pc.s, pc.b, pc.f], lsem.at[0]),
-        pltpu.make_async_copy(wd.at[pc.s], wdp.at[pc.s], lsem.at[1]),
-        pltpu.make_async_copy(small, small_all.at[pc.s], lsem.at[2]),
-    ]
-    for c in local:
-        c.start()
+    qkv = wq_ref.shape[2]
+    full = jnp.concatenate([wq_ref[0], wo_ref[0]], axis=1)
+    for y in range(ns):
+        qcol[y] = full[:, y * wide : (y + 1) * wide]
     across = []
     for d in range(1, ns):
         y = (pc.s + d) % ns
         t = (y, pc.b, pc.f)
-        across.append(remote(wd.at[y], wdp.at[pc.s], ms.at[2 * d - 2], mr.at[2 * d - 2], t))
-        across.append(remote(small, small_all.at[pc.s], ms.at[2 * d - 1], mr.at[2 * d - 1], t))
+        i = 3 * (d - 1)
+        across.append(remote(qcol.at[y], qh.at[pc.s], ms.at[i], mr.at[i], t))
+        across.append(remote(wd.at[y], wdp.at[pc.s], ms.at[i + 1], mr.at[i + 1], t))
+        across.append(remote(small, small_all.at[pc.s], ms.at[i + 2], mr.at[i + 2], t))
     for c in across:
         c.start()
-    for y in range(ns):
-        for f in range(nf):
+    qh[pc.s] = qcol[pc.s]
+    local = [
+        pltpu.make_async_copy(wd.at[pc.s], wdp.at[pc.s], lsem.at[0]),
+        pltpu.make_async_copy(small, small_all.at[pc.s], lsem.at[1]),
+    ]
+    for c in local:
+        c.start()
+    own = pltpu.make_async_copy(pack.at[pc.s, pc.f], gup.at[pc.s, pc.f], lsem.at[2])
+
+    def piece(y, f):
+        e = (y * nf + f - pc.me + pc.count) % pc.count
+        k = (e + pc.count - 1) % pc.count
+        return (
+            e,
+            remote(pack.at[y, f], gup.at[pc.s, pc.f], ps.at[k], pr.at[k], (y, pc.b, f)),
+        )
+
+    for f in range(nf):
+        for y in range(ns):
             pieces = []
             for part in range(2):
                 for b in range(nb):
                     c0 = column_start(dims, part, b, f, y, half)
                     pieces.append(w_ref[0, :, c0 : c0 + half])
             pack[y, f] = jnp.concatenate(pieces, axis=1)
-    own = pltpu.make_async_copy(pack.at[pc.s, pc.f], gup.at[pc.s, pc.f], lsem.at[3])
+            e, c = piece(y, f)
+
+            @pl.when(e != 0)
+            def _():
+                c.start()
+
     own.start()
-    plane = []
+    for d in range(ns - 1):
+        across[3 * d].wait()
+    line_q = LineGather(pc, qh, qz, rest[0:3])
+    line_gu = LineGather(pc, gup.at[0], gu_first, rest[3:6])
+    line_q.start()
+    line_q.service()
+    own.wait()
     for e in range(1, pc.count):
-        t = pc.plane(e)
-        plane.append(
-            remote(pack.at[t[0], t[2]], gup.at[pc.s, pc.f], ps.at[e - 1], pr.at[e - 1], t)
-        )
-    for c in plane:
-        c.start()
-    n = pc.count - 1
-    gathers = []
-    for d in range(nb):
-        b = (pc.b + nb - d) % nb
-        gathers.append(
-            PlaneGather(
-                pc,
-                lambda q, b=b: qo_all.at[q // nf, b, q % nf],
-                qs.at[pl.ds(d * n, n)],
-                qr.at[pl.ds(d * n, n)],
-            )
-        )
-    local[0].wait()
-    gathers[0].start()
-    own.wait()
-    for c in plane:
+        q = pc.slot_from(e)
+        remote(
+            pack.at[0, 0], gup.at[q // nf, q % nf], ps.at[e - 1], pr.at[e - 1], pc.plane(e)
+        ).wait_recv()
+    line_gu.start()
+    line_q.service()
+    line_q.finish()
+    gather = PlaneGather(pc, lambda q: columns_of(qo_first, q, nf, wide), qs, qr)
+    fill = pltpu.make_async_copy(qz.at[:, 0], columns_of(qo_first, pc.me, nf, wide), lsem.at[3])
+    fill.start()
+    fill.wait()
+    gather.start()
+    line_gu.service()
+    for step in range(1, min(6, pc.count)):
+        gather.before(step)
+    line_gu.service()
+    for step in range(min(6, pc.count), pc.count):
+        gather.before(step)
+    gather.finish()
+    for y in range(ns):
+        for f in range(nf):
+            e, c = piece(y, f)
+
+            @pl.when(e != 0)
+            def _():
+                c.wait_send()
+
+    for c in local:
         c.wait()
-    line = LineGather(pc, gup.at[0], gu_first, rest)
-    line.start()
-    for d in range(1, nb):
-        firsts[d - 1].wait()
-        gathers[d].start()
-        for step in range(1, min(6, pc.count)):
-            gathers[d - 1].before(step)
-    line.service()
-    for step in range(1, min(6, pc.count)):
-        gathers[nb - 1].before(step)
-    line.service()
-    for step in range(min(6, pc.count), pc.count):
-        for g in gathers:
-            g.before(step)
-    for g in gathers:
-        g.finish()
-    for c in local[1:]:
-        c.wait()
-    for c in across:
-        c.wait()
-    line.finish()
-
-
-def gather_weights(dims, w, wd, qo, small):
+    for i, c in enumerate(across):
+        if i % 3:
+            c.wait()
+    line_gu.finish()
+
+
+def gather_weights(dims, w, wq, wo, wd, small):
     ns, nb, nf = dims
     count = ns * nf
     half, width = wd.shape[1:]
-    dr = qo.shape[0]
+    dr = wq.shape[1]
+    cols = wq.shape[2] + wo.shape[2]
+    wide = cols // ns
     two_ff = 2 * nb * half
     sds = jax.ShapeDtypeStruct
     outs = (
         sds((ns, nf, dr, two_ff), BF),
         sds((ns, half, width), BF),
         sds((nb, nf, dr, two_ff), BF),
-        sds((ns, nb, nf) + qo.shape, BF),
+        sds((nb, nf, dr, cols), BF),
+        sds((nb, ns, dr, wide), BF),
         sds((ns,) + small.shape, F32),
     )
     dma = pltpu.SemaphoreType.DMA
@@ -685,22 +752,22 @@
         "gather_weights",
         0,
         outs,
-        [AN] * 5,
-        [VM, AN, AN, AN],
+        [AN] * 6,
+        [VM, VM, VM, AN, AN],
         [
             pltpu.VMEM((ns, nf, dr, two_ff), BF),
+            pltpu.VMEM((ns, dr, wide), BF),
+            pltpu.VMEM((ns, dr, wide), BF),
             dma((4,)),
+            dma((count,)),
+            dma((count,)),
+            dma((3 * (ns - 1),)),
+            dma((3 * (ns - 1),)),
             dma((count - 1,)),
             dma((count - 1,)),
-            dma((nb - 1,)),
-            dma((nb - 1,)),
-            dma((nb * (count - 1),)),
-            dma((nb * (count - 1),)),
-            dma((2 * (ns - 1),)),
-            dma((2 * (ns - 1),)),
         ]
-        + gather_scratch(dims),
-        (w, wd, qo, small),
+        + gather_scratch(dims) * 2,
+        (w, wq, wo, wd, small),
     )
 
 
@@ -740,10 +807,10 @@
         mask[j] = jnp.where(live, 0.0, NEG)
 
 
-def load_qo(qo_all, layer, w, wo, sems):
+def load_qo(qo, w, wo, sems):
     cols = w.shape[1]
-    c1 = pltpu.make_async_copy(qo_all.at[layer, :, 0:cols], w, sems.at[0])
-    c2 = pltpu.make_async_copy(qo_all.at[layer, :, cols : cols + wo.shape[1]], wo, sems.at[1])
+    c1 = pltpu.make_async_copy(qo.at[:, 0:cols], w, sems.at[0])
+    c2 = pltpu.make_async_copy(qo.at[:, cols : cols + wo.shape[1]], wo, sems.at[1])
     c1.start()
     c2.start()
     return (c1, c2)
@@ -779,13 +846,21 @@
     refs = refs[7:]
     pc = Place(dims)
     width, rows = h_ref.shape
-    loads = load_qo(qo_all, layer, w, wo, qsem)
+    loads = load_qo(qo_all, w, wo, qsem)
     greet(pc, "mates" if carry else None, True)
     riders, refs = plan.board(pc, ins, outs, refs)
+    if carry == "lanes":
+        own = block_ref
+        slot = lambda q: block_all.at[:, lanes(q, rows)]
+    elif carry == "columns":
+        own = block_ref.at[:, 1]
+        slot = lambda q: columns_of(block_all, q, pc.nf, block_ref.shape[3])
     gather = None
     if carry:
-        gather = PlaneGather(pc, lambda q: block_all.at[:, lanes(q, rows)], *refs)
-        block_all[:, lanes(pc.me, rows)] = block_ref[...]
+        gather = PlaneGather(pc, slot, *refs)
+        fill = pltpu.make_async_copy(own, slot(pc.me), qsem.at[2])
+        fill.start()
+        fill.wait()
         gather.start()
     g1, g2, bias = gains_of(padded_t(small_ref[layer]), width, w.shape[1])
     hidden = h_ref[...].astype(BF).astype(F32)
@@ -863,11 +938,11 @@
 
 
 def attention_forward(dims, nk, cid, layer, hidden, small, meta, docs, cos_part, sin_part, qo_all,
-                      plan, block=None):
+                      plan, carry, block):
     width, rows = hidden.shape
-    count = dims[0] * dims[2]
-    carry = block is not None
-    qkv = qo_all.shape[2] - width
+    ns, nb, nf = dims
+    count = ns * nf
+    qkv = qo_all.shape[1] - width
     sds = jax.ShapeDtypeStruct
     outs = [
         sds((width, rows), BF),
@@ -879,15 +954,17 @@
         sds((width, rows), BF),
     ] + plan.shapes
     dma = pltpu.SemaphoreType.DMA
-    if carry:
+    if carry == "lanes":
         outs.append(sds((width, count * rows), BF))
+    else:
+        outs.append(sds((nb, nf, block.shape[2], ns * block.shape[3]), BF))
     out = call(
         functools.partial(attention_forward_kernel, dims, nk, layer, plan, carry),
         "attention_forward",
         cid,
         tuple(outs),
-        [VM] * 7 + plan.places + [VM] * carry,
-        [VM] * 6 + [AN] + [VM] * carry + plan.places,
+        [VM] * 7 + plan.places + [AN],
+        [VM] * 6 + [AN, AN] + plan.places,
         [
             pltpu.VMEM((width, qkv), BF),
             pltpu.VMEM((width, width), BF),
@@ -895,11 +972,11 @@
             pltpu.VMEM((qkv, rows), F32),
             dma((nk - 1,)),
             dma((nk - 1,)),
-            dma((2,)),
+            dma((3,)),
         ]
         + plan.scratch
-        + [dma((count - 1,))] * (2 * carry),
-        (hidden, small, meta, docs, cos_part, sin_part, qo_all, *([block] * carry), *plan.arrays),
+        + [dma((count - 1,))] * 2,
+        (hidden, small, meta, docs, cos_part, sin_part, qo_all, block, *plan.arrays),
     )
     return (out[:7], out[7:])
 
@@ -909,25 +986,28 @@
     h_ref, normed_ref, q_ref, kv_ref, lse_ref, mixed_ref, qo_all, *refs
 ):
     n = plan.count
-    if carry:
-        parts_ref, res_ref, refs = (refs[0], refs[1], refs[2:])
+    parts_ref, more_ref, refs = (refs[0], refs[1], refs[2:])
     ins, refs = (refs[:n], refs[n:])
     gh_ref, dqo_ref, dsmall_ref = refs[:3]
     outs, refs = (refs[3 : 3 + n], refs[3 + n :])
-    if carry:
-        out_ref, refs = (refs[0], refs[1:])
+    out_ref, refs = (refs[0], refs[1:])
+    if carry == "columns":
+        rows_ref, refs = (refs[0], refs[1:])
     w, wo, mask, dmix, dkv, out_kv, in_kv, gj, ssem, rsem, qsem = refs[:11]
     refs = refs[11:]
     pc = Place(dims)
     width, rows = h_ref.shape
     qkv = w.shape[1]
-    loads = load_qo(qo_all, layer, w, wo, qsem)
-    greet(pc, "mates" if carry else None, True)
+    loads = load_qo(qo_all, w, wo, qsem)
+    greet(pc, "all" if carry == "columns" else "mates", True)
     riders, refs = plan.board(pc, ins, outs, refs)
-    scatter = None
-    if carry:
-        scatter = ReadyScatter(pc, parts_ref, *refs)
-        scatter.start()
+    if carry == "columns":
+        part = lambda q: columns_of(parts_ref, q, pc.nf, out_ref.shape[2])
+        hand_out = RowSends(pc, 1, rows_ref, refs[4:])
+    else:
+        part = lambda q: parts_ref.at[q]
+    scatter = ReadyScatter(pc, part, *refs[:4])
+    scatter.start()
     each(riders, "start")
     g1 = column(padded_t(small_ref[layer]), 0, width // 128)
     fill_masks(pc, mask, padded_t(meta_ref[...]), docs_ref[...])
@@ -935,9 +1015,11 @@
     loads[1].wait()
     dmix[...] = nn(wo[...], grl).astype(BF).reshape(dmix.shape)
     dqo_ref[:, qkv:] = nt(mixed_ref[...].reshape(H * HD, rows), grl).astype(BF)
-    if carry:
-        scatter.early()
-        scatter.diagonal()
+    scatter.diagonal()
+    scatter.early()
+    if carry == "columns":
+        for f in range(pc.nf):
+            hand_out.start(f, more_ref.at[f])
     cos_part = cos_ref[...]
     sin_part = sin_ref[...]
     half = HD // 2
@@ -976,7 +1058,7 @@
 
         lax.fori_loop(0, GROUP, one_head, 0)
         each(riders, "service")
-        if carry and g == 0:
+        if g == 0:
             scatter.late()
     for j in range(1, nk):
         out_kv[j - 1] = dkv[j].astype(BF)
@@ -1011,20 +1093,23 @@
     dsmall_ref[:n1, :] = rows_of(gn * unit)
     u = gn * g1
     gh_ref[...] = g_ref[...] + scale_one * (u - unit * jnp.mean(u * unit, axis=0, keepdims=True))
-    if carry:
-
-        def store(total):
-            out_ref[...] = res_ref[...] + total
-
-        scatter.finish(store)
+
+    def store(total):
+        if carry == "columns":
+            out_ref[...] = total.astype(BF)
+        else:
+            out_ref[...] = more_ref[...] + total
+
+    scatter.finish(store)
+    if carry == "columns":
+        hand_out.finish(more_ref.at[0])
     each(riders, "finish")
 
 
 def attention_backward(dims, nk, cid, layer, g, small, meta, docs, cos_part, sin_part, hidden,
-                       normed, q, kv, lse, mixed, qo_all, plan, late=()):
+                       normed, q, kv, lse, mixed, qo_all, plan, carry, late):
     width, rows = hidden.shape
-    carry = len(late) > 0
-    qkv = qo_all.shape[2] - width
+    qkv = qo_all.shape[1] - width
     sds = jax.ShapeDtypeStruct
     outs = [
         sds((width, rows), F32),
@@ -1033,14 +1118,20 @@
     ] + plan.shapes
     dma = pltpu.SemaphoreType.DMA
     block = (2 * KVH, HD, rows)
-    if carry:
-        outs.append(sds((width, rows), F32))
+    if carry == "columns":
+        summed = (dims[1], late[0].shape[2], late[0].shape[3] // dims[0])
+        outs += [sds(summed, BF), sds((dims[0] * dims[2],) + late[1].shape[1:], BF)]
+        places = [VM, AN]
+    else:
+        summed = (width, rows)
+        outs.append(sds(summed, F32))
+        places = [VM]
     out = call(
         functools.partial(attention_backward_kernel, dims, nk, layer, plan, carry),
         "attention_backward",
         cid,
         tuple(outs),
-        [VM] * 3 + plan.places + [VM] * carry,
+        [VM] * 3 + plan.places + places,
         [VM] * 12 + [AN] + [VM] * len(late) + plan.places,
         [
             pltpu.VMEM((width, qkv), BF),
@@ -1056,15 +1147,18 @@
             dma((2,)),
         ]
         + plan.scratch
-        + (scatter_scratch(dims, width, rows)[2:] if carry else []),
+        + scatter_scratch(dims, *summed)[2:]
+        + (row_scratch(dims) if carry == "columns" else []),
         (g, small, meta, docs, cos_part, sin_part, hidden, normed, q, kv, lse, mixed, qo_all,
          *late, *plan.arrays),
     )
     return (out[:3], out[3:])
 
 
-def steps_of(count):
-    return (5, count - 1)
+def sequence_of(pc):
+    if pc.two_level:
+        return ((0, 1, 2, 3, 6, 7, 4, 5), 5, 7)
+    return (tuple(range(pc.count)), pc.count - 1, pc.count - 1)
 
 
 def lanes(slot, rows):
@@ -1096,10 +1190,12 @@
     each(riders, "start")
     transpose_into(wgu_t, wgu_ref)
     transpose_into(wd_t, wd_ref)
-    neighbours, last = steps_of(pc.count)
+    sequence, diagonal_at, early_at = sequence_of(pc)
     chunk = 32 if ff % 32 == 0 else 16
 
-    def step_body(step, carry):
+    def step_body(turn, carry):
+        step = pick(turn, sequence)
+
         for k in range(pc.count):
             @pl.when(step == k)
             def _():
@@ -1121,18 +1217,21 @@
         lax.fori_loop(0, ff // chunk, act, 0)
         scatter.put(step, nn(wd_t[...], inner[...]))
 
-        @pl.when(step == 3)
+        @pl.when(turn == 3)
         def _():
             each(riders, "service")
 
-        @pl.when(step == neighbours)
+        @pl.when(turn == diagonal_at)
+        def _():
+            scatter.diagonal()
+
+        @pl.when(turn == early_at)
         def _():
             scatter.early()
 
         return carry
 
     lax.fori_loop(0, pc.count, step_body, 0)
-    scatter.diagonal()
     each(riders, "service")
 
     def store(total):
@@ -1193,10 +1292,12 @@
     g_all[:, lanes(pc.me, rows)] = g_ref[...].astype(BF)
     gather.start()
     each(riders, "start")
-    neighbours, last = steps_of(pc.count)
+    sequence, diagonal_at, early_at = sequence_of(pc)
     chunk = 32 if ff % 32 == 0 else 16
 
-    def step_body(step, carry):
+    def step_body(turn, carry):
+        step = pick(turn, sequence)
+
         for k in range(pc.count):
             @pl.when(step == k)
             def _():
@@ -1221,18 +1322,21 @@
         lax.fori_loop(0, ff // chunk, act, 0)
         scatter.put(step, nn(wgu_ref[...], ggu[:, sl]))
 
-        @pl.when(step == 3)
+        @pl.when(turn == 3)
         def _():
             each(riders, "service")
 
-        @pl.when(step == neighbours)
+        @pl.when(turn == diagonal_at)
+        def _():
+            scatter.diagonal()
+
+        @pl.when(turn == early_at)
         def _():
             scatter.early()
 
         return carry
 
     lax.fori_loop(0, pc.count, step_body, 0)
-    scatter.diagonal()
     each(riders, "service")
     dwd_ref[...] = nt(inner[...], g_all[...]).astype(BF)
     scatter.late()
@@ -1306,10 +1410,12 @@
     gather.start()
     transpose_into(wgu_t, wgu_ref)
     transpose_into(wd_t, wd_ref)
-    neighbours, last = steps_of(pc.count)
+    sequence, diagonal_at, early_at = sequence_of(pc)
     chunk = 32 if ff % 32 == 0 else 16
 
-    def step_body(step, carry):
+    def step_body(turn, carry):
+        step = pick(turn, sequence)
+
         for k in range(pc.count):
             @pl.when(step == k)
             def _():
@@ -1335,13 +1441,13 @@
         lax.fori_loop(0, ff // chunk, act, 0)
         scatter.put(step, nn(wgu_ref[...], ggu[:, sl]))
 
-        @pl.when(step == neighbours)
+        @pl.when(turn == diagonal_at)
+        def _():
+            scatter.diagonal()
+
+        @pl.when(turn == early_at)
         def _():
             scatter.early()
-
-        @pl.when(step == last)
-        def _():
-            scatter.diagonal()
 
         parts_ref[slot] = nn(wd_t[...], inner[:, sl]).astype(BF)
         return carry
@@ -1405,23 +1511,35 @@
 
 
 def reduce_kernel(
-    dims, cut, qo0, qo1, sa0, sa1, sb0, sb1, gu1, wd1, wd0, gu0a, gu0,
+    dims, cut, qo, terms, sa0, sa1, sb0, sb1, wd1, wd0, gu0a, gu0,
     qo_out, small_out, gu_got, wd_got,
-    gsum, small, sm_in, sm_mid, sm_line, z_out,
-    lsem, ps, pr, ws, wr, ls, lr, zs, zr, *rest
+    gsum, small, sm_in, sm_mid, sm_line, z_out, mine, give,
+    lsem, ws, wr, ls, lr, zs, zr, *rest
 ):
     pc = Place(dims)
     ns, nb, nf = dims
-    line_qo = rest[:4]
-    line_gu = rest[4:8]
-    near, away, back, hop, ss, sr = rest[8:]
     greet(pc, "all", True)
+    scatter = ReadyScatter(
+        pc, lambda q: columns_of(qo, q, nf, z_out.shape[2]), *rest[15:19]
+    )
+    scatter.start()
 
     def keep(value):
         gsum[...] = value.astype(BF)
 
-    line = LineReduce(pc, lambda t: gu0[t, cut:nf], keep, line_gu)
+    def keep_of(l):
+        def store(value):
+            mine[l] = value
+
+        return store
+
+    line = LineReduce(pc, lambda t: gu0[t, cut:nf], keep, rest[0:4])
+    ends = [
+        LineReduce(pc, lambda t: z_out[t], keep_of(0), rest[4:8]),
+        LineReduce(pc, lambda t: terms[t], keep_of(1), rest[8:12]),
+    ]
     line.start()
+    ends[1].start()
     n1 = sb0.shape[0]
     per = small.shape[0] // ns
     nr = sa0.shape[0] + n1
@@ -1434,58 +1552,25 @@
         remote(small, sm_in.at[e - 1], ls.at[e - 1], lr.at[e - 1], pc.plane(e))
         for e in range(1, pc.count)
     ]
-    scatter = PlaneScatter(pc, near, away, back, hop, ss, sr)
-    if pc.two_level:
-        order = pc.slots()
-    else:
-        order = tuple(pc.slot_from(e) for e in range(pc.count))
-    neighbours, last = steps_of(pc.count)
-
-    def step_body(step, carry):
-        slot = pick(step, order)
-        f = slot % nf
-        for l, ref in enumerate((qo0, qo1)):
-            @pl.when(slot // nf == l)
-            def _():
-                scatter.put(step, ref[:, f].astype(F32))
-
-        @pl.when(step == neighbours)
-        def _():
-            scatter.early()
-
-        return carry
-
-    lax.fori_loop(0, pc.count, step_body, 0)
-    scatter.diagonal()
     for c in smalls:
         c.start()
-
-    def send_rows(l, f, src):
-        e = (l * nf + f - pc.me + pc.count) % pc.count
-
-        @pl.when(e != 0)
-        def _():
-            remote(src, gu_got.at[pc.me], ps.at[e - 1], pr.at[e - 1], (l, pc.b, f)).start()
-
-        @pl.when(e == 0)
-        def _():
-            pltpu.make_async_copy(src, gu_got.at[pc.me], lsem.at[0]).start()
-
-    line.service()
-    for f in range(nf):
-        send_rows(1, f, gu1.at[f])
+    scatter.diagonal()
+    scatter.early()
+    hand_out = RowSends(pc, 0, gu_got, rest[12:15])
     for f in range(cut):
-        send_rows(0, f, gu0a.at[f])
+        hand_out.start(f, gu0a.at[f])
     for l, ref in ((0, wd0), (1, wd1)):
         @pl.when(pc.s == l)
         def _():
-            pltpu.make_async_copy(ref, wd_got.at[l], lsem.at[1]).start()
+            pltpu.make_async_copy(ref, wd_got.at[l], lsem.at[0]).start()
 
         @pl.when(pc.s != l)
         def _():
             remote(ref, wd_got.at[pc.s], ws.at[0], wr.at[0], (l, pc.b, pc.f)).start()
 
+    ends[1].service()
     scatter.late()
+    line.service()
     total = small[...]
     for e, c in enumerate(smalls):
         c.wait()
@@ -1497,38 +1582,39 @@
     ]
     for c in lines:
         c.start()
-    line.service()
 
     def store(value):
         z_out[...] = value.astype(BF)
 
     scatter.finish(store)
-
-    def leave(value):
-        qo_out[...] = value
-
-    ends = LineReduce(pc, lambda t: z_out[t], leave, line_qo)
-    ends.start()
+    ends[0].start()
+    ends[1].finish()
+    line.service()
+    ends[0].finish()
+    mate = (ns - 1 - pc.s, pc.b, pc.f)
+    swap = remote(give.at[0], give.at[1], ws.at[1], wr.at[1], mate)
+    give[0] = mine[ns - 1 - pc.s].astype(BF)
+    swap.start()
+    qo_out[pc.s] = mine[pc.s]
     line.finish()
     for f in range(cut, nf):
-        send_rows(0, f, gsum.at[f - cut])
+        hand_out.start(f, gsum.at[f - cut])
     total = sm_mid[...]
     for d, c in enumerate(lines):
         c.wait()
         total = total + sm_line[d]
     small_out[...] = total
-    ends.finish()
-    for k in range(pc.count - 1):
-        remote(gsum.at[0], gu_got.at[pc.me], ps.at[k], pr.at[k], pc.plane(1)).wait()
-    pltpu.make_async_copy(gsum.at[0], gu_got.at[pc.me], lsem.at[0]).wait()
-    pltpu.make_async_copy(wd0, wd_got.at[pc.s], lsem.at[1]).wait()
-    remote(wd0, wd_got.at[pc.s], ws.at[0], wr.at[0], pc.plane(1)).wait()
-
-
-def reduce_gradients(dims, cid, cut, qo0, qo1, smalls, gu1, wd1, wd0, gu0a, gu0):
+    swap.wait()
+    qo_out[ns - 1 - pc.s] = give[1].astype(F32)
+    hand_out.finish(gsum.at[0])
+    pltpu.make_async_copy(wd0, wd_got.at[pc.s], lsem.at[0]).wait()
+    remote(wd0, wd_got.at[pc.s], ws.at[0], wr.at[0], mate).wait()
+
+
+def reduce_gradients(dims, cid, cut, qo, terms, smalls, wd1, wd0, gu0a, gu0):
     ns, nb, nf = dims
     count = ns * nf
-    dr, cols = qo0.shape[2:]
+    dr, wide = terms.shape[1:]
     two_ff = gu0.shape[3]
     half, width = wd0.shape
     rows = smalls[0].shape[0] + smalls[2].shape[0]
@@ -1540,39 +1626,40 @@
         "reduce_gradients",
         cid,
         (
-            sds((dr, cols), F32),
+            sds((ns, dr, wide), F32),
             sds(small, F32),
             sds((count, dr, two_ff), BF),
             sds((ns, half, width), BF),
         ),
         [VM] * 4,
-        [VM] * 11,
+        [VM] * 10,
         [
             pltpu.VMEM((nf - cut, dr, two_ff), BF),
             pltpu.VMEM(small, F32),
             pltpu.VMEM((count - 1,) + small, F32),
             pltpu.VMEM(small, F32),
             pltpu.VMEM((nb - 1,) + small, F32),
-            pltpu.VMEM((nb, dr, cols), BF),
+            pltpu.VMEM((nb, dr, wide), BF),
+            pltpu.VMEM((ns, dr, wide), F32),
+            pltpu.VMEM((2, dr, wide), BF),
+            dma((1,)),
             dma((2,)),
-            dma((count - 1,)),
-            dma((count - 1,)),
-            dma((ns - 1,)),
-            dma((ns - 1,)),
+            dma((2,)),
             dma((count - 1,)),
             dma((count - 1,)),
             dma((nb - 1,)),
             dma((nb - 1,)),
         ]
-        + reduce_scratch(dims, dr, cols)
         + reduce_scratch(dims, nf - cut, dr, two_ff)
-        + scatter_scratch(dims, nb, dr, cols),
-        (qo0, qo1, *smalls, gu1, wd1, wd0, gu0a, gu0),
+        + reduce_scratch(dims, dr, wide) * 2
+        + row_scratch(dims)
+        + scatter_scratch(dims, nb, dr, wide)[2:],
+        (qo, terms, *smalls, wd1, wd0, gu0a, gu0),
     )
 
 
 def lay_out_kernel(
-    dims, gu, wd, qo, small, out0, out1, gh0, gh1, take_out, take_grad,
+    dims, gu0, gu1, wd, qo, small, out0, out1, gh0, gh1, take_out, take_grad,
     block_out, input_grad, g1, wqkv, bqkv, wout, g2, wgu, wdn
 ):
     ns, nb, nf = dims
@@ -1580,17 +1667,22 @@
     s = lax.axis_index("section")
     qkv = wqkv.shape[2]
     width = wout.shape[2]
-    wqkv[0] = qo[:, :qkv]
-    wout[0] = qo[:, qkv:]
+    full = jnp.concatenate([qo[y] for y in range(ns)], axis=1)
+    wqkv[0] = full[:, :qkv]
+    wout[0] = full[:, qkv:]
     for y in range(ns):
         wdn[0, y * half : (y + 1) * half, :] = wd[y].astype(F32)
-        for f in range(nf):
-            got = gu[y * nf + f].astype(F32)
-            for part in range(2):
-                for b in range(nb):
-                    c0 = column_start(dims, part, b, f, y, half)
-                    k0 = (part * nb + b) * half
-                    wgu[0, :, c0 : c0 + half] = got[:, k0 : k0 + half]
+    for l, gu in enumerate((gu0, gu1)):
+        @pl.when(s == l)
+        def _():
+            for y in range(ns):
+                for f in range(nf):
+                    got = gu[y * nf + f].astype(F32)
+                    for part in range(2):
+                        for b in range(nb):
+                            c0 = column_start(dims, part, b, f, y, half)
+                            k0 = (part * nb + b) * half
+                            wgu[0, :, c0 : c0 + half] = got[:, k0 : k0 + half]
     n1 = width // 128
     per = small.shape[0] // ns
     rows = small[pl.ds(pl.multiple_of(s * per, 8), per), :]
@@ -1612,9 +1704,9 @@
 
 def lay_out(dims, qkv, args):
     ns, nb, nf = dims
-    gu, wd, qo = args[:3]
-    width, rows = args[4].shape
-    dr = qo.shape[0]
+    gu, wd, qo = (args[0], args[2], args[3])
+    width, rows = args[5].shape
+    dr = qo.shape[1]
     sds = jax.ShapeDtypeStruct
     tokens = sds((1, ns, rows, width), F32)
     return pl.pallas_call(
@@ -1677,45 +1769,52 @@
     g = cot.T.astype(F32)
 
     wd = w_down[0].reshape(ns, half, width)
-    qo = jnp.concatenate([w_qkv[0], w_out[0]], axis=1)
     small = jnp.concatenate([norm1_gain[0], norm2_gain[0], b_qkv[0]])
     total = -(-small.shape[0] // 1024) * 1024
     small = jnp.pad(small, (0, total - small.shape[0])).reshape(-1, 128)
-    gup, wdp, gu_first, qo_all, small_all = gather_weights(dims, w_gate_up, wd, qo, small)
-    qo_all = qo_all.reshape(ns, width, qkv + width)
+    gup, wdp, gu_first, qo_first, qz, small_all = gather_weights(
+        dims, w_gate_up, w_qkv, w_out, wd, small
+    )
+    cols = qkv + width
     wide = (width, 2 * ff)
 
-    common = (small_all, meta, query_docs, cos_part, sin_part, qo_all)
     def ride(*pairs):
         return Riders(dims, tuple(a for a, _ in pairs), tuple(v for _, v in pairs))
 
-    a0, (wd0,) = attention_forward(dims, nk, 1, 0, hidden, *common, ride((("gather", 0), wdp)))
+    common = (small_all, meta, query_docs, cos_part, sin_part)
+    qo0 = qo_first.reshape(width, cols)
+    a0, (wd0, qo1) = attention_forward(
+        dims, nk, 1, 0, hidden, *common, qo0, ride((("gather", 0), wdp)), "columns", qz
+    )
+    qo1 = qo1.reshape(width, cols)
     wd0 = wd0.reshape(ff, width)
     wgu0 = gu_first.reshape(wide)
     f0, (gu1,) = feed_forward(dims, 3, a0[6], a0[5], wgu0, wd0, ride((("gather", 1), gup)))
     wgu1 = gu1.reshape(wide)
     a1, (wd1, g_all) = attention_forward(
-        dims, nk, 2, 1, f0[0], *common, ride((("gather", 1), wdp)), cot.T
+        dims, nk, 2, 1, f0[0], *common, qo1, ride((("gather", 1), wdp)), "lanes", cot.T
     )
     wd1 = wd1.reshape(ff, width)
 
     line_gu = (nb, nf, dr, 2 * ff)
     line_wd = (nb, half, width)
+    line_qo = (nb, nf, dr, cols)
     everything = (0, half)
     cut = nf // 2
     b1 = feed_both(dims, 4, 1, a1[6], a1[5], g, g_all, wgu1, wd1, small_all)
     ab1, (dwd1, out1) = attention_backward(
-        dims, nk, 7, 1, b1[0], *common[:5], f0[0], *a1[:5], qo_all,
-        ride((("reduce", everything), b1[2].reshape(line_wd))), (b1[4], a1[5]),
+        dims, nk, 7, 1, b1[0], *common, f0[0], *a1[:5], qo1,
+        ride((("reduce", everything), b1[2].reshape(line_wd))), "sum", (b1[4], a1[5]),
     )
     b0, (dgu1,) = feed_backward(
         dims, 6, 0, ab1[0], a0[5], f0[1], f0[2], wgu0, wd0, small_all,
         ride((("reduce", (0, nf)), b1[1].reshape(line_gu))),
     )
     dgu0 = b0[1].reshape(line_gu)
-    ab0, (dwd0, dgu0a) = attention_backward(
-        dims, nk, 8, 0, b0[0], *common[:5], hidden, *a0[:5], qo_all,
+    ab0, (dwd0, dgu0a, terms, gu_got1) = attention_backward(
+        dims, nk, 8, 0, b0[0], *common, hidden, *a0[:5], qo0,
         ride((("reduce", everything), b0[2].reshape(line_wd)), (("reduce", (0, cut)), dgu0)),
+        "columns", (ab1[1].reshape(line_qo), dgu1),
     )
 
     def swapped(values):
@@ -1724,15 +1823,15 @@
 
     take_out = swapped((f0[0], out1))
     take_grad = swapped((ab0[0], ab1[0]))
-    line_qo = (nb, nf, dr, qkv + width)
-    grad_qo, small_sum, gu_got, wd_got = reduce_gradients(
-        dims, 9, cut, ab0[1].reshape(line_qo), ab1[1].reshape(line_qo),
-        (ab0[2], ab1[2], b0[3], b1[3]), dgu1, dwd1, dwd0, dgu0a, dgu0,
+    grad_qo, small_sum, gu_got0, wd_got = reduce_gradients(
+        dims, 9, cut, ab0[1].reshape(line_qo), terms,
+        (ab0[2], ab1[2], b0[3], b1[3]), dwd1, dwd0, dgu0a, dgu0,
     )
     return lay_out(
         dims,
         qkv,
-        (gu_got, wd_got, grad_qo, small_sum, f0[0], out1, ab0[0], ab1[0], take_out, take_grad),
+        (gu_got0, gu_got1, wd_got, grad_qo, small_sum, f0[0], out1, ab0[0], ab1[0], take_out,
+         take_grad),
     )
 
 

time: 539 us -> 564 us (1.046); the launches traced: 528 us -> 560 us
  Pallas kernels: 511 us -> 544 us
    pallas_call x9, Pallas kernels: 503 us -> 536 us  [call(): pl.pallas_call(kernel, name=name, out_shape=outs, in_specs=in_specs, out_...]
  transfers between devices with their start and end apart: 2 -> 2, of which waited for: 0 -> 0; matrix products, arithmetic and copies ran while one was open for 0% -> 0% of each run, Pallas kernels for 35% -> 32%
where the time goes in v5:
time: 564 us; the launch traced here: 560 us
  Pallas kernels  544 us (96%)
  other arithmetic  9.01 us (2%)
    pallas_call x9, Pallas kernels, call(): pl.pallas_call(kernel, name=name, out_shape=outs, in_specs=in_specs, out_...  536 us
  transfers between devices with their start and end apart: 2, of which 0 were waited for; matrix products, arithmetic and copies ran while one was open for 0% of the time, Pallas kernels for 32%

profile of v5, /device:TPU:0, one launch (start us, length us, event | category | flops | bytes accessed | tf_op | source)
XLA Modules:
  0.0 560.0 jit_solution(15557668007163604712)
XLA Ops:
  0.7 0.1 broadcast_in_dim.16
  0.8 0.1 broadcast_in_dim.17
  0.9 0.7 fusion.1
  1.6 0.7 convert_reduce_fusion
  2.3 0.6 gather_fusion
  2.9 0.6 constant_dynamic-slice_fusion.2.docs_ref
  3.4 0.7 reduce
  4.1 0.7 reduce.1
  4.8 0.7 reduce.2
  5.5 1.2 constant_dynamic-slice_fusion
  6.8 0.2 copy.21
  7.0 0.2 copy.22
  7.2 1.0 convert_bitcast_fusion.h_ref
  8.2 1.0 bitcast_convert_fusion.g_ref
  9.2 0.7 broadcast_select_fusion.meta_ref
  9.9 0.8 multiply_sine_fusion
  10.7 0.6 fusion.small
  11.3 88.8 %gather_weights.1 = (bf16[2,4,56,1216]{3,2,1,0:T(8,128)(2,1)}, bf16[2,152,896]{2,1,0:T(8,128)(2,1)}, bf16[4,4,56,1216]{3,2,1,0:T(8,128)(2,1)}, bf16[4,4,56,2048]...) custom-call(bf16[1,56,9728]{2,1,0:T(8,128)(2,1)} %w_ref.1, bf16[1,56,1152]{2,1,0:T(8,128)(2,1)} %wq_ref.1, ...), custom_call_target="tpu_custom_call" | custom-call | tf_op jit(solution)/shard_map/gather_weights/pallas_call | solution.py:614
  100.1 52.6 %attention_forward.2 = (bf16[896,256]{1,0:T(8,128)(2,1)}, bf16[14,64,256]{2,1,0:T(8,128)(2,1)}, bf16[3,4,64,256]{3,2,1,0:T(8,128)(2,1)}, f32[14,1,256]{2,1,0:T(1...) custom-call(f32[896,256]{1,0:T(8,128)} %convert_bitcast_fusion.h_ref, ...), custom_call_target="tpu_custom_call" | custom-call | tf_op jit(solution)/shard_map/attention_forward/pallas_call | solution.py:614
  152.7 55.6 %feed_forward.1 = (f32[896,256]{1,0:T(8,128)}, bf16[896,2048]{1,0:T(8,128)(2,1)}, bf16[1216,2048]{1,0:T(8,128)(2,1)}, bf16[4,4,56,1216]{3,2,1,0:T(8,128)(2,1)}) custom-call(bf16[896,256]{1,0:T(8,128)(2,1)} %get-tuple-element.67.x_ref, f32[896,256]{1,0:T(8,128)} %get-tuple-element.68.res_ref, bf16[896,1216]{1,0:T(8,128)(2,1)} %bitcast.33, ...), custom_call_target="tpu_custom_call" | custom-call | tf_op jit(solution)/shard_map/feed_forward/pallas_call | solution.py:614
  208.3 50.5 %attention_forward.3 = (bf16[896,256]{1,0:T(8,128)(2,1)}, bf16[14,64,256]{2,1,0:T(8,128)(2,1)}, bf16[3,4,64,256]{3,2,1,0:T(8,128)(2,1)}, f32[14,1,256]{2,1,0:T(1...) custom-call(f32[896,256]{1,0:T(8,128)} %get-tuple-element.72.h_ref.o, ...), custom_call_target="tpu_custom_call" | custom-call | tf_op jit(solution)/shard_map/attention_forward/pallas_call | solution.py:614
  258.8 61.5 %feed_both.1 = (f32[896,256]{1,0:T(8,128)}, bf16[896,1216]{1,0:T(8,128)(2,1)}, bf16[608,896]{1,0:T(8,128)(2,1)}, f32[7,128]{1,0:T(8,128)}, bf16[8,896,256]{2,1,0:T(8,128)(2,1)}) custom-call(bf16[896,256]{1,0:T(8,128)(2,1)} %get-tuple-element.74.x_ref, f32[896,256]{1,0:T(8,128)} %get-tuple-element.75.res_ref.refs_1_, f32[896,256]{1,0:T(8,128)} %bitcast_convert_fusion.g_ref, ...), custom_call_target="tpu_custom_call" | custom-call | tf_op jit(solution)/shard_map/feed_both/pallas_call | solution.py:614
  320.3 45.5 %attention_backward.2 = (f32[896,256]{1,0:T(8,128)}, bf16[896,2048]{1,0:T(8,128)(2,1)}, f32[16,128]{1,0:T(8,128)}, bf16[152,896]{1,0:T(8,128)(2,1)}, f32[896,256]{1,0:T(8,128)}) custom-call(f32[896,256]{1,0:T(8,128)} %get-tuple-element.79.g_ref, f32[2,24,128]{2,1,0:T(8,128)} %get-tuple-element.63.small_ref, f32[6,128]{1,0:T(8,128)} %broadcast_select_fusion.meta_ref, ...), custom_call_target="tpu_custom_call" | custom-call | tf_op jit(solution)/shard_map/attention_backward/pallas_call | solution.py:614
  365.9 1.3 select_convert_fusion.1
  367.2 56.2 %feed_backward.1 = (f32[896,256]{1,0:T(8,128)}, bf16[896,1216]{1,0:T(8,128)(2,1)}, bf16[608,896]{1,0:T(8,128)(2,1)}, f32[7,128]{1,0:T(8,128)}, bf16[4,56,1216]{2,1,0:T(8,128)(2,1)}) custom-call(f32[896,256]{1,0:T(8,128)} %get-tuple-element.87.g_ref.gh1, f32[896,256]{1,0:T(8,128)} %get-tuple-element.68.res_ref, bf16[896,2048]{1,0:T(8,128)(2,1)} %get-tuple-element.88.x_all, ...), custom_call_target="tpu_custom_call" | custom-call | tf_op jit(solution)/shard_map/feed_backward/pallas_call | solution.py:614
  423.4 58.4 %attention_backward.3 = (f32[896,256]{1,0:T(8,128)}, bf16[896,2048]{1,0:T(8,128)(2,1)}, f32[16,128]{1,0:T(8,128)}, bf16[152,896]{1,0:T(8,128)(2,1)}, bf16[2,56,1...) custom-call(f32[896,256]{1,0:T(8,128)} %get-tuple-element.91.g_ref, ...), custom_call_target="tpu_custom_call" | custom-call | tf_op jit(solution)/shard_map/attention_backward/pallas_call | solution.py:614
  481.8 0.1 select_convert_fusion
  481.9 2.0 collective-permute-start.1
  483.9 67.0 %reduce_gradients.1 = (f32[2,56,1024]{2,1,0:T(8,128)}, f32[48,128]{1,0:T(8,128)}, bf16[8,56,1216]{2,1,0:T(8,128)(2,1)}, bf16[2,152,896]{2,1,0:T(8,128)(2,1)}) custom-call(bf16[4,4,56,2048]{3,2,1,0:T(8,128)(2,1)} %bitcast.38, bf16[4,56,1024]{2,1,0:T(8,128)(2,1)} %get-tuple-element.102.terms, f32[16,128]{1,0:T(8,128)} %get-tuple-element.103.sa0, ...), custom_call_target="tpu_custom_call" | custom-call | tf_op jit(solution)/shard_map/reduce_gradients/pallas_call | solution.py:614
  551.0 0.7 copy-done.3
  551.7 0.2 copy-done.4
  551.9 7.9 %lay_out.1 = (f32[1,2,256,896]{3,2,1,0:T(8,128)}, f32[1,2,256,896]{3,2,1,0:T(8,128)}, f32[1,896]{1,0:T(1,128)}, f32[1,56,1152]{2,1,0:T(8,128)}, f32[1,1152]{1,0:...) custom-call(bf16[8,56,1216]{2,1,0:T(8,128)(2,1)} %get-tuple-element.110.gu, ...), custom_call_target="tpu_custom_call" | custom-call | tf_op jit(solution)/shard_map/lay_out/pallas_call | solution.py:1712
  (17 shorter events, 0.2 us)
Async XLA Ops:
  7.0 93.1 %copy-start.2 = (bf16[1,256,896]{1,2,0:T(8,128)(2,1)}, bf16[1,256,896]{1,2,0:T(8,128)(2,1)S(1)}, u32[]{:S(2)}) copy-start(bf16[1,256,896]{1,2,0:T(8,128)(2,1)S(1)} %copy.21) | copy-start | bytes 1376260
  320.3 45.6 %copy-start = (f32[896,256]{1,0:T(8,128)S(1)}, f32[896,256]{1,0:T(8,128)}, u32[]{:S(2)}) copy-start(f32[896,256]{1,0:T(8,128)} %get-tuple-element.72.h_ref.out0) | copy-start | bytes 2752516
  367.2 183.8 %collective-permute-start = (bf16[896,256]{1,0:T(8,128)(2,1)S(1)}, bf16[896,256]{1,0:T(8,128)(2,1)S(1)}, u32[]{:S(2)}, u32[]{:S(2)}) collective-permute-start(bf16[896,256]{1,0:T(8,128)(2,1)S(1)} %select_convert_fusion.1), channel_id=1, source_target_pairs={{0,16},{16,0},{1,17},{17,1},{2,18},{18,2},{3,19},{19,3},{4,20},{20... | collective-permute-start | bytes 1376264 | tf_op jit(solution)/shard_map/ppermute | solution.py:1822
  423.4 58.4 %copy-start.1 = (f32[896,256]{1,0:T(8,128)S(1)}, f32[896,256]{1,0:T(8,128)}, u32[]{:S(2)}) copy-start(f32[896,256]{1,0:T(8,128)} %get-tuple-element.87.g_ref.gh1) | copy-start | bytes 2752516
  481.9 69.0 %collective-permute-start.1 = (bf16[896,256]{1,0:T(8,128)(2,1)S(1)}, bf16[896,256]{1,0:T(8,128)(2,1)S(1)}, u32[]{:S(2)}, u32[]{:S(2)}) collective-permute-start(bf16[896,256]{1,0:T(8,128)(2,1)S(1)} %select_convert_fusion), channel_id=1, source_target_pairs={{0,16},{16,0},{1,17},{17,1},{2,18},{18,2},{3,19},{19,3},{4,20},{20... | collective-permute-start | bytes 1376264 | tf_op jit(solution)/shard_map/ppermute | solution.py:1822
  551.0 0.8 copy-start.3
  551.0 0.9 copy-start.4

commit v6 on v5

--- a/solution.py
+++ b/solution.py
@@ -115,65 +115,83 @@
     )
 
 
+def cut_in(parts, view, c):
+    n = view.shape[0] // parts
+    return view.at[pl.ds(c * n, n)]
+
+
+def gather_sems(dims):
+    n = 2 * (dims[0] * dims[2] - 1)
+    return [pltpu.SemaphoreType.DMA((n,)), pltpu.SemaphoreType.DMA((n,))]
+
+
 class PlaneGather:
     def __init__(self, place, slot, ssem, rsem):
         self.place, self.slot, self.ssem, self.rsem = (place, slot, ssem, rsem)
+        self.parts = 2 if place.two_level else 1
         if place.two_level:
             self.order = place.slots()
         else:
             self.order = tuple(place.slot_from(e) for e in range(place.count))
 
-    def copy(self, k, q, device):
-        v = self.slot(q)
-        return remote(v, v, self.ssem.at[k], self.rsem.at[k], device)
+    def copy(self, k, c, q, device):
+        v = cut_in(self.parts, self.slot(q), c)
+        i = k * self.parts + c
+        return remote(v, v, self.ssem.at[i], self.rsem.at[i], device)
 
     def start(self):
         pc = self.place
         if pc.two_level:
             core, xm, ym = pc.mates()
-            self.copy(1, self.order[0], xm).start()
-            self.copy(2, self.order[0], ym).start()
-            self.copy(0, self.order[0], core).start()
+            for c in range(2):
+                self.copy(1, c, self.order[0], xm).start()
+                self.copy(2, c, self.order[0], ym).start()
+            for c in range(2):
+                self.copy(0, c, self.order[0], core).start()
         else:
             for e in range(1, pc.count):
-                self.copy(e - 1, self.order[0], pc.plane(e)).start()
-
-    def waited(self, k):
-        self.copy(k, self.order[k + 1], self.place.plane(1)).wait_recv()
+                self.copy(e - 1, 0, self.order[0], pc.plane(e)).start()
+
+    def came(self, k, c):
+        self.copy(k, c, self.order[k + 1], self.place.plane(1)).wait_recv()
 
     def before(self, step):
         if step == 0:
             return
         pc = self.place
         if not pc.two_level:
-            self.waited(step - 1)
+            self.came(step - 1, 0)
             return
         core, xm, ym = pc.mates()
-        c = pc.f % 2
+        h = pc.f % 2
         if step == 2:
-            self.waited(1)
-            self.copy(3, self.order[2], core).start()
-            self.waited(2)
-            self.copy(4, self.order[3], core).start()
-            which = c * self.order[3] + (1 - c) * self.order[2]
+            which = h * self.order[3] + (1 - h) * self.order[2]
             far = (
-                c * xm[0] + (1 - c) * ym[0],
+                h * xm[0] + (1 - h) * ym[0],
                 pc.b,
-                c * xm[2] + (1 - c) * ym[2],
+                h * xm[2] + (1 - h) * ym[2],
             )
-            self.copy(5, which, far).start()
+            for c in range(2):
+                self.came(1, c)
+                self.came(2, c)
+                self.copy(5, c, which, far).start()
+                self.copy(3, c, self.order[2], core).start()
+                self.copy(4, c, self.order[3], core).start()
         elif step == 3:
             return
         elif step == 6:
-            self.waited(5)
-            self.copy(6, self.order[6], core).start()
+            for c in range(2):
+                self.came(5, c)
+                self.copy(6, c, self.order[6], core).start()
         else:
-            self.waited(step - 1)
+            for c in range(2):
+                self.came(step - 1, c)
 
     def finish(self):
         n = self.place.count - 1
         for k in range(n):
-            self.copy(k, self.order[0], self.place.plane(1)).wait_send()
+            for c in range(self.parts):
+                self.copy(k, c, self.order[0], self.place.plane(1)).wait_send()
 
 
 class PlaneScatter:
@@ -223,10 +241,19 @@
         return remote(self.away.at[e - 1], self.back.at[e - 1], self.ssem.at[e - 1],
                       self.rsem.at[e - 1], self.place.plane(e))
 
-    def hop_copy(self, k, device):
+    def hop_copy(self, k, c, device):
+        i = 4 + 2 * k + c
         return remote(
-            self.hop.at[k], self.hop.at[k + 3], self.ssem.at[4 + k], self.rsem.at[4 + k], device
+            cut_in(2, self.hop.at[k], c),
+            cut_in(2, self.hop.at[k + 3], c),
+            self.ssem.at[i],
+            self.rsem.at[i],
+            device,
         )
+
+    def rows(self, c):
+        n = self.hop.shape[1] // 2
+        return slice(c * n, (c + 1) * n)
 
     def targets(self):
         pc = self.place
@@ -245,8 +272,10 @@
         self.core_copy(1).wait_recv()
         self.core_copy(2).wait_recv()
         q = c * 1 + (1 - c) * 2
-        self.hop[0] = (self.mine(q) + self.back[q].astype(F32)).astype(BF)
-        self.hop_copy(0, first).start()
+        for k in range(2):
+            r = self.rows(k)
+            self.hop[0, r] = (self.mine(q, r) + self.back[q, r].astype(F32)).astype(BF)
+            self.hop_copy(0, k, first).start()
 
     def diagonal(self):
         pc = self.place
@@ -254,11 +283,13 @@
             return
         first, second = self.targets()
         self.core_copy(3).wait_recv()
-        self.hop[1] = (self.mine(3) + self.back[3].astype(F32)).astype(BF)
-        self.hop_copy(1, first).start()
-
-    def mine(self, q):
-        return self.near[q]
+        for k in range(2):
+            r = self.rows(k)
+            self.hop[1, r] = (self.mine(3, r) + self.back[3, r].astype(F32)).astype(BF)
+            self.hop_copy(1, k, first).start()
+
+    def mine(self, q, r=slice(None)):
+        return self.near[q, r]
 
     def result(self, store):
         self.late()
@@ -270,12 +301,14 @@
             return
         c = pc.f % 2
         first, second = self.targets()
-        self.hop_copy(1, first).wait_recv()
         q = c * 2 + (1 - c) * 1
-        self.hop[2] = (
-            self.mine(q) + self.back[q].astype(F32) + self.hop[4].astype(F32)
-        ).astype(BF)
-        self.hop_copy(2, second).start()
+        for k in range(2):
+            r = self.rows(k)
+            self.hop_copy(1, k, first).wait_recv()
+            self.hop[2, r] = (
+                self.mine(q, r) + self.back[q, r].astype(F32) + self.hop[4, r].astype(F32)
+            ).astype(BF)
+            self.hop_copy(2, k, second).start()
 
     def finish(self, store):
         pc = self.place
@@ -288,8 +321,9 @@
             return
         first, second = self.targets()
         self.core_copy(0).wait_recv()
-        self.hop_copy(0, first).wait_recv()
-        self.hop_copy(2, second).wait_recv()
+        for k in range(2):
+            self.hop_copy(0, k, first).wait_recv()
+            self.hop_copy(2, k, second).wait_recv()
         store(
             self.mine(0)
             + self.back[0].astype(F32)
@@ -298,9 +332,10 @@
         )
         for q in range(4):
             self.core_copy(q).wait_send()
-        self.hop_copy(0, first).wait_send()
-        self.hop_copy(1, first).wait_send()
-        self.hop_copy(2, second).wait_send()
+        for k in range(2):
+            self.hop_copy(0, k, first).wait_send()
+            self.hop_copy(1, k, first).wait_send()
+            self.hop_copy(2, k, second).wait_send()
 
 
 class ReadyScatter(PlaneScatter):
@@ -312,10 +347,10 @@
             self.here = (o[0], o[2], o[3], o[6])
             self.gone = (o[1], o[4], o[5], o[7])
 
-    def mine(self, q):
+    def mine(self, q, r=slice(None)):
         if not self.place.two_level:
             return self.part(self.place.me)[...].astype(F32)
-        return self.part(pick(q, self.here))[...].astype(F32)
+        return self.part(pick(q, self.here))[r].astype(F32)
 
     def core_copy(self, q):
         core = self.place.mates()[0]
@@ -388,21 +423,22 @@
 
 
 class LineGather:
-    def __init__(self, place, piece, out, sems):
-        self.place, self.piece, self.out = (place, piece, out)
+    def __init__(self, place, piece, out, sems, part=None):
+        self.place, self.piece = (place, piece)
+        self.view = lambda t: out.at[t] if part is None else out.at[t, part]
         self.lsem, self.ss, self.sr = sems
         self.k = 0
 
     def local(self):
-        return pltpu.make_async_copy(self.piece, self.out.at[self.place.b], self.lsem)
+        return pltpu.make_async_copy(self.piece, self.view(self.place.b), self.lsem)
 
     def hop(self, way, k, came):
         pc = self.place
         t = pc.b - way * (k - (0 if came else 1))
-        src = self.piece if k == 1 and not came else self.out.at[t]
+        src = self.piece if k == 1 and not came else self.view(t)
         i = k - 1 + (0 if way == 1 else pc.nb - 1)
         return remote(
-            src, self.out.at[t], self.ss.at[i], self.sr.at[i], (pc.s, pc.b + way, pc.f)
+            src, self.view(t), self.ss.at[i], self.sr.at[i], (pc.s, pc.b + way, pc.f)
         )
 
     def sends(self, way, k):
@@ -448,8 +484,8 @@
 
 
 class LineReduce:
-    def __init__(self, place, terms, store, sems):
-        self.place, self.terms, self.store = (place, terms, store)
+    def __init__(self, place, terms, store, sems, load=None):
+        self.place, self.terms, self.store, self.load = (place, terms, store, load)
         self.out, self.came, self.ss, self.sr = sems
         self.k = 0
 
@@ -473,6 +509,8 @@
         return (r < k) & (r < self.place.nb - 1)
 
     def start(self):
+        if self.load is not None:
+            self.load.wait()
         self.service()
 
     def service(self):
@@ -550,19 +588,22 @@
     def __init__(self, dims, specs, arrays):
         self.dims, self.specs, self.arrays = (dims, specs, arrays)
         self.shapes = []
-        self.places = []
+        self.places = [AN] * len(specs)
+        self.outs = []
         self.scratch = []
         self.sizes = []
         for spec, a in zip(specs, arrays):
             if spec[0] == "gather":
                 shape = (dims[1],) + a.shape[1:]
-                self.places.append(AN)
                 scratch = gather_scratch(dims)
             else:
                 lo, hi = spec[1]
                 shape = (hi - lo,) + a.shape[2:]
-                self.places.append(VM)
                 scratch = reduce_scratch(dims, *shape)
+                scratch += [
+                    pltpu.VMEM((dims[1],) + shape, BF), pltpu.SemaphoreType.DMA(())
+                ]
+            self.outs.append(AN if spec[0] == "gather" else VM)
             self.shapes.append(jax.ShapeDtypeStruct(shape, a.dtype))
             self.scratch += scratch
             self.sizes.append(len(scratch))
@@ -580,8 +621,11 @@
                 def store(value, o=o):
                     o[...] = value.astype(BF)
 
+                terms, sem = mine[4:]
+                load = pltpu.make_async_copy(a.at[:, lo:hi], terms, sem)
+                load.start()
                 out.append(
-                    LineReduce(place, lambda t, a=a, lo=lo, hi=hi: a[t, lo:hi], store, mine)
+                    LineReduce(place, lambda t, r=terms: r[t], store, mine[:4], load)
                 )
         return (out, scratch)
 
@@ -594,7 +638,7 @@
 def scatter_scratch(dims, *block):
     count = dims[0] * dims[2]
     if dims[0] == 2 and dims[2] == 4:
-        near, away, hops, sems = (4, 4, 6, 7)
+        near, away, hops, sems = (4, 4, 6, 10)
     else:
         near, away, hops, sems = (1, count - 1, 1, count - 1)
     return [
@@ -689,30 +733,41 @@
     for d in range(ns - 1):
         across[3 * d].wait()
     line_q = LineGather(pc, qh, qz, rest[0:3])
-    line_gu = LineGather(pc, gup.at[0], gu_first, rest[3:6])
+    lines = [
+        LineGather(pc, gup.at[0, f], gu_first, rest[3 + 3 * f : 6 + 3 * f], f) for f in range(nf)
+    ]
     line_q.start()
+
+    def arrived(y, f):
+        e, c = piece(y, f)
+        k = (2 * pc.count - e - 1) % pc.count
+
+        @pl.when(e != 0)
+        def _():
+            remote(pack.at[0, 0], gup.at[y, f], ps.at[k], pr.at[k], (y, pc.b, f)).wait_recv()
+
+    own.wait()
     line_q.service()
-    own.wait()
-    for e in range(1, pc.count):
-        q = pc.slot_from(e)
-        remote(
-            pack.at[0, 0], gup.at[q // nf, q % nf], ps.at[e - 1], pr.at[e - 1], pc.plane(e)
-        ).wait_recv()
-    line_gu.start()
+    for f in range(nf):
+        arrived(0, f)
+        lines[f].start()
     line_q.service()
+    for line in lines:
+        line.service()
     line_q.finish()
     gather = PlaneGather(pc, lambda q: columns_of(qo_first, q, nf, wide), qs, qr)
-    fill = pltpu.make_async_copy(qz.at[:, 0], columns_of(qo_first, pc.me, nf, wide), lsem.at[3])
-    fill.start()
-    fill.wait()
+    columns_of(qo_first, pc.me, nf, wide)[...] = qz[:, 0]
     gather.start()
-    line_gu.service()
     for step in range(1, min(6, pc.count)):
         gather.before(step)
-    line_gu.service()
+    for line in lines:
+        line.service()
     for step in range(min(6, pc.count), pc.count):
         gather.before(step)
     gather.finish()
+    for y in range(1, ns):
+        for f in range(nf):
+            arrived(y, f)
     for y in range(ns):
         for f in range(nf):
             e, c = piece(y, f)
@@ -726,7 +781,8 @@
     for i, c in enumerate(across):
         if i % 3:
             c.wait()
-    line_gu.finish()
+    for line in lines:
+        line.finish()
 
 
 def gather_weights(dims, w, wq, wo, wd, small):
@@ -752,7 +808,7 @@
         "gather_weights",
         0,
         outs,
-        [AN] * 6,
+        [AN, AN, AN, VM, VM, AN],
         [VM, VM, VM, AN, AN],
         [
             pltpu.VMEM((ns, nf, dr, two_ff), BF),
@@ -763,10 +819,9 @@
             dma((count,)),
             dma((3 * (ns - 1),)),
             dma((3 * (ns - 1),)),
-            dma((count - 1,)),
-            dma((count - 1,)),
         ]
-        + gather_scratch(dims) * 2,
+        + gather_sems(dims)
+        + gather_scratch(dims) * (1 + nf),
         (w, wq, wo, wd, small),
     )
 
@@ -858,10 +913,9 @@
     gather = None
     if carry:
         gather = PlaneGather(pc, slot, *refs)
-        fill = pltpu.make_async_copy(own, slot(pc.me), qsem.at[2])
-        fill.start()
-        fill.wait()
+        slot(pc.me)[...] = own[...]
         gather.start()
+    each(riders, "start")
     g1, g2, bias = gains_of(padded_t(small_ref[layer]), width, w.shape[1])
     hidden = h_ref[...].astype(BF).astype(F32)
     normed = (hidden * rms(hidden) * g1).astype(BF)
@@ -897,7 +951,7 @@
         q_ref[head, half:, :] = (r2 * scale).astype(BF)
     for c in sends:
         c.wait()
-    each(riders, "start")
+    each(riders, "service")
     for g in range(KVH):
         keys = [kv_ref[j, g].T for j in range(nk)]
         values = [kv_ref[j, KVH + g] for j in range(nk)]
@@ -963,8 +1017,8 @@
         "attention_forward",
         cid,
         tuple(outs),
-        [VM] * 7 + plan.places + [AN],
-        [VM] * 6 + [AN, AN] + plan.places,
+        [VM] * 7 + plan.outs + [VM],
+        [VM] * 6 + [AN, VM] + plan.places,
         [
             pltpu.VMEM((width, qkv), BF),
             pltpu.VMEM((width, width), BF),
@@ -972,10 +1026,10 @@
             pltpu.VMEM((qkv, rows), F32),
             dma((nk - 1,)),
             dma((nk - 1,)),
-            dma((3,)),
+            dma((2,)),
         ]
         + plan.scratch
-        + [dma((count - 1,))] * 2,
+        + gather_sems(dims),
         (hidden, small, meta, docs, cos_part, sin_part, qo_all, block, *plan.arrays),
     )
     return (out[:7], out[7:])
@@ -999,11 +1053,16 @@
     width, rows = h_ref.shape
     qkv = w.shape[1]
     loads = load_qo(qo_all, w, wo, qsem)
-    greet(pc, "all" if carry == "columns" else "mates", True)
     riders, refs = plan.board(pc, ins, outs, refs)
     if carry == "columns":
-        part = lambda q: columns_of(parts_ref, q, pc.nf, out_ref.shape[2])
-        hand_out = RowSends(pc, 1, rows_ref, refs[4:])
+        held, held_sem = refs[7:]
+        coming = pltpu.make_async_copy(parts_ref, held, held_sem)
+        coming.start()
+    greet(pc, "all" if carry == "columns" else "mates", True)
+    if carry == "columns":
+        part = lambda q: columns_of(held, q, pc.nf, out_ref.shape[2])
+        hand_out = RowSends(pc, 1, rows_ref, refs[4:7])
+        coming.wait()
     else:
         part = lambda q: parts_ref.at[q]
     scatter = ReadyScatter(pc, part, *refs[:4])
@@ -1131,8 +1190,8 @@
         "attention_backward",
         cid,
         tuple(outs),
-        [VM] * 3 + plan.places + places,
-        [VM] * 12 + [AN] + [VM] * len(late) + plan.places,
+        [VM] * 3 + plan.outs + places,
+        [VM] * 12 + [AN] + [AN if carry == "columns" else VM, VM] + plan.places,
         [
             pltpu.VMEM((width, qkv), BF),
             pltpu.VMEM((width, width), BF),
@@ -1148,7 +1207,11 @@
         ]
         + plan.scratch
         + scatter_scratch(dims, *summed)[2:]
-        + (row_scratch(dims) if carry == "columns" else []),
+        + (
+            row_scratch(dims) + [pltpu.VMEM(late[0].shape, BF), dma(())]
+            if carry == "columns"
+            else []
+        ),
         (g, small, meta, docs, cos_part, sin_part, hidden, normed, q, kv, lse, mixed, qo_all,
          *late, *plan.arrays),
     )
@@ -1175,14 +1238,14 @@
 def feed_forward_kernel(dims, plan, x_ref, res_ref, wgu_ref, wd_ref, *refs):
     n = plan.count
     ins, refs = (refs[:n], refs[n:])
-    out_ref, x_all, gu_all = refs[:3]
+    out_ref, x_out, gu_out = refs[:3]
     outs, refs = (refs[3 : 3 + n], refs[3 + n :])
-    wgu_t, wd_t, gu, inner, near, away, back, hop, ss, sr, gs, gr = refs[:12]
+    x_all, gu_all, lsem, wgu_t, wd_t, gu, inner, near, away, back, hop, ss, sr, gs, gr = refs[:15]
     pc = Place(dims)
     width, rows = x_ref.shape
     ff = wd_ref.shape[0]
+    riders, _ = plan.board(pc, ins, outs, refs[15:])
     greet(pc, "mates", n > 0)
-    riders, _ = plan.board(pc, ins, outs, refs[12:])
     gather = PlaneGather(pc, lambda q: x_all.at[:, lanes(q, rows)], gs, gr)
     scatter = PlaneScatter(pc, near, away, back, hop, ss, sr)
     x_all[:, lanes(pc.me, rows)] = x_ref[...]
@@ -1232,6 +1295,11 @@
         return carry
 
     lax.fori_loop(0, pc.count, step_body, 0)
+    leaving = [
+        pltpu.make_async_copy(gu_all, gu_out, lsem.at[0]),
+        pltpu.make_async_copy(x_all, x_out, lsem.at[1]),
+    ]
+    each(leaving, "start")
     each(riders, "service")
 
     def store(total):
@@ -1239,6 +1307,7 @@
 
     scatter.result(store)
     gather.finish()
+    each(leaving, "wait")
     each(riders, "finish")
 
 
@@ -1258,16 +1327,19 @@
             sds((two_ff, count * rows), BF),
             *plan.shapes,
         ),
-        [VM] * 3 + plan.places,
+        [VM, AN, AN] + plan.outs,
         [VM] * 4 + plan.places,
         [
+            pltpu.VMEM((width, count * rows), BF),
+            pltpu.VMEM((two_ff, count * rows), BF),
+            dma((2,)),
             pltpu.VMEM((two_ff, width), BF),
             pltpu.VMEM((width, ff), BF),
             pltpu.VMEM((two_ff, rows), F32),
             pltpu.VMEM((ff, rows), BF),
         ]
         + scatter_scratch(dims, width, rows)
-        + [dma((count - 1,)), dma((count - 1,))]
+        + gather_sems(dims)
         + plan.scratch,
         (x, residual, wgu, wd, *plan.arrays),
     )
@@ -1275,23 +1347,29 @@
 
 
 def feed_backward_kernel(
-    dims, layer, plan, g_ref, res_ref, x_all, gu_all, wgu_ref, wd_ref, small_ref, *refs
+    dims, layer, plan, g_ref, res_ref, x_in, gu_in, wgu_ref, wd_ref, small_ref, *refs
 ):
     n = plan.count
     ins, refs = (refs[:n], refs[n:])
     gr_ref, dwgu_ref, dwd_ref, dsmall_ref = refs[:4]
     outs, refs = (refs[4 : 4 + n], refs[4 + n :])
-    g_all, inner, ggu, gi, near, away, back, hop, ss, sr, gs, gr = refs[:12]
+    x_all, gu_all, lsem, g_all, inner, ggu, gi, near, away, back, hop, ss, sr, gs, gr = refs[:15]
+    coming = [
+        pltpu.make_async_copy(gu_in, gu_all, lsem.at[0]),
+        pltpu.make_async_copy(x_in, x_all, lsem.at[1]),
+    ]
+    each(coming, "start")
     pc = Place(dims)
     width, rows = g_ref.shape
     ff = wd_ref.shape[0]
+    riders, _ = plan.board(pc, ins, outs, refs[15:])
     greet(pc, "mates", n > 0)
-    riders, _ = plan.board(pc, ins, outs, refs[12:])
     gather = PlaneGather(pc, lambda q: g_all.at[:, lanes(q, rows)], gs, gr)
     scatter = PlaneScatter(pc, near, away, back, hop, ss, sr)
     g_all[:, lanes(pc.me, rows)] = g_ref[...].astype(BF)
     gather.start()
     each(riders, "start")
+    coming[0].wait()
     sequence, diagonal_at, early_at = sequence_of(pc)
     chunk = 32 if ff % 32 == 0 else 16
 
@@ -1340,6 +1418,7 @@
     each(riders, "service")
     dwd_ref[...] = nt(inner[...], g_all[...]).astype(BF)
     scatter.late()
+    coming[1].wait()
     part = width // 2
     for r in range(2):
         dwgu_ref[r * part : (r + 1) * part, :] = nt(
@@ -1379,16 +1458,19 @@
             sds((width // 128, 128), F32),
             *plan.shapes,
         ),
-        [VM] * 4 + plan.places,
-        [VM] * 7 + plan.places,
+        [VM] * 4 + plan.outs,
+        [VM, VM, AN, AN, VM, VM, VM] + plan.places,
         [
+            pltpu.VMEM((width, count * rows), BF),
+            pltpu.VMEM((two_ff, count * rows), BF),
+            dma((2,)),
             pltpu.VMEM((width, count * rows), BF),
             pltpu.VMEM((ff, count * rows), BF),
             pltpu.VMEM((two_ff, count * rows), BF),
             pltpu.VMEM((ff, rows), F32),
         ]
         + scatter_scratch(dims, width, rows)
-        + [dma((count - 1,)), dma((count - 1,))]
+        + gather_sems(dims)
         + plan.scratch,
         (g, residual, x_all, gu_all, wgu, wd, small, *plan.arrays),
     )
@@ -1505,7 +1587,7 @@
             pltpu.VMEM((ff, rows), F32),
         ]
         + scatter_scratch(dims, width, rows)
-        + [dma((count - 1,)), dma((count - 1,))],
+        + gather_sems(dims),
         (x, residual, g, g_all, wgu, wd, small),
     )
 

time: 564 us -> 517 us (0.917)
  Pallas kernels: 544 us -> 492 us
    pallas_call x9, Pallas kernels: 536 us -> 484 us  [call(): pl.pallas_call(kernel, name=name, out_shape=outs, in_specs=in_specs, out_...]
  transfers between devices with their start and end apart: 2 -> 2, of which waited for: 0 -> 0; matrix products, arithmetic and copies ran while one was open for 0% -> 0% of each run, Pallas kernels for 32% -> 35%
where the time goes in v6:
time: 517 us; the launch traced here: 508 us
  Pallas kernels  492 us (95%)
  other arithmetic  9.01 us (2%)
    pallas_call x9, Pallas kernels, call(): pl.pallas_call(kernel, name=name, out_shape=outs, in_specs=in_specs, out_...  484 us
  transfers between devices with their start and end apart: 2, of which 0 were waited for; matrix products, arithmetic and copies ran while one was open for 0% of the time, Pallas kernels for 35%

profile of v6, /device:TPU:0, one launch (start us, length us, event | category | flops | bytes accessed | tf_op | source)
XLA Modules:
  0.0 508.4 jit_solution(5993089991893280261)
XLA Ops:
  0.7 0.1 broadcast_in_dim.16
  0.8 0.1 broadcast_in_dim.17
  0.9 0.7 fusion.1
  1.6 0.7 convert_reduce_fusion
  2.3 0.6 gather_fusion
  2.9 0.6 constant_dynamic-slice_fusion.2.docs_ref
  3.4 0.7 reduce
  4.1 0.7 reduce.1
  4.8 0.7 reduce.2
  5.5 1.2 constant_dynamic-slice_fusion
  6.8 0.2 copy.21
  7.0 0.2 copy.22
  7.2 1.0 convert_bitcast_fusion.h_ref
  8.2 1.0 bitcast_convert_fusion.g_ref
  9.2 0.7 broadcast_select_fusion.meta_ref
  9.9 0.8 multiply_sine_fusion
  10.7 0.6 fusion.small
  11.3 75.1 %gather_weights.1 = (bf16[2,4,56,1216]{3,2,1,0:T(8,128)(2,1)}, bf16[2,152,896]{2,1,0:T(8,128)(2,1)}, bf16[4,4,56,1216]{3,2,1,0:T(8,128)(2,1)}, bf16[4,4,56,2048]...) custom-call(bf16[1,56,9728]{2,1,0:T(8,128)(2,1)} %w_ref.1, bf16[1,56,1152]{2,1,0:T(8,128)(2,1)} %wq_ref.1, ...), custom_call_target="tpu_custom_call" | custom-call | tf_op jit(solution)/shard_map/gather_weights/pallas_call | solution.py:658
  86.4 38.0 %attention_forward.2 = (bf16[896,256]{1,0:T(8,128)(2,1)}, bf16[14,64,256]{2,1,0:T(8,128)(2,1)}, bf16[3,4,64,256]{3,2,1,0:T(8,128)(2,1)}, f32[14,1,256]{2,1,0:T(1...) custom-call(f32[896,256]{1,0:T(8,128)} %convert_bitcast_fusion.h_ref, ...), custom_call_target="tpu_custom_call" | custom-call | tf_op jit(solution)/shard_map/attention_forward/pallas_call | solution.py:658
  124.4 49.2 %feed_forward.1 = (f32[896,256]{1,0:T(8,128)}, bf16[896,2048]{1,0:T(8,128)(2,1)}, bf16[1216,2048]{1,0:T(8,128)(2,1)}, bf16[4,4,56,1216]{3,2,1,0:T(8,128)(2,1)}) custom-call(bf16[896,256]{1,0:T(8,128)(2,1)} %get-tuple-element.67.x_ref, f32[896,256]{1,0:T(8,128)} %get-tuple-element.68.res_ref, bf16[896,1216]{1,0:T(8,128)(2,1)} %bitcast.33, ...), custom_call_target="tpu_custom_call" | custom-call | tf_op jit(solution)/shard_map/feed_forward/pallas_call | solution.py:658
  173.6 36.7 %attention_forward.3 = (bf16[896,256]{1,0:T(8,128)(2,1)}, bf16[14,64,256]{2,1,0:T(8,128)(2,1)}, bf16[3,4,64,256]{3,2,1,0:T(8,128)(2,1)}, f32[14,1,256]{2,1,0:T(1...) custom-call(f32[896,256]{1,0:T(8,128)} %get-tuple-element.72.h_ref.o, ...), custom_call_target="tpu_custom_call" | custom-call | tf_op jit(solution)/shard_map/attention_forward/pallas_call | solution.py:658
  210.3 60.0 %feed_both.1 = (f32[896,256]{1,0:T(8,128)}, bf16[896,1216]{1,0:T(8,128)(2,1)}, bf16[608,896]{1,0:T(8,128)(2,1)}, f32[7,128]{1,0:T(8,128)}, bf16[8,896,256]{2,1,0:T(8,128)(2,1)}) custom-call(bf16[896,256]{1,0:T(8,128)(2,1)} %get-tuple-element.74.x_ref, f32[896,256]{1,0:T(8,128)} %get-tuple-element.75.res_ref.refs_1_, f32[896,256]{1,0:T(8,128)} %bitcast_convert_fusion.g_ref, ...), custom_call_target="tpu_custom_call" | custom-call | tf_op jit(solution)/shard_map/feed_both/pallas_call | solution.py:658
  270.2 45.7 %attention_backward.2 = (f32[896,256]{1,0:T(8,128)}, bf16[896,2048]{1,0:T(8,128)(2,1)}, f32[16,128]{1,0:T(8,128)}, bf16[152,896]{1,0:T(8,128)(2,1)}, f32[896,256]{1,0:T(8,128)}) custom-call(f32[896,256]{1,0:T(8,128)} %get-tuple-element.79.g_ref, f32[2,24,128]{2,1,0:T(8,128)} %get-tuple-element.63.small_ref, f32[6,128]{1,0:T(8,128)} %broadcast_select_fusion.meta_ref, ...), custom_call_target="tpu_custom_call" | custom-call | tf_op jit(solution)/shard_map/attention_backward/pallas_call | solution.py:658
  316.0 1.3 select_convert_fusion.1
  317.3 54.2 %feed_backward.1 = (f32[896,256]{1,0:T(8,128)}, bf16[896,1216]{1,0:T(8,128)(2,1)}, bf16[608,896]{1,0:T(8,128)(2,1)}, f32[7,128]{1,0:T(8,128)}, bf16[4,56,1216]{2,1,0:T(8,128)(2,1)}) custom-call(f32[896,256]{1,0:T(8,128)} %get-tuple-element.87.g_ref.gh1, f32[896,256]{1,0:T(8,128)} %get-tuple-element.68.res_ref, bf16[896,2048]{1,0:T(8,128)(2,1)} %get-tuple-element.88.x_in, ...), custom_call_target="tpu_custom_call" | custom-call | tf_op jit(solution)/shard_map/feed_backward/pallas_call | solution.py:658
  371.6 56.6 %attention_backward.3 = (f32[896,256]{1,0:T(8,128)}, bf16[896,2048]{1,0:T(8,128)(2,1)}, f32[16,128]{1,0:T(8,128)}, bf16[152,896]{1,0:T(8,128)(2,1)}, bf16[2,56,1...) custom-call(f32[896,256]{1,0:T(8,128)} %get-tuple-element.91.g_ref, ...), custom_call_target="tpu_custom_call" | custom-call | tf_op jit(solution)/shard_map/attention_backward/pallas_call | solution.py:658
  428.2 0.1 select_convert_fusion
  428.3 2.1 collective-permute-start.1
  430.4 68.7 %reduce_gradients.1 = (f32[2,56,1024]{2,1,0:T(8,128)}, f32[48,128]{1,0:T(8,128)}, bf16[8,56,1216]{2,1,0:T(8,128)(2,1)}, bf16[2,152,896]{2,1,0:T(8,128)(2,1)}) custom-call(bf16[4,4,56,2048]{3,2,1,0:T(8,128)(2,1)} %bitcast.38, bf16[4,56,1024]{2,1,0:T(8,128)(2,1)} %get-tuple-element.102.terms, f32[16,128]{1,0:T(8,128)} %get-tuple-element.103.sa0, ...), custom_call_target="tpu_custom_call" | custom-call | tf_op jit(solution)/shard_map/reduce_gradients/pallas_call | solution.py:658
  499.2 0.7 copy-done.3
  499.9 0.2 copy-done.4
  500.1 7.9 %lay_out.1 = (f32[1,2,256,896]{3,2,1,0:T(8,128)}, f32[1,2,256,896]{3,2,1,0:T(8,128)}, f32[1,896]{1,0:T(1,128)}, f32[1,56,1152]{2,1,0:T(8,128)}, f32[1,1152]{1,0:...) custom-call(bf16[8,56,1216]{2,1,0:T(8,128)(2,1)} %get-tuple-element.110.gu, ...), custom_call_target="tpu_custom_call" | custom-call | tf_op jit(solution)/shard_map/lay_out/pallas_call | solution.py:1794
  (17 shorter events, 0.2 us)
Async XLA Ops:
  7.0 79.4 %copy-start.2 = (bf16[1,256,896]{1,2,0:T(8,128)(2,1)}, bf16[1,256,896]{1,2,0:T(8,128)(2,1)S(1)}, u32[]{:S(2)}) copy-start(bf16[1,256,896]{1,2,0:T(8,128)(2,1)S(1)} %copy.21) | copy-start | bytes 1376260
  270.2 45.7 %copy-start = (f32[896,256]{1,0:T(8,128)S(1)}, f32[896,256]{1,0:T(8,128)}, u32[]{:S(2)}) copy-start(f32[896,256]{1,0:T(8,128)} %get-tuple-element.72.h_ref.out0) | copy-start | bytes 2752516
  317.2 181.9 %collective-permute-start = (bf16[896,256]{1,0:T(8,128)(2,1)S(1)}, bf16[896,256]{1,0:T(8,128)(2,1)S(1)}, u32[]{:S(2)}, u32[]{:S(2)}) collective-permute-start(bf16[896,256]{1,0:T(8,128)(2,1)S(1)} %select_convert_fusion.1), channel_id=1, source_target_pairs={{0,16},{16,0},{1,17},{17,1},{2,18},{18,2},{3,19},{19,3},{4,20},{20... | collective-permute-start | bytes 1376264 | tf_op jit(solution)/shard_map/ppermute | solution.py:1904
  371.6 56.6 %copy-start.1 = (f32[896,256]{1,0:T(8,128)S(1)}, f32[896,256]{1,0:T(8,128)}, u32[]{:S(2)}) copy-start(f32[896,256]{1,0:T(8,128)} %get-tuple-element.87.g_ref.gh1) | copy-start | bytes 2752516
  428.3 70.9 %collective-permute-start.1 = (bf16[896,256]{1,0:T(8,128)(2,1)S(1)}, bf16[896,256]{1,0:T(8,128)(2,1)S(1)}, u32[]{:S(2)}, u32[]{:S(2)}) collective-permute-start(bf16[896,256]{1,0:T(8,128)(2,1)S(1)} %select_convert_fusion), channel_id=1, source_target_pairs={{0,16},{16,0},{1,17},{17,1},{2,18},{18,2},{3,19},{19,3},{4,20},{20... | collective-permute-start | bytes 1376264 | tf_op jit(solution)/shard_map/ppermute | solution.py:1904
  499.2 0.8 copy-start.3
  499.2 0.9 copy-start.4

commit v7 on v6

--- a/solution.py
+++ b/solution.py
@@ -897,8 +897,8 @@
     outs, refs = (refs[7 : 7 + n], refs[7 + n :])
     if carry:
         block_all, refs = (refs[0], refs[1:])
-    w, wo, mask, joined, ssem, rsem, qsem = refs[:7]
-    refs = refs[7:]
+    w, wo, mask, joined, top_own, sum_own, out_own, ssem, rsem, qsem = refs[:10]
+    refs = refs[10:]
     pc = Place(dims)
     width, rows = h_ref.shape
     loads = load_qo(qo_all, w, wo, qsem)
@@ -949,36 +949,53 @@
         r1, r2 = turned(head * HD)
         q_ref[head, :half, :] = (r1 * scale).astype(BF)
         q_ref[head, half:, :] = (r2 * scale).astype(BF)
+    for g in range(KVH):
+        keys = kv_ref[0, g].T
+        values = kv_ref[0, KVH + g]
+
+        def own_keys(i, carried):
+            head = g * GROUP + i
+            x = nn(keys, q_ref[head]) + mask[0]
+            top = x.max(axis=0, keepdims=True)
+            e = jnp.exp(x - top)
+            top_own[head] = top
+            sum_own[head] = e.sum(axis=0, keepdims=True)
+            out_own[head] = nn(values, e.astype(BF))
+            return carried
+
+        lax.fori_loop(0, GROUP, own_keys, 0)
     for c in sends:
         c.wait()
     each(riders, "service")
     for g in range(KVH):
-        keys = [kv_ref[j, g].T for j in range(nk)]
-        values = [kv_ref[j, KVH + g] for j in range(nk)]
+        keys = [kv_ref[j, g].T for j in range(1, nk)]
+        values = [kv_ref[j, KVH + g] for j in range(1, nk)]
 
         def one_head(i, carried):
             head = g * GROUP + i
             q = q_ref[head]
-            s = [nn(keys[j], q) + mask[j] for j in range(nk)]
-            top = s[0].max(axis=0, keepdims=True)
-            for j in range(1, nk):
-                top = jnp.maximum(top, s[j].max(axis=0, keepdims=True))
+            s = [nn(keys[j], q) + mask[j + 1] for j in range(nk - 1)]
+            first = top_own[head]
+            top = first
+            for x in s:
+                top = jnp.maximum(top, x.max(axis=0, keepdims=True))
             e = [jnp.exp(x - top) for x in s]
-            total = e[0].sum(axis=0, keepdims=True)
-            for j in range(1, nk):
+            fade = jnp.exp(first - top)
+            total = sum_own[head] * fade
+            out = out_own[head] * fade
+            for j in range(nk - 1):
                 total = total + e[j].sum(axis=0, keepdims=True)
-            out = nn(values[0], e[0].astype(BF))
-            for j in range(1, nk):
                 out = out + nn(values[j], e[j].astype(BF))
             lse_ref[head] = top + jnp.log(total)
             mixed_ref[head] = (out / total).astype(BF)
             return carried
 
         lax.fori_loop(0, GROUP, one_head, 0)
-        each(riders, "service")
-        if carry and g == 0:
+        if g == 0:
             for step in range(1, min(6, pc.count)):
                 gather.before(step)
+        else:
+            each(riders, "service")
     mixed = mixed_ref[...].reshape(H * HD, rows)
     loads[1].wait()
     residual = hidden + tn(wo[...], mixed)
@@ -1024,6 +1041,9 @@
             pltpu.VMEM((width, width), BF),
             pltpu.VMEM((nk, rows, rows), F32),
             pltpu.VMEM((qkv, rows), F32),
+            pltpu.VMEM((H, 1, rows), F32),
+            pltpu.VMEM((H, 1, rows), F32),
+            pltpu.VMEM((H, HD, rows), F32),
             dma((nk - 1,)),
             dma((nk - 1,)),
             dma((2,)),
@@ -1047,8 +1067,8 @@
     out_ref, refs = (refs[0], refs[1:])
     if carry == "columns":
         rows_ref, refs = (refs[0], refs[1:])
-    w, wo, mask, dmix, dkv, out_kv, in_kv, gj, ssem, rsem, qsem = refs[:11]
-    refs = refs[11:]
+    w, wo, mask, dmix, dkv, delta, dq_some, out_kv, in_kv, gj, ssem, rsem, qsem = refs[:13]
+    refs = refs[13:]
     pc = Place(dims)
     width, rows = h_ref.shape
     qkv = w.shape[1]
@@ -1088,37 +1108,36 @@
     def unturned(d1, d2):
         return (d1 * cos_part + d2 * sin_part, d2 * cos_part - d1 * sin_part)
 
+    def of_block(j, g, head, keys, keys_t, values):
+        q = q_ref[head]
+        do = dmix[head]
+        p = jnp.exp(nn(keys, q) + mask[j] - lse_ref[head])
+        ds = (p * (nn(values, do) - delta[head])).astype(BF)
+        dkv[j, g] += nt(q, ds)
+        dkv[j, KVH + g] += nt(do, p.astype(BF))
+        return nn(keys_t, ds)
+
     for g in range(KVH):
-        keys_t = [kv_ref[j, g] for j in range(nk)]
+        keys_t = [kv_ref[j, g] for j in range(1, nk)]
         keys = [k.T for k in keys_t]
-        values = [kv_ref[j, KVH + g].T for j in range(nk)]
-
-        def one_head(i, carried):
+        values = [kv_ref[j, KVH + g].T for j in range(1, nk)]
+
+        def earlier(i, carried):
             head = g * GROUP + i
-            q = q_ref[head]
-            do = dmix[head]
-            lse = lse_ref[head]
-            p = [jnp.exp(nn(keys[j], q) + mask[j] - lse) for j in range(nk)]
-            dp = [nn(values[j], do) for j in range(nk)]
-            delta = (p[0] * dp[0]).sum(axis=0, keepdims=True)
-            for j in range(1, nk):
-                delta = delta + (p[j] * dp[j]).sum(axis=0, keepdims=True)
-            dq = jnp.zeros((HD, rows), F32)
-            for j in range(nk):
-                ds = (p[j] * (dp[j] - delta)).astype(BF)
-                dkv[j, g] += nt(q, ds)
-                dkv[j, KVH + g] += nt(do, p[j].astype(BF))
-                dq = dq + nn(keys_t[j], ds)
-            dq = dq * scale
-            r1, r2 = unturned(dq[:half], dq[half:])
-            gj[pl.ds(pl.multiple_of(head * HD, HD), half), :] = r1.astype(BF)
-            gj[pl.ds(pl.multiple_of(head * HD + half, half), half), :] = r2.astype(BF)
+            delta[head] = (dmix[head].astype(F32) * mixed_ref[head].astype(F32)).sum(
+                axis=0, keepdims=True
+            )
+            dq = of_block(1, g, head, keys[0], keys_t[0], values[0])
+            for j in range(2, nk):
+                dq = dq + of_block(j, g, head, keys[j - 1], keys_t[j - 1], values[j - 1])
+            dq_some[head] = dq
             return carried
 
-        lax.fori_loop(0, GROUP, one_head, 0)
-        each(riders, "service")
+        lax.fori_loop(0, GROUP, earlier, 0)
         if g == 0:
             scatter.late()
+        if g == 1 or carry == "sum":
+            each(riders, "service")
     for j in range(1, nk):
         out_kv[j - 1] = dkv[j].astype(BF)
     sends = [
@@ -1128,8 +1147,23 @@
     ]
     for c in sends:
         c.start()
+    for g in range(KVH):
+        keys_t = kv_ref[0, g]
+        keys = keys_t.T
+        values = kv_ref[0, KVH + g].T
+
+        def own_keys(i, carried):
+            head = g * GROUP + i
+            dq = (dq_some[head] + of_block(0, g, head, keys, keys_t, values)) * scale
+            r1, r2 = unturned(dq[:half], dq[half:])
+            gj[pl.ds(pl.multiple_of(head * HD, HD), half), :] = r1.astype(BF)
+            gj[pl.ds(pl.multiple_of(head * HD + half, half), half), :] = r2.astype(BF)
+            return carried
+
+        lax.fori_loop(0, GROUP, own_keys, 0)
     for c in sends:
         c.wait()
+    each(riders, "service")
     own = dkv[0]
     for j in range(1, nk):
         own = own + in_kv[j - 1].astype(F32)
@@ -1198,6 +1232,8 @@
             pltpu.VMEM((nk, rows, rows), F32),
             pltpu.VMEM((H, HD, rows), BF),
             pltpu.VMEM((nk,) + block, F32),
+            pltpu.VMEM((H, 1, rows), F32),
+            pltpu.VMEM((H, HD, rows), F32),
             pltpu.VMEM((nk - 1,) + block, BF),
             pltpu.VMEM((nk - 1,) + block, BF),
             pltpu.VMEM((qkv, rows), BF),
@@ -1593,35 +1629,18 @@
 
 
 def reduce_kernel(
-    dims, cut, qo, terms, sa0, sa1, sb0, sb1, wd1, wd0, gu0a, gu0,
+    dims, qo, terms, sa0, sa1, sb0, sb1, wd1, gu0a, gu0, wd0,
     qo_out, small_out, gu_got, wd_got,
-    gsum, small, sm_in, sm_mid, sm_line, z_out, mine, give,
+    held, rest_gu, gsum, wsum, small, sm_in, sm_mid, sm_line, z_out, mine, give,
     lsem, ws, wr, ls, lr, zs, zr, *rest
 ):
     pc = Place(dims)
     ns, nb, nf = dims
-    greet(pc, "all", True)
-    scatter = ReadyScatter(
-        pc, lambda q: columns_of(qo, q, nf, z_out.shape[2]), *rest[15:19]
-    )
-    scatter.start()
-
-    def keep(value):
-        gsum[...] = value.astype(BF)
-
-    def keep_of(l):
-        def store(value):
-            mine[l] = value
-
-        return store
-
-    line = LineReduce(pc, lambda t: gu0[t, cut:nf], keep, rest[0:4])
-    ends = [
-        LineReduce(pc, lambda t: z_out[t], keep_of(0), rest[4:8]),
-        LineReduce(pc, lambda t: terms[t], keep_of(1), rest[8:12]),
-    ]
-    line.start()
-    ends[1].start()
+    coming = pltpu.make_async_copy(qo, held, lsem.at[1])
+    coming.start()
+    cut = gu0a.shape[0]
+    coming_gu = pltpu.make_async_copy(gu0.at[:, cut:nf], rest_gu, lsem.at[2])
+    coming_gu.start()
     n1 = sb0.shape[0]
     per = small.shape[0] // ns
     nr = sa0.shape[0] + n1
@@ -1630,6 +1649,35 @@
         small[l * per : l * per + n1] = a[0:n1]
         small[l * per + n1 : l * per + 2 * n1] = g[...]
         small[l * per + 2 * n1 : l * per + nr] = a[n1 : a.shape[0]]
+    greet(pc, "all", True)
+
+    def keep(value):
+        wsum[...] = value.astype(BF)
+
+    def keep_of(l):
+        def store(value):
+            mine[l] = value
+
+        return store
+
+    line = LineReduce(pc, lambda t: wd0[t], keep, rest[0:4])
+    ends = [
+        LineReduce(pc, lambda t: z_out[t], keep_of(0), rest[4:8]),
+        LineReduce(pc, lambda t: terms[t], keep_of(1), rest[8:12]),
+    ]
+    def keep_gu(value):
+        gsum[...] = value.astype(BF)
+
+    line_gu = LineReduce(pc, lambda t: rest_gu[t], keep_gu, rest[19:23])
+    ends[1].start()
+    coming_gu.wait()
+    line_gu.start()
+    line.start()
+    scatter = ReadyScatter(
+        pc, lambda q: columns_of(held, q, nf, z_out.shape[2]), *rest[15:19]
+    )
+    coming.wait()
+    scatter.start()
     smalls = [
         remote(small, sm_in.at[e - 1], ls.at[e - 1], lr.at[e - 1], pc.plane(e))
         for e in range(1, pc.count)
@@ -1641,7 +1689,8 @@
     hand_out = RowSends(pc, 0, gu_got, rest[12:15])
     for f in range(cut):
         hand_out.start(f, gu0a.at[f])
-    for l, ref in ((0, wd0), (1, wd1)):
+
+    def split(l, ref):
         @pl.when(pc.s == l)
         def _():
             pltpu.make_async_copy(ref, wd_got.at[l], lsem.at[0]).start()
@@ -1650,9 +1699,12 @@
         def _():
             remote(ref, wd_got.at[pc.s], ws.at[0], wr.at[0], (l, pc.b, pc.f)).start()
 
+    split(1, wd1)
     ends[1].service()
+    line_gu.service()
+    line.service()
     scatter.late()
-    line.service()
+    ends[1].service()
     total = small[...]
     for e, c in enumerate(smalls):
         c.wait()
@@ -1664,6 +1716,8 @@
     ]
     for c in lines:
         c.start()
+    line_gu.service()
+    line.service()
 
     def store(value):
         z_out[...] = value.astype(BF)
@@ -1671,40 +1725,43 @@
     scatter.finish(store)
     ends[0].start()
     ends[1].finish()
-    line.service()
+    line_gu.finish()
+    for f in range(cut, nf):
+        hand_out.start(f, gsum.at[f - cut])
+    ends[0].service()
+    line.finish()
+    split(0, wsum)
     ends[0].finish()
     mate = (ns - 1 - pc.s, pc.b, pc.f)
     swap = remote(give.at[0], give.at[1], ws.at[1], wr.at[1], mate)
     give[0] = mine[ns - 1 - pc.s].astype(BF)
     swap.start()
     qo_out[pc.s] = mine[pc.s]
-    line.finish()
-    for f in range(cut, nf):
-        hand_out.start(f, gsum.at[f - cut])
     total = sm_mid[...]
     for d, c in enumerate(lines):
         c.wait()
         total = total + sm_line[d]
     small_out[...] = total
+    hand_out.finish(gu0a.at[0])
+    pltpu.make_async_copy(wsum, wd_got.at[pc.s], lsem.at[0]).wait()
+    remote(wsum, wd_got.at[pc.s], ws.at[0], wr.at[0], mate).wait()
     swap.wait()
     qo_out[ns - 1 - pc.s] = give[1].astype(F32)
-    hand_out.finish(gsum.at[0])
-    pltpu.make_async_copy(wd0, wd_got.at[pc.s], lsem.at[0]).wait()
-    remote(wd0, wd_got.at[pc.s], ws.at[0], wr.at[0], mate).wait()
-
-
-def reduce_gradients(dims, cid, cut, qo, terms, smalls, wd1, wd0, gu0a, gu0):
+
+
+def reduce_gradients(dims, cid, qo, terms, smalls, wd1, gu0a, gu0, wd0):
     ns, nb, nf = dims
     count = ns * nf
     dr, wide = terms.shape[1:]
     two_ff = gu0.shape[3]
-    half, width = wd0.shape
+    cut = gu0a.shape[0]
+    half, width = wd1.shape
     rows = smalls[0].shape[0] + smalls[2].shape[0]
     small = (ns * (-(-rows // 8) * 8), 128)
     sds = jax.ShapeDtypeStruct
     dma = pltpu.SemaphoreType.DMA
     return call(
-        functools.partial(reduce_kernel, dims, cut),
+        functools.partial(reduce_kernel, dims),
         "reduce_gradients",
         cid,
         (
@@ -1714,9 +1771,12 @@
             sds((ns, half, width), BF),
         ),
         [VM] * 4,
-        [VM] * 10,
+        [AN] + [VM] * 7 + [AN, VM],
         [
+            pltpu.VMEM(qo.shape, BF),
+            pltpu.VMEM((nb, nf - cut, dr, two_ff), BF),
             pltpu.VMEM((nf - cut, dr, two_ff), BF),
+            pltpu.VMEM((half, width), BF),
             pltpu.VMEM(small, F32),
             pltpu.VMEM((count - 1,) + small, F32),
             pltpu.VMEM(small, F32),
@@ -1724,7 +1784,7 @@
             pltpu.VMEM((nb, dr, wide), BF),
             pltpu.VMEM((ns, dr, wide), F32),
             pltpu.VMEM((2, dr, wide), BF),
-            dma((1,)),
+            dma((3,)),
             dma((2,)),
             dma((2,)),
             dma((count - 1,)),
@@ -1732,11 +1792,12 @@
             dma((nb - 1,)),
             dma((nb - 1,)),
         ]
-        + reduce_scratch(dims, nf - cut, dr, two_ff)
+        + reduce_scratch(dims, half, width)
         + reduce_scratch(dims, dr, wide) * 2
         + row_scratch(dims)
-        + scatter_scratch(dims, nb, dr, wide)[2:],
-        (qo, terms, *smalls, wd1, wd0, gu0a, gu0),
+        + scatter_scratch(dims, nb, dr, wide)[2:]
+        + reduce_scratch(dims, nf - cut, dr, two_ff),
+        (qo, terms, *smalls, wd1, gu0a, gu0, wd0),
     )
 
 
@@ -1882,7 +1943,6 @@
     line_wd = (nb, half, width)
     line_qo = (nb, nf, dr, cols)
     everything = (0, half)
-    cut = nf // 2
     b1 = feed_both(dims, 4, 1, a1[6], a1[5], g, g_all, wgu1, wd1, small_all)
     ab1, (dwd1, out1) = attention_backward(
         dims, nk, 7, 1, b1[0], *common, f0[0], *a1[:5], qo1,
@@ -1893,9 +1953,10 @@
         ride((("reduce", (0, nf)), b1[1].reshape(line_gu))),
     )
     dgu0 = b0[1].reshape(line_gu)
-    ab0, (dwd0, dgu0a, terms, gu_got1) = attention_backward(
+    cut = nf - nf // 4
+    ab0, (dgu0a, terms, gu_got1) = attention_backward(
         dims, nk, 8, 0, b0[0], *common, hidden, *a0[:5], qo0,
-        ride((("reduce", everything), b0[2].reshape(line_wd)), (("reduce", (0, cut)), dgu0)),
+        ride((("reduce", (0, cut)), dgu0)),
         "columns", (ab1[1].reshape(line_qo), dgu1),
     )
 
@@ -1906,8 +1967,8 @@
     take_out = swapped((f0[0], out1))
     take_grad = swapped((ab0[0], ab1[0]))
     grad_qo, small_sum, gu_got0, wd_got = reduce_gradients(
-        dims, 9, cut, ab0[1].reshape(line_qo), terms,
-        (ab0[2], ab1[2], b0[3], b1[3]), dwd1, dwd0, dgu0a, dgu0,
+        dims, 9, ab0[1].reshape(line_qo), terms,
+        (ab0[2], ab1[2], b0[3], b1[3]), dwd1, dgu0a, dgu0, b0[2].reshape(line_wd),
     )
     return lay_out(
         dims,

time: 517 us -> 503 us (0.973)
  Pallas kernels: 492 us -> 472 us
    pallas_call x9, Pallas kernels: 484 us -> 464 us  [call(): pl.pallas_call(kernel, name=name, out_shape=outs, in_specs=in_specs, out_...]
  transfers between devices with their start and end apart: 2 -> 2, of which waited for: 0 -> 0; matrix products, arithmetic and copies ran while one was open for 0% -> 0% of each run, Pallas kernels for 35% -> 33%
where the time goes in v7:
time: 503 us; the launch traced here: 494 us
  Pallas kernels  472 us (94%)
  other arithmetic  9.01 us (2%)
  starting transfers between devices  7.32 us (1%)
    pallas_call x9, Pallas kernels, call(): pl.pallas_call(kernel, name=name, out_shape=outs, in_specs=in_specs, out_...  464 us
  transfers between devices with their start and end apart: 2, of which 0 were waited for; matrix products, arithmetic and copies ran while one was open for 0% of the time, Pallas kernels for 33%

profile of v7, /device:TPU:0, one launch (start us, length us, event | category | flops | bytes accessed | tf_op | source)
XLA Modules:
  0.0 493.7 jit_solution(7891964343509727818)
XLA Ops:
  0.7 0.1 broadcast_in_dim.16
  0.8 0.1 broadcast_in_dim.17
  0.9 0.7 fusion.1
  1.6 0.7 convert_reduce_fusion
  2.3 0.6 gather_fusion
  2.9 0.6 constant_dynamic-slice_fusion.2.docs_ref
  3.4 0.7 reduce
  4.1 0.7 reduce.1
  4.8 0.7 reduce.2
  5.5 1.2 constant_dynamic-slice_fusion
  6.8 0.2 copy.21
  7.0 0.2 copy.22
  7.2 1.0 convert_bitcast_fusion.h_ref
  8.2 1.0 bitcast_convert_fusion.g_ref
  9.2 0.7 broadcast_select_fusion.meta_ref
  9.9 0.8 multiply_sine_fusion
  10.7 0.6 fusion.small
  11.3 75.1 %gather_weights.1 = (bf16[2,4,56,1216]{3,2,1,0:T(8,128)(2,1)}, bf16[2,152,896]{2,1,0:T(8,128)(2,1)}, bf16[4,4,56,1216]{3,2,1,0:T(8,128)(2,1)}, bf16[4,4,56,2048]...) custom-call(bf16[1,56,9728]{2,1,0:T(8,128)(2,1)} %w_ref.1, bf16[1,56,1152]{2,1,0:T(8,128)(2,1)} %wq_ref.1, ...), custom_call_target="tpu_custom_call" | custom-call | tf_op jit(solution)/shard_map/gather_weights/pallas_call | solution.py:658
  86.4 36.5 %attention_forward.2 = (bf16[896,256]{1,0:T(8,128)(2,1)}, bf16[14,64,256]{2,1,0:T(8,128)(2,1)}, bf16[3,4,64,256]{3,2,1,0:T(8,128)(2,1)}, f32[14,1,256]{2,1,0:T(1...) custom-call(f32[896,256]{1,0:T(8,128)} %convert_bitcast_fusion.h_ref, ...), custom_call_target="tpu_custom_call" | custom-call | tf_op jit(solution)/shard_map/attention_forward/pallas_call | solution.py:658
  122.9 48.7 %feed_forward.1 = (f32[896,256]{1,0:T(8,128)}, bf16[896,2048]{1,0:T(8,128)(2,1)}, bf16[1216,2048]{1,0:T(8,128)(2,1)}, bf16[4,4,56,1216]{3,2,1,0:T(8,128)(2,1)}) custom-call(bf16[896,256]{1,0:T(8,128)(2,1)} %get-tuple-element.66.x_ref, f32[896,256]{1,0:T(8,128)} %get-tuple-element.67.res_ref, bf16[896,1216]{1,0:T(8,128)(2,1)} %bitcast.33, ...), custom_call_target="tpu_custom_call" | custom-call | tf_op jit(solution)/shard_map/feed_forward/pallas_call | solution.py:658
  171.7 36.0 %attention_forward.3 = (bf16[896,256]{1,0:T(8,128)(2,1)}, bf16[14,64,256]{2,1,0:T(8,128)(2,1)}, bf16[3,4,64,256]{3,2,1,0:T(8,128)(2,1)}, f32[14,1,256]{2,1,0:T(1...) custom-call(f32[896,256]{1,0:T(8,128)} %get-tuple-element.71.h_ref.o, ...), custom_call_target="tpu_custom_call" | custom-call | tf_op jit(solution)/shard_map/attention_forward/pallas_call | solution.py:658
  207.7 60.6 %feed_both.1 = (f32[896,256]{1,0:T(8,128)}, bf16[896,1216]{1,0:T(8,128)(2,1)}, bf16[608,896]{1,0:T(8,128)(2,1)}, f32[7,128]{1,0:T(8,128)}, bf16[8,896,256]{2,1,0:T(8,128)(2,1)}) custom-call(bf16[896,256]{1,0:T(8,128)(2,1)} %get-tuple-element.73.x_ref, f32[896,256]{1,0:T(8,128)} %get-tuple-element.74.res_ref.refs_1_, f32[896,256]{1,0:T(8,128)} %bitcast_convert_fusion.g_ref, ...), custom_call_target="tpu_custom_call" | custom-call | tf_op jit(solution)/shard_map/feed_both/pallas_call | solution.py:658
  268.2 44.8 %attention_backward.2 = (f32[896,256]{1,0:T(8,128)}, bf16[896,2048]{1,0:T(8,128)(2,1)}, f32[16,128]{1,0:T(8,128)}, bf16[152,896]{1,0:T(8,128)(2,1)}, f32[896,256]{1,0:T(8,128)}) custom-call(f32[896,256]{1,0:T(8,128)} %get-tuple-element.78.g_ref, f32[2,24,128]{2,1,0:T(8,128)} %get-tuple-element.62.small_ref, f32[6,128]{1,0:T(8,128)} %broadcast_select_fusion.meta_ref, ...), custom_call_target="tpu_custom_call" | custom-call | tf_op jit(solution)/shard_map/attention_backward/pallas_call | solution.py:658
  313.0 1.3 select_convert_fusion.1
  314.4 52.7 %feed_backward.1 = (f32[896,256]{1,0:T(8,128)}, bf16[896,1216]{1,0:T(8,128)(2,1)}, bf16[608,896]{1,0:T(8,128)(2,1)}, f32[7,128]{1,0:T(8,128)}, bf16[4,56,1216]{2,1,0:T(8,128)(2,1)}) custom-call(f32[896,256]{1,0:T(8,128)} %get-tuple-element.86.g_ref.gh1, f32[896,256]{1,0:T(8,128)} %get-tuple-element.67.res_ref, bf16[896,2048]{1,0:T(8,128)(2,1)} %get-tuple-element.87.x_in, ...), custom_call_target="tpu_custom_call" | custom-call | tf_op jit(solution)/shard_map/feed_backward/pallas_call | solution.py:658
  367.1 51.4 %attention_backward.3 = (f32[896,256]{1,0:T(8,128)}, bf16[896,2048]{1,0:T(8,128)(2,1)}, f32[16,128]{1,0:T(8,128)}, bf16[3,56,1216]{2,1,0:T(8,128)(2,1)}, bf16[4,...) custom-call(f32[896,256]{1,0:T(8,128)} %get-tuple-element.90.g_ref, f32[2,24,128]{2,1,0:T(8,128)} %get-tuple-element.62.small_ref, ...), custom_call_target="tpu_custom_call" | custom-call | tf_op jit(solution)/shard_map/attention_backward/pallas_call | solution.py:658
  418.6 0.1 select_convert_fusion
  418.7 7.2 %collective-permute-start.1 = (bf16[896,256]{1,0:T(8,128)(2,1)S(1)}, bf16[896,256]{1,0:T(8,128)(2,1)S(1)}, u32[]{:S(2)}, u32[]{:S(2)}) collective-permute-start(bf16[896,256]{1,0:T(8,128)(2,1)S(1)} %select_convert_fusion), channel_id=1, source_target_pairs={{0,16},{16,0},{1,17},{17,1},{2,18},{18,2},{3,19},{19,3},{4,20},{20... | collective-permute-start | bytes 1376264 | tf_op jit(solution)/shard_map/ppermute | solution.py:1965
  425.9 58.7 %reduce_gradients.1 = (f32[2,56,1024]{2,1,0:T(8,128)}, f32[48,128]{1,0:T(8,128)}, bf16[8,56,1216]{2,1,0:T(8,128)(2,1)}, bf16[2,152,896]{2,1,0:T(8,128)(2,1)}) custom-call(bf16[4,4,56,2048]{3,2,1,0:T(8,128)(2,1)} %bitcast.38, bf16[4,56,1024]{2,1,0:T(8,128)(2,1)} %get-tuple-element.100.terms, f32[16,128]{1,0:T(8,128)} %get-tuple-element.101.sa0, ...), custom_call_target="tpu_custom_call" | custom-call | tf_op jit(solution)/shard_map/reduce_gradients/pallas_call | solution.py:658
  484.6 0.7 copy-done.3
  485.4 0.2 copy-done.4
  485.5 7.7 %lay_out.1 = (f32[1,2,256,896]{3,2,1,0:T(8,128)}, f32[1,2,256,896]{3,2,1,0:T(8,128)}, f32[1,896]{1,0:T(1,128)}, f32[1,56,1152]{2,1,0:T(8,128)}, f32[1,1152]{1,0:...) custom-call(bf16[8,56,1216]{2,1,0:T(8,128)(2,1)} %get-tuple-element.108.gu, ...), custom_call_target="tpu_custom_call" | custom-call | tf_op jit(solution)/shard_map/lay_out/pallas_call | solution.py:1855
  (17 shorter events, 0.2 us)
Async XLA Ops:
  7.0 79.4 %copy-start.2 = (bf16[1,256,896]{1,2,0:T(8,128)(2,1)}, bf16[1,256,896]{1,2,0:T(8,128)(2,1)S(1)}, u32[]{:S(2)}) copy-start(bf16[1,256,896]{1,2,0:T(8,128)(2,1)S(1)} %copy.21) | copy-start | bytes 1376260
  268.2 44.8 %copy-start = (f32[896,256]{1,0:T(8,128)S(1)}, f32[896,256]{1,0:T(8,128)}, u32[]{:S(2)}) copy-start(f32[896,256]{1,0:T(8,128)} %get-tuple-element.71.h_ref.out0) | copy-start | bytes 2752516
  314.3 170.3 %collective-permute-start = (bf16[896,256]{1,0:T(8,128)(2,1)S(1)}, bf16[896,256]{1,0:T(8,128)(2,1)S(1)}, u32[]{:S(2)}, u32[]{:S(2)}) collective-permute-start(bf16[896,256]{1,0:T(8,128)(2,1)S(1)} %select_convert_fusion.1), channel_id=1, source_target_pairs={{0,16},{16,0},{1,17},{17,1},{2,18},{18,2},{3,19},{19,3},{4,20},{20... | collective-permute-start | bytes 1376264 | tf_op jit(solution)/shard_map/ppermute | solution.py:1965
  367.1 51.5 %copy-start.1 = (f32[896,256]{1,0:T(8,128)S(1)}, f32[896,256]{1,0:T(8,128)}, u32[]{:S(2)}) copy-start(f32[896,256]{1,0:T(8,128)} %get-tuple-element.86.g_ref.gh1) | copy-start | bytes 2752516
  418.7 65.9 %collective-permute-start.1 = (bf16[896,256]{1,0:T(8,128)(2,1)S(1)}, bf16[896,256]{1,0:T(8,128)(2,1)S(1)}, u32[]{:S(2)}, u32[]{:S(2)}) collective-permute-start(bf16[896,256]{1,0:T(8,128)(2,1)S(1)} %select_convert_fusion), channel_id=1, source_target_pairs={{0,16},{16,0},{1,17},{17,1},{2,18},{18,2},{3,19},{19,3},{4,20},{20... | collective-permute-start | bytes 1376264 | tf_op jit(solution)/shard_map/ppermute | solution.py:1965
  484.6 0.8 copy-start.3
  484.6 0.9 copy-start.4

commit v8 on v7

--- a/solution.py
+++ b/solution.py
@@ -885,36 +885,44 @@
     return jnp.concatenate([v, jnp.zeros((128 - n, 128), v.dtype)], axis=0).T
 
 
-def attention_forward_kernel(
-    dims, nk, layer, plan, carry, h_ref, small_ref, meta_ref, docs_ref, cos_ref, sin_ref, qo_all,
+def attention_forward_kernel(dims, *args):
+    pc = Place(dims)
+    riders, gather = attention_forward_part(pc, *args)
+    last_blocks(pc, gather)
+    gather.finish()
+    each(riders, "finish")
+
+
+def last_blocks(pc, gather):
+    for step in range(min(6, pc.count), pc.count):
+        gather.before(step)
+
+
+def attention_forward_part(
+    pc, nk, layer, plan, carry, h_ref, small_ref, meta_ref, docs_ref, cos_ref, sin_ref, qo_all,
     *refs
 ):
     n = plan.count
-    if carry:
-        block_ref, refs = (refs[0], refs[1:])
+    block_ref, refs = (refs[0], refs[1:])
     ins, refs = (refs[:n], refs[n:])
     normed_ref, q_ref, kv_ref, lse_ref, mixed_ref, res_ref, n2_ref = refs[:7]
     outs, refs = (refs[7 : 7 + n], refs[7 + n :])
-    if carry:
-        block_all, refs = (refs[0], refs[1:])
+    block_all, refs = (refs[0], refs[1:])
     w, wo, mask, joined, top_own, sum_own, out_own, ssem, rsem, qsem = refs[:10]
     refs = refs[10:]
-    pc = Place(dims)
     width, rows = h_ref.shape
     loads = load_qo(qo_all, w, wo, qsem)
-    greet(pc, "mates" if carry else None, True)
+    greet(pc, "mates", True)
     riders, refs = plan.board(pc, ins, outs, refs)
     if carry == "lanes":
         own = block_ref
         slot = lambda q: block_all.at[:, lanes(q, rows)]
-    elif carry == "columns":
+    else:
         own = block_ref.at[:, 1]
         slot = lambda q: columns_of(block_all, q, pc.nf, block_ref.shape[3])
-    gather = None
-    if carry:
-        gather = PlaneGather(pc, slot, *refs)
-        slot(pc.me)[...] = own[...]
-        gather.start()
+    gather = PlaneGather(pc, slot, *refs)
+    slot(pc.me)[...] = own[...]
+    gather.start()
     each(riders, "start")
     g1, g2, bias = gains_of(padded_t(small_ref[layer]), width, w.shape[1])
     hidden = h_ref[...].astype(BF).astype(F32)
@@ -1001,11 +1009,23 @@
     residual = hidden + tn(wo[...], mixed)
     res_ref[...] = residual
     n2_ref[...] = (residual * rms(residual) * g2).astype(BF)
-    if carry:
-        for step in range(min(6, pc.count), pc.count):
-            gather.before(step)
-        gather.finish()
-    each(riders, "finish")
+    return (riders, gather)
+
+
+def attention_scratch(dims, nk, width, rows, qkv):
+    dma = pltpu.SemaphoreType.DMA
+    return [
+        pltpu.VMEM((width, qkv), BF),
+        pltpu.VMEM((width, width), BF),
+        pltpu.VMEM((nk, rows, rows), F32),
+        pltpu.VMEM((qkv, rows), F32),
+        pltpu.VMEM((H, 1, rows), F32),
+        pltpu.VMEM((H, 1, rows), F32),
+        pltpu.VMEM((H, HD, rows), F32),
+        dma((nk - 1,)),
+        dma((nk - 1,)),
+        dma((2,)),
+    ]
 
 
 def attention_forward(dims, nk, cid, layer, hidden, small, meta, docs, cos_part, sin_part, qo_all,
@@ -1024,7 +1044,6 @@
         sds((width, rows), F32),
         sds((width, rows), BF),
     ] + plan.shapes
-    dma = pltpu.SemaphoreType.DMA
     if carry == "lanes":
         outs.append(sds((width, count * rows), BF))
     else:
@@ -1036,18 +1055,7 @@
         tuple(outs),
         [VM] * 7 + plan.outs + [VM],
         [VM] * 6 + [AN, VM] + plan.places,
-        [
-            pltpu.VMEM((width, qkv), BF),
-            pltpu.VMEM((width, width), BF),
-            pltpu.VMEM((nk, rows, rows), F32),
-            pltpu.VMEM((qkv, rows), F32),
-            pltpu.VMEM((H, 1, rows), F32),
-            pltpu.VMEM((H, 1, rows), F32),
-            pltpu.VMEM((H, HD, rows), F32),
-            dma((nk - 1,)),
-            dma((nk - 1,)),
-            dma((2,)),
-        ]
+        attention_scratch(dims, nk, width, rows, qkv)
         + plan.scratch
         + gather_sems(dims),
         (hidden, small, meta, docs, cos_part, sin_part, qo_all, block, *plan.arrays),
@@ -1271,21 +1279,26 @@
         dst[c0:c1, :] = src[:, c0:c1].T
 
 
-def feed_forward_kernel(dims, plan, x_ref, res_ref, wgu_ref, wd_ref, *refs):
+def feed_forward_kernel(dims, *args):
+    pc = Place(dims)
+    feed_forward_part(pc, lambda: greet(pc, "mates", True), lambda: None, *args)
+
+
+def feed_forward_part(pc, enter, ready, plan, x_ref, res_ref, wgu_ref, wd_ref, *refs):
     n = plan.count
     ins, refs = (refs[:n], refs[n:])
     out_ref, x_out, gu_out = refs[:3]
     outs, refs = (refs[3 : 3 + n], refs[3 + n :])
     x_all, gu_all, lsem, wgu_t, wd_t, gu, inner, near, away, back, hop, ss, sr, gs, gr = refs[:15]
-    pc = Place(dims)
     width, rows = x_ref.shape
     ff = wd_ref.shape[0]
     riders, _ = plan.board(pc, ins, outs, refs[15:])
-    greet(pc, "mates", n > 0)
+    enter()
     gather = PlaneGather(pc, lambda q: x_all.at[:, lanes(q, rows)], gs, gr)
     scatter = PlaneScatter(pc, near, away, back, hop, ss, sr)
     x_all[:, lanes(pc.me, rows)] = x_ref[...]
     gather.start()
+    ready()
     each(riders, "start")
     transpose_into(wgu_t, wgu_ref)
     transpose_into(wd_t, wd_ref)
@@ -1513,19 +1526,24 @@
     return (out[:4], out[4:])
 
 
-def feed_both_kernel(
-    dims, layer, x_ref, res_ref, g_ref, g_all, wgu_ref, wd_ref, small_ref,
+def feed_both_kernel(dims, *args):
+    pc = Place(dims)
+    feed_both_part(pc, lambda: greet(pc, "mates", False), lambda: None, *args)
+
+
+def feed_both_part(
+    pc, enter, ready, layer, x_ref, res_ref, g_ref, g_all, wgu_ref, wd_ref, small_ref,
     gr_ref, dwgu_ref, dwd_ref, dsmall_ref, parts_ref,
     x_all, inner, ggu, wgu_t, wd_t, gu, gi, near, away, back, hop, ss, sr, gs, gr,
 ):
-    pc = Place(dims)
     width, rows = g_ref.shape
     ff = wd_ref.shape[0]
-    greet(pc, "mates", False)
+    enter()
     gather = PlaneGather(pc, lambda q: x_all.at[:, lanes(q, rows)], gs, gr)
     scatter = PlaneScatter(pc, near, away, back, hop, ss, sr)
     x_all[:, lanes(pc.me, rows)] = x_ref[...]
     gather.start()
+    ready()
     transpose_into(wgu_t, wgu_ref)
     transpose_into(wd_t, wd_ref)
     sequence, diagonal_at, early_at = sequence_of(pc)
@@ -1626,6 +1644,178 @@
         + gather_sems(dims),
         (x, residual, g, g_all, wgu, wd, small),
     )
+
+
+def wait_for_weights(pc, riders, gather, wd_all, pieces, wd, sem, others):
+    last_blocks(pc, gather)
+    each(riders, "finish")
+    load = pltpu.make_async_copy(wd_all, pieces, sem)
+    load.start()
+    each(others, "wait")
+    load.wait()
+    half = pieces.shape[1]
+    for t in range(pc.nb):
+        wd[t * half : (t + 1) * half, :] = pieces[t]
+    gather.finish()
+
+
+def lower_kernel(dims, nk, plan_a, plan_f, *refs):
+    pc = Place(dims)
+    a_in, wgu_in, refs = (refs[:9], refs[9], refs[10:])
+    f_in, refs = (refs[: plan_f.count], refs[plan_f.count :])
+    a_out, wd_all, qo_next, refs = (refs[:6], refs[6], refs[7], refs[8:])
+    f_out, refs = (refs[: 3 + plan_f.count], refs[3 + plan_f.count :])
+    n2, wgu, pieces, wd, wsem, dsem, refs = (*refs[:6], refs[6:])
+    a_scratch, f_scratch = (refs[: 10 + len(plan_a.scratch) + 2], refs[10 + len(plan_a.scratch) + 2 :])
+    load = pltpu.make_async_copy(wgu_in, wgu, wsem)
+    load.start()
+    riders, gather = attention_forward_part(
+        pc, nk, 0, plan_a, "columns", *a_in, *a_out, n2, wd_all, qo_next, *a_scratch
+    )
+    feed_forward_part(
+        pc,
+        lambda: None,
+        lambda: wait_for_weights(pc, riders, gather, wd_all, pieces, wd, dsem, [load]),
+        plan_f, n2, a_out[5], wgu, wd, *f_in, *f_out, *f_scratch,
+    )
+
+
+def lower_layer(dims, nk, cid, hidden, small, meta, docs, cos_part, sin_part, qo, plan_a, block,
+                wgu, plan_f):
+    ns, nb, nf = dims
+    width, rows = hidden.shape
+    count = ns * nf
+    qkv = qo.shape[1] - width
+    two_ff = wgu.shape[1]
+    ff = two_ff // 2
+    sds = jax.ShapeDtypeStruct
+    dma = pltpu.SemaphoreType.DMA
+    outs = [
+        sds((width, rows), BF),
+        sds((H, HD, rows), BF),
+        sds((nk, 2 * KVH, HD, rows), BF),
+        sds((H, 1, rows), F32),
+        sds((H, HD, rows), BF),
+        sds((width, rows), F32),
+        *plan_a.shapes,
+        sds((nb, nf, block.shape[2], ns * block.shape[3]), BF),
+        sds((width, rows), F32),
+        sds((width, count * rows), BF),
+        sds((two_ff, count * rows), BF),
+        *plan_f.shapes,
+    ]
+    out = call(
+        functools.partial(lower_kernel, dims, nk, plan_a, plan_f),
+        "lower_layer",
+        cid,
+        tuple(outs),
+        [VM] * 6 + plan_a.outs + [VM] + [VM, AN, AN] + plan_f.outs,
+        [VM] * 6 + [AN, VM] + plan_a.places + [AN] + plan_f.places,
+        [
+            pltpu.VMEM((width, rows), BF),
+            pltpu.VMEM(wgu.shape, BF),
+            pltpu.VMEM((nb, ff // nb, width), BF),
+            pltpu.VMEM((ff, width), BF),
+            dma(()),
+            dma(()),
+        ]
+        + attention_scratch(dims, nk, width, rows, qkv)
+        + plan_a.scratch
+        + gather_sems(dims)
+        + [
+            pltpu.VMEM((width, count * rows), BF),
+            pltpu.VMEM((two_ff, count * rows), BF),
+            dma((2,)),
+            pltpu.VMEM((two_ff, width), BF),
+            pltpu.VMEM((width, ff), BF),
+            pltpu.VMEM((two_ff, rows), F32),
+            pltpu.VMEM((ff, rows), BF),
+        ]
+        + scatter_scratch(dims, width, rows)
+        + gather_sems(dims)
+        + plan_f.scratch,
+        (hidden, small, meta, docs, cos_part, sin_part, qo, block, *plan_a.arrays, wgu,
+         *plan_f.arrays),
+    )
+    return (out[:6], out[6], out[7], out[8:11], out[11:])
+
+
+def upper_kernel(dims, nk, plan, *refs):
+    pc = Place(dims)
+    a_in, g_ref, wgu_in, refs = (refs[:9], refs[9], refs[10], refs[11:])
+    a_out, wd_all, f_out, refs = (refs[:6], refs[6], refs[7:12], refs[12:])
+    n2, g_all, wgu, pieces, wd, wsem, dsem, refs = (*refs[:7], refs[7:])
+    a_scratch, f_scratch = (refs[: 10 + len(plan.scratch) + 2], refs[10 + len(plan.scratch) + 2 :])
+    load = pltpu.make_async_copy(wgu_in, wgu, wsem)
+    load.start()
+    riders, gather = attention_forward_part(
+        pc, nk, 1, plan, "lanes", *a_in, *a_out, n2, wd_all, g_all, *a_scratch
+    )
+    feed_both_part(
+        pc,
+        lambda: None,
+        lambda: wait_for_weights(pc, riders, gather, wd_all, pieces, wd, dsem, [load]),
+        1, n2, a_out[5], g_ref, g_all, wgu, wd, a_in[1], *f_out, *f_scratch,
+    )
+
+
+def upper_layer(dims, nk, cid, hidden, small, meta, docs, cos_part, sin_part, qo, plan, block, g,
+                wgu):
+    ns, nb, nf = dims
+    width, rows = hidden.shape
+    count = ns * nf
+    qkv = qo.shape[1] - width
+    two_ff = wgu.shape[1]
+    ff = two_ff // 2
+    sds = jax.ShapeDtypeStruct
+    dma = pltpu.SemaphoreType.DMA
+    outs = [
+        sds((width, rows), BF),
+        sds((H, HD, rows), BF),
+        sds((nk, 2 * KVH, HD, rows), BF),
+        sds((H, 1, rows), F32),
+        sds((H, HD, rows), BF),
+        sds((width, rows), F32),
+        *plan.shapes,
+        sds((width, rows), F32),
+        sds(wgu.shape, BF),
+        sds((ff, width), BF),
+        sds((width // 128, 128), F32),
+        sds((count, width, rows), BF),
+    ]
+    out = call(
+        functools.partial(upper_kernel, dims, nk, plan),
+        "upper_layer",
+        cid,
+        tuple(outs),
+        [VM] * 6 + plan.outs + [VM] * 5,
+        [VM] * 6 + [AN, VM] + plan.places + [VM, AN],
+        [
+            pltpu.VMEM((width, rows), BF),
+            pltpu.VMEM((width, count * rows), BF),
+            pltpu.VMEM(wgu.shape, BF),
+            pltpu.VMEM((nb, ff // nb, width), BF),
+            pltpu.VMEM((ff, width), BF),
+            dma(()),
+            dma(()),
+        ]
+        + attention_scratch(dims, nk, width, rows, qkv)
+        + plan.scratch
+        + gather_sems(dims)
+        + [
+            pltpu.VMEM((width, count * rows), BF),
+            pltpu.VMEM((ff, count * rows), BF),
+            pltpu.VMEM((two_ff, count * rows), BF),
+            pltpu.VMEM((two_ff, width), BF),
+            pltpu.VMEM((width, ff), BF),
+            pltpu.VMEM((two_ff, rows), F32),
+            pltpu.VMEM((ff, rows), F32),
+        ]
+        + scatter_scratch(dims, width, rows)
+        + gather_sems(dims),
+        (hidden, small, meta, docs, cos_part, sin_part, qo, block, *plan.arrays, g, wgu),
+    )
+    return (out[:6], out[7:])
 
 
 def reduce_kernel(
@@ -1926,24 +2116,36 @@
 
     common = (small_all, meta, query_docs, cos_part, sin_part)
     qo0 = qo_first.reshape(width, cols)
-    a0, (wd0, qo1) = attention_forward(
-        dims, nk, 1, 0, hidden, *common, qo0, ride((("gather", 0), wdp)), "columns", qz
-    )
+    wgu0 = gu_first.reshape(wide)
+    first = ride((("gather", 0), wdp))
+    second = ride((("gather", 1), gup))
+    third = ride((("gather", 1), wdp))
+    together = half % 8 == 0
+    if together:
+        a0, wd0, qo1, f0, (gu1,) = lower_layer(
+            dims, nk, 1, hidden, *common, qo0, first, qz, wgu0, second
+        )
+    else:
+        a0, (wd0, qo1) = attention_forward(
+            dims, nk, 1, 0, hidden, *common, qo0, first, "columns", qz
+        )
+        f0, (gu1,) = feed_forward(dims, 3, a0[6], a0[5], wgu0, wd0.reshape(ff, width), second)
     qo1 = qo1.reshape(width, cols)
     wd0 = wd0.reshape(ff, width)
-    wgu0 = gu_first.reshape(wide)
-    f0, (gu1,) = feed_forward(dims, 3, a0[6], a0[5], wgu0, wd0, ride((("gather", 1), gup)))
     wgu1 = gu1.reshape(wide)
-    a1, (wd1, g_all) = attention_forward(
-        dims, nk, 2, 1, f0[0], *common, qo1, ride((("gather", 1), wdp)), "lanes", cot.T
-    )
-    wd1 = wd1.reshape(ff, width)
+    if together:
+        a1, b1 = upper_layer(dims, nk, 2, f0[0], *common, qo1, third, cot.T, g, wgu1)
+    else:
+        a1, (wd1, g_all) = attention_forward(
+            dims, nk, 2, 1, f0[0], *common, qo1, third, "lanes", cot.T
+        )
+        wd1 = wd1.reshape(ff, width)
+        b1 = feed_both(dims, 4, 1, a1[6], a1[5], g, g_all, wgu1, wd1, small_all)
 
     line_gu = (nb, nf, dr, 2 * ff)
     line_wd = (nb, half, width)
     line_qo = (nb, nf, dr, cols)
     everything = (0, half)
-    b1 = feed_both(dims, 4, 1, a1[6], a1[5], g, g_all, wgu1, wd1, small_all)
     ab1, (dwd1, out1) = attention_backward(
         dims, nk, 7, 1, b1[0], *common, f0[0], *a1[:5], qo1,
         ride((("reduce", everything), b1[2].reshape(line_wd))), "sum", (b1[4], a1[5]),

time: 503 us -> 493 us (0.980)
  Pallas kernels: 472 us -> 466 us
    pallas_call x9 -> x7, Pallas kernels: 464 us -> 459 us  [call(): pl.pallas_call(kernel, name=name, out_shape=outs, in_specs=in_specs, out_...]
  transfers between devices with their start and end apart: 2 -> 2, of which waited for: 0 -> 0; matrix products, arithmetic and copies ran while one was open for 0% -> 0% of each run, Pallas kernels for 33% -> 35%
where the time goes in v8:
time: 493 us; the launch traced here: 484 us
  Pallas kernels  466 us (95%)
  other arithmetic  9.01 us (2%)
    pallas_call x7, Pallas kernels, call(): pl.pallas_call(kernel, name=name, out_shape=outs, in_specs=in_specs, out_...  459 us
  transfers between devices with their start and end apart: 2, of which 0 were waited for; matrix products, arithmetic and copies ran while one was open for 0% of the time, Pallas kernels for 35%

profile of v8, /device:TPU:0, one launch (start us, length us, event | category | flops | bytes accessed | tf_op | source)
XLA Modules:
  0.0 483.7 jit_solution(8564270163875188944)
XLA Ops:
  0.7 0.1 broadcast_in_dim.16
  0.8 0.1 broadcast_in_dim.17
  0.9 0.7 fusion.1
  1.6 0.7 convert_reduce_fusion
  2.3 0.6 gather_fusion
  2.9 0.6 constant_dynamic-slice_fusion.2.refs_3_.docs_ref
  3.4 0.7 reduce
  4.1 0.7 reduce.1
  4.8 0.7 reduce.2
  5.5 1.2 constant_dynamic-slice_fusion
  6.8 0.2 copy.21
  7.0 0.0 copy-start.2
  7.0 0.2 copy.22
  7.2 1.0 convert_bitcast_fusion.refs_0_.h_ref
  8.2 1.0 bitcast_convert_fusion.refs_9_
  9.2 0.7 broadcast_select_fusion.refs_2_.meta_ref
  9.9 0.8 multiply_sine_fusion
  10.7 0.6 fusion.small
  11.3 75.1 %gather_weights.1 = (bf16[2,4,56,1216]{3,2,1,0:T(8,128)(2,1)}, bf16[2,152,896]{2,1,0:T(8,128)(2,1)}, bf16[4,4,56,1216]{3,2,1,0:T(8,128)(2,1)}, bf16[4,4,56,2048]...) custom-call(bf16[1,56,9728]{2,1,0:T(8,128)(2,1)} %w_ref.1, bf16[1,56,1152]{2,1,0:T(8,128)(2,1)} %wq_ref.1, ...), custom_call_target="tpu_custom_call" | custom-call | tf_op jit(solution)/shard_map/gather_weights/pallas_call | solution.py:658
  86.4 81.5 %lower_layer.1 = (bf16[896,256]{1,0:T(8,128)(2,1)}, bf16[14,64,256]{2,1,0:T(8,128)(2,1)}, bf16[3,4,64,256]{3,2,1,0:T(8,128)(2,1)}, f32[14,1,256]{2,1,0:T(1,128)}...) custom-call(f32[896,256]{1,0:T(8,128)} %convert_bitcast_fusion.refs_, ...), custom_call_target="tpu_custom_call" | custom-call | tf_op jit(solution)/shard_map/lower_layer/pallas_call | solution.py:658
  167.9 88.2 %upper_layer.1 = (bf16[896,256]{1,0:T(8,128)(2,1)}, bf16[14,64,256]{2,1,0:T(8,128)(2,1)}, bf16[3,4,64,256]{3,2,1,0:T(8,128)(2,1)}, f32[14,1,256]{2,1,0:T(1,128)}...) custom-call(f32[896,256]{1,0:T(8,128)} %get-tuple-element.64.refs_0_, ...), custom_call_target="tpu_custom_call" | custom-call | tf_op jit(solution)/shard_map/upper_layer/pallas_call | solution.py:658
  256.1 45.5 %attention_backward.2 = (f32[896,256]{1,0:T(8,128)}, bf16[896,2048]{1,0:T(8,128)(2,1)}, f32[16,128]{1,0:T(8,128)}, bf16[152,896]{1,0:T(8,128)(2,1)}, f32[896,256]{1,0:T(8,128)}) custom-call(f32[896,256]{1,0:T(8,128)} %get-tuple-element.67.g_ref, f32[2,24,128]{2,1,0:T(8,128)} %get-tuple-element.58.refs_1_.small_ref, ...), custom_call_target="tpu_custom_call" | custom-call | tf_op jit(solution)/shard_map/attention_backward/pallas_call | solution.py:658
  301.6 1.3 select_convert_fusion.1
  302.9 0.1 collective-permute-start
  303.0 55.6 %feed_backward.1 = (f32[896,256]{1,0:T(8,128)}, bf16[896,1216]{1,0:T(8,128)(2,1)}, bf16[608,896]{1,0:T(8,128)(2,1)}, f32[7,128]{1,0:T(8,128)}, bf16[4,56,1216]{2,1,0:T(8,128)(2,1)}) custom-call(f32[896,256]{1,0:T(8,128)} %get-tuple-element.76.g_ref.gh1, f32[896,256]{1,0:T(8,128)} %get-tuple-element.77.res_ref, bf16[896,2048]{1,0:T(8,128)(2,1)} %get-tuple-element.78.x_in, ...), custom_call_target="tpu_custom_call" | custom-call | tf_op jit(solution)/shard_map/feed_backward/pallas_call | solution.py:658
  358.6 54.5 %attention_backward.3 = (f32[896,256]{1,0:T(8,128)}, bf16[896,2048]{1,0:T(8,128)(2,1)}, f32[16,128]{1,0:T(8,128)}, bf16[3,56,1216]{2,1,0:T(8,128)(2,1)}, bf16[4,...) custom-call(f32[896,256]{1,0:T(8,128)} %get-tuple-element.82.g_ref, ...), custom_call_target="tpu_custom_call" | custom-call | tf_op jit(solution)/shard_map/attention_backward/pallas_call | solution.py:658
  413.0 0.1 select_convert_fusion
  413.2 3.1 collective-permute-start.1
  416.3 58.3 %reduce_gradients.1 = (f32[2,56,1024]{2,1,0:T(8,128)}, f32[48,128]{1,0:T(8,128)}, bf16[8,56,1216]{2,1,0:T(8,128)(2,1)}, bf16[2,152,896]{2,1,0:T(8,128)(2,1)}) custom-call(bf16[4,4,56,2048]{3,2,1,0:T(8,128)(2,1)} %bitcast.35, bf16[4,56,1024]{2,1,0:T(8,128)(2,1)} %get-tuple-element.92.terms, f32[16,128]{1,0:T(8,128)} %get-tuple-element.93.sa0, ...), custom_call_target="tpu_custom_call" | custom-call | tf_op jit(solution)/shard_map/reduce_gradients/pallas_call | solution.py:658
  474.6 0.7 copy-done.3
  475.4 0.2 copy-done.4
  475.5 7.8 %lay_out.1 = (f32[1,2,256,896]{3,2,1,0:T(8,128)}, f32[1,2,256,896]{3,2,1,0:T(8,128)}, f32[1,896]{1,0:T(1,128)}, f32[1,56,1152]{2,1,0:T(8,128)}, f32[1,1152]{1,0:...) custom-call(bf16[8,56,1216]{2,1,0:T(8,128)(2,1)} %get-tuple-element.100.gu, ...), custom_call_target="tpu_custom_call" | custom-call | tf_op jit(solution)/shard_map/lay_out/pallas_call | solution.py:2045
  (15 shorter events, 0.1 us)
Async XLA Ops:
  7.0 79.4 %copy-start.2 = (bf16[1,256,896]{1,2,0:T(8,128)(2,1)}, bf16[1,256,896]{1,2,0:T(8,128)(2,1)S(1)}, u32[]{:S(2)}) copy-start(bf16[1,256,896]{1,2,0:T(8,128)(2,1)S(1)} %copy.21) | copy-start | bytes 1376260
  256.1 45.5 %copy-start = (f32[896,256]{1,0:T(8,128)S(1)}, f32[896,256]{1,0:T(8,128)}, u32[]{:S(2)}) copy-start(f32[896,256]{1,0:T(8,128)} %get-tuple-element.64.refs_0_.h_ref.out0) | copy-start | bytes 2752516
  302.9 171.7 %collective-permute-start = (bf16[896,256]{1,0:T(8,128)(2,1)S(1)}, bf16[896,256]{1,0:T(8,128)(2,1)S(1)}, u32[]{:S(2)}, u32[]{:S(2)}) collective-permute-start(bf16[896,256]{1,0:T(8,128)(2,1)S(1)} %select_convert_fusion.1), channel_id=1, source_target_pairs={{0,16},{16,0},{1,17},{17,1},{2,18},{18,2},{3,19},{19,3},{4,20},{20... | collective-permute-start | bytes 1376264 | tf_op jit(solution)/shard_map/ppermute | solution.py:2167
  358.6 54.5 %copy-start.1 = (f32[896,256]{1,0:T(8,128)S(1)}, f32[896,256]{1,0:T(8,128)}, u32[]{:S(2)}) copy-start(f32[896,256]{1,0:T(8,128)} %get-tuple-element.76.g_ref.gh1) | copy-start | bytes 2752516
  413.2 61.5 %collective-permute-start.1 = (bf16[896,256]{1,0:T(8,128)(2,1)S(1)}, bf16[896,256]{1,0:T(8,128)(2,1)S(1)}, u32[]{:S(2)}, u32[]{:S(2)}) collective-permute-start(bf16[896,256]{1,0:T(8,128)(2,1)S(1)} %select_convert_fusion), channel_id=1, source_target_pairs={{0,16},{16,0},{1,17},{17,1},{2,18},{18,2},{3,19},{19,3},{4,20},{20... | collective-permute-start | bytes 1376264 | tf_op jit(solution)/shard_map/ppermute | solution.py:2167
  474.6 0.8 copy-start.3
  474.6 0.9 copy-start.4

commit v9 on v8

--- a/solution.py
+++ b/solution.py
@@ -971,7 +971,7 @@
             out_own[head] = nn(values, e.astype(BF))
             return carried
 
-        lax.fori_loop(0, GROUP, own_keys, 0)
+        lax.fori_loop(0, GROUP, own_keys, 0, unroll=True)
     for c in sends:
         c.wait()
     each(riders, "service")
@@ -998,7 +998,7 @@
             mixed_ref[head] = (out / total).astype(BF)
             return carried
 
-        lax.fori_loop(0, GROUP, one_head, 0)
+        lax.fori_loop(0, GROUP, one_head, 0, unroll=True)
         if g == 0:
             for step in range(1, min(6, pc.count)):
                 gather.before(step)
@@ -1141,7 +1141,7 @@
             dq_some[head] = dq
             return carried
 
-        lax.fori_loop(0, GROUP, earlier, 0)
+        lax.fori_loop(0, GROUP, earlier, 0, unroll=True)
         if g == 0:
             scatter.late()
         if g == 1 or carry == "sum":
@@ -1168,7 +1168,7 @@
             gj[pl.ds(pl.multiple_of(head * HD + half, half), half), :] = r2.astype(BF)
             return carried
 
-        lax.fori_loop(0, GROUP, own_keys, 0)
+        lax.fori_loop(0, GROUP, own_keys, 0, unroll=True)
     for c in sends:
         c.wait()
     each(riders, "service")
@@ -1326,7 +1326,7 @@
             inner[pl.ds(r, chunk), :] = (gate * jax.nn.sigmoid(gate) * up).astype(BF)
             return c
 
-        lax.fori_loop(0, ff // chunk, act, 0)
+        lax.fori_loop(0, ff // chunk, act, 0, unroll=True)
         scatter.put(step, nn(wd_t[...], inner[...]))
 
         @pl.when(turn == 3)
@@ -1446,7 +1446,7 @@
             ggu[pl.ds(ff + r, chunk), sl] = (grad * silu).astype(BF)
             return c
 
-        lax.fori_loop(0, ff // chunk, act, 0)
+        lax.fori_loop(0, ff // chunk, act, 0, unroll=True)
         scatter.put(step, nn(wgu_ref[...], ggu[:, sl]))
 
         @pl.when(turn == 3)
@@ -1574,7 +1574,7 @@
             ggu[pl.ds(ff + r, chunk), sl] = (grad * silu).astype(BF)
             return c
 
-        lax.fori_loop(0, ff // chunk, act, 0)
+        lax.fori_loop(0, ff // chunk, act, 0, unroll=True)
         scatter.put(step, nn(wgu_ref[...], ggu[:, sl]))
 
         @pl.when(turn == diagonal_at)

time: 493 us -> 484 us (0.982)
  Pallas kernels: 466 us -> 457 us
    pallas_call x7, Pallas kernels: 459 us -> 449 us  [call(): pl.pallas_call(kernel, name=name, out_shape=outs, in_specs=in_specs, out_...]
where the time goes in v9:
time: 484 us; the launch traced here: 474 us
  Pallas kernels  457 us (94%)
  other arithmetic  9.01 us (2%)
    pallas_call x7, Pallas kernels, call(): pl.pallas_call(kernel, name=name, out_shape=outs, in_specs=in_specs, out_...  449 us
  transfers between devices with their start and end apart: 2, of which 0 were waited for; matrix products, arithmetic and copies ran while one was open for 0% of the time, Pallas kernels for 35%

profile of v9, /device:TPU:0, one launch (start us, length us, event | category | flops | bytes accessed | tf_op | source)
XLA Modules:
  0.0 474.1 jit_solution(5753564347971675668)
XLA Ops:
  0.7 0.1 broadcast_in_dim.16
  0.8 0.1 broadcast_in_dim.17
  0.9 0.7 fusion.1
  1.6 0.7 convert_reduce_fusion
  2.3 0.6 gather_fusion
  2.9 0.6 constant_dynamic-slice_fusion.2.refs_3_.docs_ref
  3.4 0.7 reduce
  4.1 0.7 reduce.1
  4.8 0.7 reduce.2
  5.5 1.2 constant_dynamic-slice_fusion
  6.8 0.2 copy.21
  7.0 0.0 copy-start.2
  7.0 0.2 copy.22
  7.2 1.0 convert_bitcast_fusion.refs_0_.h_ref
  8.2 1.0 bitcast_convert_fusion.refs_9_
  9.2 0.7 broadcast_select_fusion.refs_2_.meta_ref
  9.9 0.8 multiply_sine_fusion
  10.7 0.6 fusion.small
  11.3 75.1 %gather_weights.1 = (bf16[2,4,56,1216]{3,2,1,0:T(8,128)(2,1)}, bf16[2,152,896]{2,1,0:T(8,128)(2,1)}, bf16[4,4,56,1216]{3,2,1,0:T(8,128)(2,1)}, bf16[4,4,56,2048]...) custom-call(bf16[1,56,9728]{2,1,0:T(8,128)(2,1)} %w_ref.1, bf16[1,56,1152]{2,1,0:T(8,128)(2,1)} %wq_ref.1, ...), custom_call_target="tpu_custom_call" | custom-call | tf_op jit(solution)/shard_map/gather_weights/pallas_call | solution.py:658
  86.4 80.9 %lower_layer.1 = (bf16[896,256]{1,0:T(8,128)(2,1)}, bf16[14,64,256]{2,1,0:T(8,128)(2,1)}, bf16[3,4,64,256]{3,2,1,0:T(8,128)(2,1)}, f32[14,1,256]{2,1,0:T(1,128)}...) custom-call(f32[896,256]{1,0:T(8,128)} %convert_bitcast_fusion.refs_, ...), custom_call_target="tpu_custom_call" | custom-call | tf_op jit(solution)/shard_map/lower_layer/pallas_call | solution.py:658
  167.3 84.2 %upper_layer.1 = (bf16[896,256]{1,0:T(8,128)(2,1)}, bf16[14,64,256]{2,1,0:T(8,128)(2,1)}, bf16[3,4,64,256]{3,2,1,0:T(8,128)(2,1)}, f32[14,1,256]{2,1,0:T(1,128)}...) custom-call(f32[896,256]{1,0:T(8,128)} %get-tuple-element.64.refs_0_, ...), custom_call_target="tpu_custom_call" | custom-call | tf_op jit(solution)/shard_map/upper_layer/pallas_call | solution.py:658
  251.5 44.5 %attention_backward.2 = (f32[896,256]{1,0:T(8,128)}, bf16[896,2048]{1,0:T(8,128)(2,1)}, f32[16,128]{1,0:T(8,128)}, bf16[152,896]{1,0:T(8,128)(2,1)}, f32[896,256]{1,0:T(8,128)}) custom-call(f32[896,256]{1,0:T(8,128)} %get-tuple-element.67.g_ref, f32[2,24,128]{2,1,0:T(8,128)} %get-tuple-element.58.refs_1_.small_ref, ...), custom_call_target="tpu_custom_call" | custom-call | tf_op jit(solution)/shard_map/attention_backward/pallas_call | solution.py:658
  296.0 1.3 select_convert_fusion.1
  297.3 0.1 collective-permute-start
  297.4 50.5 %feed_backward.1 = (f32[896,256]{1,0:T(8,128)}, bf16[896,1216]{1,0:T(8,128)(2,1)}, bf16[608,896]{1,0:T(8,128)(2,1)}, f32[7,128]{1,0:T(8,128)}, bf16[4,56,1216]{2,1,0:T(8,128)(2,1)}) custom-call(f32[896,256]{1,0:T(8,128)} %get-tuple-element.76.g_ref.gh1, f32[896,256]{1,0:T(8,128)} %get-tuple-element.77.res_ref, bf16[896,2048]{1,0:T(8,128)(2,1)} %get-tuple-element.78.x_in, ...), custom_call_target="tpu_custom_call" | custom-call | tf_op jit(solution)/shard_map/feed_backward/pallas_call | solution.py:658
  347.9 54.5 %attention_backward.3 = (f32[896,256]{1,0:T(8,128)}, bf16[896,2048]{1,0:T(8,128)(2,1)}, f32[16,128]{1,0:T(8,128)}, bf16[3,56,1216]{2,1,0:T(8,128)(2,1)}, bf16[4,...) custom-call(f32[896,256]{1,0:T(8,128)} %get-tuple-element.82.g_ref, ...), custom_call_target="tpu_custom_call" | custom-call | tf_op jit(solution)/shard_map/attention_backward/pallas_call | solution.py:658
  402.4 0.1 select_convert_fusion
  402.5 3.0 collective-permute-start.1
  405.5 59.4 %reduce_gradients.1 = (f32[2,56,1024]{2,1,0:T(8,128)}, f32[48,128]{1,0:T(8,128)}, bf16[8,56,1216]{2,1,0:T(8,128)(2,1)}, bf16[2,152,896]{2,1,0:T(8,128)(2,1)}) custom-call(bf16[4,4,56,2048]{3,2,1,0:T(8,128)(2,1)} %bitcast.35, bf16[4,56,1024]{2,1,0:T(8,128)(2,1)} %get-tuple-element.92.terms, f32[16,128]{1,0:T(8,128)} %get-tuple-element.93.sa0, ...), custom_call_target="tpu_custom_call" | custom-call | tf_op jit(solution)/shard_map/reduce_gradients/pallas_call | solution.py:658
  465.0 0.7 copy-done.3
  465.7 0.2 copy-done.4
  465.9 7.8 %lay_out.1 = (f32[1,2,256,896]{3,2,1,0:T(8,128)}, f32[1,2,256,896]{3,2,1,0:T(8,128)}, f32[1,896]{1,0:T(1,128)}, f32[1,56,1152]{2,1,0:T(8,128)}, f32[1,1152]{1,0:...) custom-call(bf16[8,56,1216]{2,1,0:T(8,128)(2,1)} %get-tuple-element.100.gu, ...), custom_call_target="tpu_custom_call" | custom-call | tf_op jit(solution)/shard_map/lay_out/pallas_call | solution.py:2045
  (15 shorter events, 0.1 us)
Async XLA Ops:
  7.0 79.4 %copy-start.2 = (bf16[1,256,896]{1,2,0:T(8,128)(2,1)}, bf16[1,256,896]{1,2,0:T(8,128)(2,1)S(1)}, u32[]{:S(2)}) copy-start(bf16[1,256,896]{1,2,0:T(8,128)(2,1)S(1)} %copy.21) | copy-start | bytes 1376260
  251.5 44.5 %copy-start = (f32[896,256]{1,0:T(8,128)S(1)}, f32[896,256]{1,0:T(8,128)}, u32[]{:S(2)}) copy-start(f32[896,256]{1,0:T(8,128)} %get-tuple-element.64.refs_0_.h_ref.out0) | copy-start | bytes 2752516
  297.3 167.6 %collective-permute-start = (bf16[896,256]{1,0:T(8,128)(2,1)S(1)}, bf16[896,256]{1,0:T(8,128)(2,1)S(1)}, u32[]{:S(2)}, u32[]{:S(2)}) collective-permute-start(bf16[896,256]{1,0:T(8,128)(2,1)S(1)} %select_convert_fusion.1), channel_id=1, source_target_pairs={{0,16},{16,0},{1,17},{17,1},{2,18},{18,2},{3,19},{19,3},{4,20},{20... | collective-permute-start | bytes 1376264 | tf_op jit(solution)/shard_map/ppermute | solution.py:2167
  347.9 54.6 %copy-start.1 = (f32[896,256]{1,0:T(8,128)S(1)}, f32[896,256]{1,0:T(8,128)}, u32[]{:S(2)}) copy-start(f32[896,256]{1,0:T(8,128)} %get-tuple-element.76.g_ref.gh1) | copy-start | bytes 2752516
  402.5 62.4 %collective-permute-start.1 = (bf16[896,256]{1,0:T(8,128)(2,1)S(1)}, bf16[896,256]{1,0:T(8,128)(2,1)S(1)}, u32[]{:S(2)}, u32[]{:S(2)}) collective-permute-start(bf16[896,256]{1,0:T(8,128)(2,1)S(1)} %select_convert_fusion), channel_id=1, source_target_pairs={{0,16},{16,0},{1,17},{17,1},{2,18},{18,2},{3,19},{19,3},{4,20},{20... | collective-permute-start | bytes 1376264 | tf_op jit(solution)/shard_map/ppermute | solution.py:2167
  465.0 0.8 copy-start.3
  465.0 0.9 copy-start.4
